TPU v7x, 128 devices: a whole 4x4x4 slice. The times are simulated.
128 devices in a mesh: wide: 16 (over x, y), narrow: 8 (over z, core).
Axes of the slice: x: 4, y: 4, z: 4, core: 2. Of those that a mesh axis runs over, the one named last changes fastest.
Arguments:
- features: bfloat16 [1024, 64, 512], P(('wide', 'narrow')), may hold values from -6 to 6
- kernel_one: bfloat16 [27, 64, 64], replicated, may hold values from -0.15625 to 0.15625
- kernel_two: bfloat16 [27, 64, 64], replicated, may hold values from -0.15625 to 0.15625
- cotangent: bfloat16 [1024, 64, 512], P(('wide', 'narrow')), may hold values from -6 to 6
- neighbours: int32 [1024, 26], P(('wide', 'narrow')), may hold values from -1 to 1023, as said below
- occupancy: int32 [1024, 512], P(('wide', 'narrow')), may hold values from 0 to 1, as said below
Outputs:
- output: bfloat16 [1024, 64, 512], P(('wide', 'narrow'))
- grad_in: bfloat16 [1024, 64, 512], P(('wide', 'narrow'))
- grad_one: float32 [27, 64, 64], replicated
- grad_two: float32 [27, 64, 64], replicated
Inputs may be any that keep to these rules, and one draw needn't show every extreme that they name: neighbours[b, dir] is the global slot (device index along wide then narrow, times 8, plus the slot) of the live brick beside brick b in direction dir, or -1. The lists are symmetric: c stands in direction dir of b exactly when b stands in direction 25 - dir of c. Every neighbour lies on the device of b or on the device just before or just after it in that order. On every device at most 4 bricks have a neighbour on the next device, and at most as many on the previous one; every device but the last has exactly 4 toward the next. A slot that holds no brick lists no neighbours. `occupancy`: A slot that holds no brick has no active voxel.
All inputs are finite; a program needn't handle non-finite values.
Results may differ from a plain program's by a relative error of at most 0.005.
Values may be sent and summed in bfloat16 or wider, within the bound.
No kernel may reach another device: no remote copies, remote signals or barrier semaphores. Data moves between devices by JAX's collectives and lax.ppermute only.
A program may use at most 192 MiB of HBM per device.

v0:
```python
import jax
import jax.numpy as jnp
import numpy as np
from jax import lax
from jax.sharding import PartitionSpec as P

EDGE = 8


def from_behind(block, axis, distance):
    devices = range(lax.axis_size(axis))
    route = [(i - distance, i) for i in devices if i - distance in devices]
    return lax.ppermute(block, axis, route)


def offset_tables(edge):
    cell_ids = np.arange(edge**3)
    first = cell_ids // (edge * edge)
    second = cell_ids // edge % edge
    third = cell_ids % edge
    direction_codes = []
    source_cells = []
    for a in range(3):
        for b in range(3):
            for c in range(3):
                shifted_ids = [first + a - 1, second + b - 1, third + c - 1]
                side_codes = [
                    (m >= edge).astype(np.int64) - (m < 0).astype(np.int64) for m in shifted_ids
                ]
                direction_codes.append(
                    (side_codes[0] + 1) * 9 + (side_codes[1] + 1) * 3 + side_codes[2] + 1
                )
                wrapped = [m % edge for m in shifted_ids]
                source_cells.append((wrapped[0] * edge + wrapped[1]) * edge + wrapped[2])
    return (np.stack(direction_codes).astype(np.int32), np.stack(source_cells).astype(np.int32))


def gather_index(lookup, usable, zero_at):
    brick_count = lookup.shape[0]
    voxel_count = EDGE**3
    direction_codes, source_cells = offset_tables(EDGE)
    own_slots = jnp.arange(brick_count, dtype=jnp.int32)[:, None]
    lookup_full = jnp.concatenate([lookup[:, :13], own_slots, lookup[:, 13:]], axis=1)
    usable_full = jnp.concatenate(
        [usable[:, :13], jnp.ones((brick_count, 1), bool), usable[:, 13:]], axis=1
    )
    brick_ids = jnp.take(lookup_full, jnp.asarray(direction_codes), axis=1)
    present = jnp.take(usable_full, jnp.asarray(direction_codes), axis=1)
    gather_rows = jnp.where(
        present, brick_ids * voxel_count + jnp.asarray(source_cells)[None], zero_at
    )
    return gather_rows.transpose(1, 0, 2).reshape(27, -1).astype(jnp.int32)


def flatten(volume):
    return volume.transpose(1, 0, 2).reshape(volume.shape[1], -1)


def unflatten(flattened, brick_count):
    return flattened.reshape(flattened.shape[0], brick_count, -1).transpose(1, 0, 2)


def pooled(volume):
    flattened = flatten(volume)
    return jnp.concatenate(
        [flattened, jnp.zeros((flattened.shape[0], volume.shape[2]), flattened.dtype)], axis=1
    )


def convolve(pool_flat, gather_rows, weights):
    accumulated = None
    for group in range(9):
        shifted = jnp.take(pool_flat, gather_rows[3 * group : 3 * group + 3], axis=1)
        summand = jnp.einsum(
            "qcm,cpq->pm",
            shifted,
            weights[3 * group : 3 * group + 3],
            preferred_element_type=jnp.float32,
        )
        accumulated = summand if accumulated is None else accumulated + summand
    return accumulated


def kernel_grad(pool_flat, gather_rows, grad_flat):
    pieces = []
    for group in range(9):
        shifted = jnp.take(pool_flat, gather_rows[3 * group : 3 * group + 3], axis=1)
        pieces.append(
            jnp.einsum("pm,qcm->cpq", grad_flat, shifted, preferred_element_type=jnp.float32)
        )
    return jnp.concatenate(pieces, axis=0)


def flipped(weights):
    return jnp.flip(weights, 0).transpose(0, 2, 1)


def placement_info(neighbours, slot_count):
    position = lax.axis_index(("wide", "narrow"))
    usable = neighbours >= 0
    owners = jnp.where(usable, neighbours // slot_count, position)
    within = neighbours % slot_count
    relative = owners - position
    return (usable, within, relative)


def brick_lookup(neighbours, slot_count):
    usable, within, relative = placement_info(neighbours, slot_count)
    lookup = within + jnp.where(
        relative < 0, slot_count, jnp.where(relative > 0, 2 * slot_count, 0)
    )
    pool_count = 3 * slot_count
    return gather_index(lookup, usable, pool_count * EDGE**3)


def exchanged(volume):
    earlier_bricks = from_behind(volume, ("wide", "narrow"), 1)
    later_bricks = from_behind(volume, ("wide", "narrow"), -1)
    return pooled(jnp.concatenate([volume, earlier_bricks, later_bricks], axis=0))


def local(features, kernel_one, kernel_two, cotangent, neighbours, occupancy):
    slot_count = features.shape[0]
    active = occupancy.astype(jnp.bfloat16)[:, None, :]
    mask_flat = occupancy.astype(jnp.float32).reshape(1, -1)
    gather_rows = brick_lookup(neighbours, slot_count)
    inputs = exchanged(features * active)
    preact = convolve(inputs, gather_rows, kernel_one)
    hidden_flat = (jax.nn.silu(preact) * mask_flat).astype(jnp.bfloat16)
    hidden = exchanged(unflatten(hidden_flat, slot_count))
    output = (convolve(hidden, gather_rows, kernel_two) * mask_flat).astype(jnp.bfloat16)
    grad_out = cotangent * active
    grad_out_flat = flatten(grad_out)
    back_two = convolve(exchanged(grad_out), gather_rows, flipped(kernel_two))
    sigmoid_pre = jax.nn.sigmoid(preact)
    grad_pre = (back_two * sigmoid_pre * (1.0 + preact * (1.0 - sigmoid_pre)) * mask_flat).astype(
        jnp.bfloat16
    )
    grad_in = (
        convolve(exchanged(unflatten(grad_pre, slot_count)), gather_rows, flipped(kernel_one))
        * mask_flat
    ).astype(jnp.bfloat16)
    local_one = kernel_grad(inputs, gather_rows, grad_pre)
    local_two = kernel_grad(hidden, gather_rows, grad_out_flat)
    sum_one, sum_two = lax.psum((local_one, local_two), ("wide", "narrow"))
    normalizer = 1.0 / jnp.sqrt(
        jnp.float32(slot_count * EDGE**3 * lax.axis_size(("wide", "narrow")))
    )
    return (
        unflatten(output, slot_count),
        unflatten(grad_in, slot_count),
        sum_one * normalizer,
        sum_two * normalizer,
    )


def solution(mesh):
    in_specs = (
        P(("wide", "narrow"), None, None),
        P(),
        P(),
        P(("wide", "narrow"), None, None),
        P(("wide", "narrow"), None),
        P(("wide", "narrow"), None),
    )
    out_specs = (P(("wide", "narrow"), None, None), P(("wide", "narrow"), None, None), P(), P())
    return jax.shard_map(local, mesh=mesh, in_specs=in_specs, out_specs=out_specs, check_vma=False)
```

profile of v0, /device:TPU:1, one launch (start us, length us, event | category | flops | bytes accessed | tf_op | source)
XLA Modules:
  0.0 2136.8 jit_solution(4518358633023287263)
XLA Ops:
  22.4 26.9 %gather_fusion = pred[13824,8]{1,0:T(8,128)(4,1)} fusion(pred[8,27]{0,1:T(8,128)(4,1)S(1)} %copy.117, s32[14336]{0:T(1024)S(1)} %pad_clamp_fusion), kind=kCustom, calls=%fused_computation.36 | custom fusion | bytes 276480 | tf_op jit(solution)/shard_map/jit(_take)/gather | solution.py:48
  52.7 26.1 %gather_fusion.1 = s32[13824,8]{1,0:T(8,128)} fusion(s32[8,27]{0,1:T(8,128)S(1)} %copy.118, s32[14336]{0:T(1024)S(1)} %pad_clamp_fusion), kind=kCustom, calls=%fused_computation.37 | custom fusion | bytes 940032 | tf_op jit(solution)/shard_map/jit(_take)/gather | solution.py:47
  78.9 5.1 broadcast_multiply_fusion
  84.0 4.6 copy.119
  114.5 43.3 %gather_fusion.22 = bf16[12288,64]{1,0:T(8,128)(2,1)} fusion(bf16[64,12800]{0,1:T(8,128)(2,1)S(1)} %concatenate.43, s32[12288]{0:T(1024)S(1)} %get-tuple-element.44), kind=kCustom, calls=%fused_computation.20.clone | custom fusion | bytes 3194880 | tf_op jit(solution)/shard_map/jit(_take)/gather | solution.py:73
  157.8 43.7 %gather_fusion.4 = bf16[12288,64]{1,0:T(8,128)(2,1)} fusion(bf16[64,12800]{0,1:T(8,128)(2,1)} %concatenate.37, s32[12288]{0:T(1024)S(1)} %get-tuple-element.44), kind=kCustom, calls=%fused_computation.2.clone | custom fusion | bytes 3194880 | tf_op jit(solution)/shard_map/jit(_take)/gather | solution.py:73
  201.5 43.3 %gather_fusion.21 = bf16[12288,64]{1,0:T(8,128)(2,1)} fusion(bf16[64,12800]{0,1:T(8,128)(2,1)S(1)} %concatenate.43, s32[12288]{0:T(1024)S(1)} %get-tuple-element.45), kind=kCustom, calls=%fused_computation.19.clone | custom fusion | bytes 3194880 | tf_op jit(solution)/shard_map/jit(_take)/gather | solution.py:73
  244.8 43.8 %gather_fusion.3 = bf16[12288,64]{1,0:T(8,128)(2,1)} fusion(bf16[64,12800]{0,1:T(8,128)(2,1)} %concatenate.37, s32[12288]{0:T(1024)S(1)} %get-tuple-element.45), kind=kCustom, calls=%fused_computation.1.clone | custom fusion | bytes 3194880 | tf_op jit(solution)/shard_map/jit(_take)/gather | solution.py:73
  288.6 43.3 %gather_fusion.24 = bf16[12288,64]{1,0:T(8,128)(2,1)} fusion(bf16[64,12800]{0,1:T(8,128)(2,1)S(1)} %concatenate.43, s32[12288]{0:T(1024)S(1)} %copy-done.31), kind=kCustom, calls=%fused_computation.22.clone | custom fusion | bytes 3194880 | tf_op jit(solution)/shard_map/jit(_take)/gather | solution.py:73
  331.9 43.8 %gather_fusion.6 = bf16[12288,64]{1,0:T(8,128)(2,1)} fusion(bf16[64,12800]{0,1:T(8,128)(2,1)} %concatenate.37, s32[12288]{0:T(1024)S(1)} %copy-done.31), kind=kCustom, calls=%fused_computation.4.clone | custom fusion | bytes 3194880 | tf_op jit(solution)/shard_map/jit(_take)/gather | solution.py:73
  375.6 43.3 %gather_fusion.23 = bf16[12288,64]{1,0:T(8,128)(2,1)} fusion(bf16[64,12800]{0,1:T(8,128)(2,1)S(1)} %concatenate.43, s32[12288]{0:T(1024)S(1)} %get-tuple-element.43), kind=kCustom, calls=%fused_computation.21.clone | custom fusion | bytes 3194880 | tf_op jit(solution)/shard_map/jit(_take)/gather | solution.py:73
  418.9 43.9 %gather_fusion.5 = bf16[12288,64]{1,0:T(8,128)(2,1)} fusion(bf16[64,12800]{0,1:T(8,128)(2,1)} %concatenate.37, s32[12288]{0:T(1024)S(1)} %get-tuple-element.43), kind=kCustom, calls=%fused_computation.3.clone | custom fusion | bytes 3194880 | tf_op jit(solution)/shard_map/jit(_take)/gather | solution.py:73
  462.9 43.3 %gather_fusion.26 = bf16[12288,64]{1,0:T(8,128)(2,1)} fusion(bf16[64,12800]{0,1:T(8,128)(2,1)S(1)} %concatenate.43, s32[12288]{0:T(1024)S(1)} %copy-done.34), kind=kCustom, calls=%fused_computation.24.clone | custom fusion | bytes 3194880 | tf_op jit(solution)/shard_map/jit(_take)/gather | solution.py:73
  506.2 43.9 %gather_fusion.8 = bf16[12288,64]{1,0:T(8,128)(2,1)} fusion(bf16[64,12800]{0,1:T(8,128)(2,1)} %concatenate.37, s32[12288]{0:T(1024)S(1)} %copy-done.34), kind=kCustom, calls=%fused_computation.6.clone | custom fusion | bytes 3194880 | tf_op jit(solution)/shard_map/jit(_take)/gather | solution.py:73
  550.1 43.3 %gather_fusion.25 = bf16[12288,64]{1,0:T(8,128)(2,1)} fusion(bf16[64,12800]{0,1:T(8,128)(2,1)S(1)} %concatenate.43, s32[12288]{0:T(1024)S(1)} %get-tuple-element.41), kind=kCustom, calls=%fused_computation.23.clone | custom fusion | bytes 3194880 | tf_op jit(solution)/shard_map/jit(_take)/gather | solution.py:73
  593.4 43.8 %gather_fusion.7 = bf16[12288,64]{1,0:T(8,128)(2,1)} fusion(bf16[64,12800]{0,1:T(8,128)(2,1)} %concatenate.37, s32[12288]{0:T(1024)S(1)} %get-tuple-element.41), kind=kCustom, calls=%fused_computation.5.clone | custom fusion | bytes 3194880 | tf_op jit(solution)/shard_map/jit(_take)/gather | solution.py:73
  637.2 43.3 %gather_fusion.28 = bf16[12288,64]{1,0:T(8,128)(2,1)} fusion(bf16[64,12800]{0,1:T(8,128)(2,1)S(1)} %concatenate.43, s32[12288]{0:T(1024)S(1)} %copy-done.33), kind=kCustom, calls=%fused_computation.26.clone | custom fusion | bytes 3194880 | tf_op jit(solution)/shard_map/jit(_take)/gather | solution.py:73
  680.5 44.0 %gather_fusion.10 = bf16[12288,64]{1,0:T(8,128)(2,1)} fusion(bf16[64,12800]{0,1:T(8,128)(2,1)} %concatenate.37, s32[12288]{0:T(1024)S(1)} %copy-done.33), kind=kCustom, calls=%fused_computation.8.clone | custom fusion | bytes 3194880 | tf_op jit(solution)/shard_map/jit(_take)/gather | solution.py:73
  724.4 43.3 %gather_fusion.27 = bf16[12288,64]{1,0:T(8,128)(2,1)} fusion(bf16[64,12800]{0,1:T(8,128)(2,1)S(1)} %concatenate.43, s32[12288]{0:T(1024)S(1)} %copy-done.30), kind=kCustom, calls=%fused_computation.25.clone | custom fusion | bytes 3194880 | tf_op jit(solution)/shard_map/jit(_take)/gather | solution.py:73
  767.7 43.8 %gather_fusion.9 = bf16[12288,64]{1,0:T(8,128)(2,1)} fusion(bf16[64,12800]{0,1:T(8,128)(2,1)} %concatenate.37, s32[12288]{0:T(1024)S(1)} %copy-done.30), kind=kCustom, calls=%fused_computation.7.clone | custom fusion | bytes 3194880 | tf_op jit(solution)/shard_map/jit(_take)/gather | solution.py:73
  811.5 43.3 %gather_fusion.20 = bf16[12288,64]{1,0:T(8,128)(2,1)} fusion(bf16[64,12800]{0,1:T(8,128)(2,1)S(1)} %concatenate.43, s32[12288]{0:T(1024)S(1)} %broadcast_clamp_fusion.8), kind=kCustom, calls=%fused_computation.18.clone | custom fusion | bytes 3194880 | tf_op jit(solution)/shard_map/jit(_take)/gather | solution.py:73
  854.8 43.9 %gather_fusion.2 = bf16[12288,64]{1,0:T(8,128)(2,1)} fusion(bf16[64,12800]{0,1:T(8,128)(2,1)} %concatenate.37, s32[12288]{0:T(1024)S(1)} %broadcast_clamp_fusion.8), kind=kCustom, calls=%fused_computation.clone | custom fusion | bytes 3194880 | tf_op jit(solution)/shard_map/jit(_take)/gather | solution.py:73
  905.6 4.5 copy.145
  971.5 4.5 copy.152
  983.7 4.9 copy.143
  991.0 4.4 copy.122
  1037.2 43.3 %gather_fusion.37 = bf16[12288,64]{1,0:T(8,128)(2,1)} fusion(bf16[64,12800]{0,1:T(8,128)(2,1)S(1)} %concatenate.45, s32[12288]{0:T(1024)S(1)} %copy-done.33), kind=kCustom, calls=%fused_computation.35.clone | custom fusion | bytes 3194880 | tf_op jit(solution)/shard_map/jit(_take)/gather | solution.py:73
  1080.5 43.3 %gather_fusion.36 = bf16[12288,64]{1,0:T(8,128)(2,1)} fusion(bf16[64,12800]{0,1:T(8,128)(2,1)S(1)} %concatenate.45, s32[12288]{0:T(1024)S(1)} %copy-done.30), kind=kCustom, calls=%fused_computation.34.clone | custom fusion | bytes 3194880 | tf_op jit(solution)/shard_map/jit(_take)/gather | solution.py:73
  1126.5 4.6 copy.131
  1134.5 43.7 %gather_fusion.19 = bf16[12288,64]{1,0:T(8,128)(2,1)} fusion(bf16[64,12800]{0,1:T(8,128)(2,1)} %concatenate.41, s32[12288]{0:T(1024)S(1)} %copy-done.33), kind=kCustom, calls=%fused_computation.17.clone | custom fusion | bytes 3194880 | tf_op jit(solution)/shard_map/jit(_take)/gather | solution.py:73
  1178.2 43.8 %gather_fusion.18 = bf16[12288,64]{1,0:T(8,128)(2,1)} fusion(bf16[64,12800]{0,1:T(8,128)(2,1)} %concatenate.41, s32[12288]{0:T(1024)S(1)} %copy-done.30), kind=kCustom, calls=%fused_computation.16.clone | custom fusion | bytes 3194880 | tf_op jit(solution)/shard_map/jit(_take)/gather | solution.py:73
  1222.0 43.3 %gather_fusion.35 = bf16[12288,64]{1,0:T(8,128)(2,1)} fusion(bf16[64,12800]{0,1:T(8,128)(2,1)S(1)} %concatenate.45, s32[12288]{0:T(1024)S(1)} %copy-done.34), kind=kCustom, calls=%fused_computation.33.clone | custom fusion | bytes 3194880 | tf_op jit(solution)/shard_map/jit(_take)/gather | solution.py:73
  1265.3 43.9 %gather_fusion.17 = bf16[12288,64]{1,0:T(8,128)(2,1)} fusion(bf16[64,12800]{0,1:T(8,128)(2,1)} %concatenate.41, s32[12288]{0:T(1024)S(1)} %copy-done.34), kind=kCustom, calls=%fused_computation.15.clone | custom fusion | bytes 3194880 | tf_op jit(solution)/shard_map/jit(_take)/gather | solution.py:73
  1309.2 43.3 %gather_fusion.34 = bf16[12288,64]{1,0:T(8,128)(2,1)} fusion(bf16[64,12800]{0,1:T(8,128)(2,1)S(1)} %concatenate.45, s32[12288]{0:T(1024)S(1)} %get-tuple-element.41), kind=kCustom, calls=%fused_computation.32.clone | custom fusion | bytes 3194880 | tf_op jit(solution)/shard_map/jit(_take)/gather | solution.py:73
  1352.5 43.8 %gather_fusion.16 = bf16[12288,64]{1,0:T(8,128)(2,1)} fusion(bf16[64,12800]{0,1:T(8,128)(2,1)} %concatenate.41, s32[12288]{0:T(1024)S(1)} %get-tuple-element.41), kind=kCustom, calls=%fused_computation.14.clone | custom fusion | bytes 3194880 | tf_op jit(solution)/shard_map/jit(_take)/gather | solution.py:73
  1396.3 43.3 %gather_fusion.33 = bf16[12288,64]{1,0:T(8,128)(2,1)} fusion(bf16[64,12800]{0,1:T(8,128)(2,1)S(1)} %concatenate.45, s32[12288]{0:T(1024)S(1)} %copy-done.32), kind=kCustom, calls=%fused_computation.31.clone | custom fusion | bytes 3194880 | tf_op jit(solution)/shard_map/jit(_take)/gather | solution.py:73
  1439.6 43.8 %gather_fusion.15 = bf16[12288,64]{1,0:T(8,128)(2,1)} fusion(bf16[64,12800]{0,1:T(8,128)(2,1)} %concatenate.41, s32[12288]{0:T(1024)S(1)} %copy-done.32), kind=kCustom, calls=%fused_computation.13.clone | custom fusion | bytes 3194880 | tf_op jit(solution)/shard_map/jit(_take)/gather | solution.py:73
  1483.4 43.3 %gather_fusion.32 = bf16[12288,64]{1,0:T(8,128)(2,1)} fusion(bf16[64,12800]{0,1:T(8,128)(2,1)S(1)} %concatenate.45, s32[12288]{0:T(1024)S(1)} %copy-done.27), kind=kCustom, calls=%fused_computation.30.clone | custom fusion | bytes 3194880 | tf_op jit(solution)/shard_map/jit(_take)/gather | solution.py:73
  1526.6 43.9 %gather_fusion.14 = bf16[12288,64]{1,0:T(8,128)(2,1)} fusion(bf16[64,12800]{0,1:T(8,128)(2,1)} %concatenate.41, s32[12288]{0:T(1024)S(1)} %copy-done.27), kind=kCustom, calls=%fused_computation.12.clone | custom fusion | bytes 3194880 | tf_op jit(solution)/shard_map/jit(_take)/gather | solution.py:73
  1570.6 43.3 %gather_fusion.31 = bf16[12288,64]{1,0:T(8,128)(2,1)} fusion(bf16[64,12800]{0,1:T(8,128)(2,1)S(1)} %concatenate.45, s32[12288]{0:T(1024)S(1)} %copy-done.29), kind=kCustom, calls=%fused_computation.29.clone | custom fusion | bytes 3194880 | tf_op jit(solution)/shard_map/jit(_take)/gather | solution.py:73
  1613.9 43.8 %gather_fusion.13 = bf16[12288,64]{1,0:T(8,128)(2,1)} fusion(bf16[64,12800]{0,1:T(8,128)(2,1)} %concatenate.41, s32[12288]{0:T(1024)S(1)} %copy-done.29), kind=kCustom, calls=%fused_computation.11.clone | custom fusion | bytes 3194880 | tf_op jit(solution)/shard_map/jit(_take)/gather | solution.py:73
  1657.7 43.3 %gather_fusion.30 = bf16[12288,64]{1,0:T(8,128)(2,1)} fusion(bf16[64,12800]{0,1:T(8,128)(2,1)S(1)} %concatenate.45, s32[12288]{0:T(1024)S(1)} %copy-done.25), kind=kCustom, calls=%fused_computation.28.clone | custom fusion | bytes 3194880 | tf_op jit(solution)/shard_map/jit(_take)/gather | solution.py:73
  1701.0 43.3 %gather_fusion.29 = bf16[12288,64]{1,0:T(8,128)(2,1)} fusion(bf16[64,12800]{0,1:T(8,128)(2,1)S(1)} %concatenate.45, s32[12288]{0:T(1024)S(1)} %broadcast_clamp_fusion.8), kind=kCustom, calls=%fused_computation.27.clone | custom fusion | bytes 3194880 | tf_op jit(solution)/shard_map/jit(_take)/gather | solution.py:73
  1744.3 44.1 %gather_fusion.11 = bf16[12288,64]{1,0:T(8,128)(2,1)} fusion(bf16[64,12800]{0,1:T(8,128)(2,1)} %concatenate.41, s32[12288]{0:T(1024)S(1)} %broadcast_clamp_fusion.8), kind=kCustom, calls=%fused_computation.9.clone | custom fusion | bytes 3194880 | tf_op jit(solution)/shard_map/jit(_take)/gather | solution.py:73
  1788.4 43.3 %gather_fusion.12 = bf16[12288,64]{1,0:T(8,128)(2,1)} fusion(bf16[64,12800]{0,1:T(8,128)(2,1)S(1)} %copy-done, s32[12288]{0:T(1024)S(1)} %copy-done.25), kind=kCustom, calls=%fused_computation.10.clone | custom fusion | bytes 3194880 | tf_op jit(solution)/shard_map/jit(_take)/gather | solution.py:73
  1857.1 4.6 copy.161
  1908.1 4.5 copy.157
  1962.8 162.9 %all-reduce.7.cloned.1.call-done = (f32[27,64,64]{1,2,0:T(8,128)}, f32[27,64,64]{1,2,0:T(8,128)}) async-done(((f32[27,64,64]{1,2,0:T(8,128)}, f32[27,64,64]{1,2,0:T(8,128)}), (f32[27,64,64]{1,2,0:T(8,128)}, f32[27,64,64]{1,2,0:T(8,128)})) %all-reduce.7.cloned.1.call-update) | async-done | bytes 884752 | tf_op jit(solution)/shard_map/psum | solution.py:145
  (391 shorter events, 295.9 us)
Async XLA Ops:
  7.2 15.2 copy-start.78
  7.2 14.6 copy-start.102
  7.2 2118.5 %all-reduce.7.cloned.1.call-start = ((), (), s32[]{:S(2)}) async-start(), calls=%async_computation | async-start | bytes 3538944 | tf_op jit(solution)/shard_map/psum | solution.py:145
  9.3 96.1 %collective-permute-start.1 = (bf16[8,64,512]{2,1,0:T(8,128)(2,1)S(1)}, bf16[8,64,512]{2,1,0:T(8,128)(2,1)}, u32[]{:S(2)}, u32[]{:S(2)}) collective-permute-start(bf16[8,64,512]{2,1,0:T(8,128)(2,1)S(1)} %get-tuple-element.31), channel_id=1, source_target_pairs={{1,0},{2,1},{3,2},{4,3},{5,4},{6,5},{7,6},{8,7},{9,8},{10,9},{11,1... | collective-permute-start | bytes 1572872 | tf_op jit(solution)/shard_map/ppermute | solution.py:13
  12.6 92.7 %collective-permute-start = (bf16[8,64,512]{2,1,0:T(8,128)(2,1)S(1)}, bf16[8,64,512]{2,1,0:T(8,128)(2,1)}, u32[]{:S(2)}, u32[]{:S(2)}) collective-permute-start(bf16[8,64,512]{2,1,0:T(8,128)(2,1)S(1)} %get-tuple-element.31), channel_id=1, source_target_pairs={{0,1},{1,2},{2,3},{3,4},{4,5},{5,6},{6,7},{7,8},{8,9},{9,10},{10,1... | collective-permute-start | bytes 1572872 | tf_op jit(solution)/shard_map/ppermute | solution.py:13
  16.2 84.3 %collective-permute-start.5 = (bf16[8,64,512]{2,1,0:T(8,128)(2,1)S(1)}, bf16[8,64,512]{2,1,0:T(8,128)(2,1)S(1)}, u32[]{:S(2)}, u32[]{:S(2)}) collective-permute-start(bf16[8,64,512]{2,1,0:T(8,128)(2,1)S(1)} %get-tuple-element.30), channel_id=1, source_target_pairs={{1,0},{2,1},{3,2},{4,3},{5,4},{6,5},{7,6},{8,7},{9,8},{10,9},{11,1... | collective-permute-start | bytes 1572872 | tf_op jit(solution)/shard_map/ppermute | solution.py:13
  18.1 83.2 %collective-permute-start.4 = (bf16[8,64,512]{2,1,0:T(8,128)(2,1)S(1)}, bf16[8,64,512]{2,1,0:T(8,128)(2,1)}, u32[]{:S(2)}, u32[]{:S(2)}) collective-permute-start(bf16[8,64,512]{2,1,0:T(8,128)(2,1)S(1)} %get-tuple-element.30), channel_id=1, source_target_pairs={{0,1},{1,2},{2,3},{3,4},{4,5},{5,6},{6,7},{7,8},{8,9},{9,10},{10,1... | collective-permute-start | bytes 1572872 | tf_op jit(solution)/shard_map/ppermute | solution.py:13
  84.0 4.7 copy-start.77
  91.7 5.2 copy-start.73
  96.9 322.0 %copy-start.26 = (s32[12288]{0:T(1024)}, s32[12288]{0:T(1024)S(1)}, u32[]{:S(2)}) copy-start(s32[12288]{0:T(1024)S(1)} %get-tuple-element.43) | copy-start | bytes 147460
  96.9 60.9 %copy-start.28 = (s32[12288]{0:T(1024)}, s32[12288]{0:T(1024)S(1)}, u32[]{:S(2)}) copy-start(s32[12288]{0:T(1024)S(1)} %get-tuple-element.44) | copy-start | bytes 147460
  96.9 147.9 %copy-start.24 = (s32[12288]{0:T(1024)}, s32[12288]{0:T(1024)S(1)}, u32[]{:S(2)}) copy-start(s32[12288]{0:T(1024)S(1)} %get-tuple-element.45) | copy-start | bytes 147460
  244.8 43.8 %copy-start.31 = (s32[12288]{0:T(1024)S(1)}, s32[12288]{0:T(1024)}, u32[]{:S(2)}) copy-start(s32[12288]{0:T(1024)} %get-tuple-element.42) | copy-start | bytes 147460
  418.9 43.9 %copy-start.34 = (s32[12288]{0:T(1024)S(1)}, s32[12288]{0:T(1024)}, u32[]{:S(2)}) copy-start(s32[12288]{0:T(1024)} %get-tuple-element.40) | copy-start | bytes 147460
  593.4 43.8 %copy-start.33 = (s32[12288]{0:T(1024)S(1)}, s32[12288]{0:T(1024)}, u32[]{:S(2)}) copy-start(s32[12288]{0:T(1024)} %get-tuple-element.38) | copy-start | bytes 147460
  680.5 44.0 %copy-start.30 = (s32[12288]{0:T(1024)S(1)}, s32[12288]{0:T(1024)}, u32[]{:S(2)}) copy-start(s32[12288]{0:T(1024)} %get-tuple-element.39) | copy-start | bytes 147460
  898.8 4.4 copy-start.19
  905.6 4.5 copy-start.18
  971.4 4.5 copy-start.7
  983.7 4.9 copy-start.5
  991.0 4.5 copy-start.3
  1001.7 4.5 copy-start.67
  1001.7 4.8 copy-start.68
  1001.7 5.1 copy-start.69
  1009.3 12.6 copy-start.38
  1009.5 21.1 collective-permute-start.7
  1011.5 19.1 collective-permute-start.6
  1016.1 6.3 copy-start.35
  1016.1 107.6 %collective-permute-start.3 = (bf16[8,64,512]{2,0,1:T(8,128)(2,1)}, bf16[8,64,512]{2,0,1:T(8,128)(2,1)}, u32[]{:S(2)}, u32[]{:S(2)}) collective-permute-start(bf16[8,64,512]{2,0,1:T(8,128)(2,1)} %bitcast.33), channel_id=1, source_target_pairs={{1,0},{2,1},{3,2},{4,3},{5,4},{6,5},{7,6},{8,7},{9,8},{10,9},{11,1... | collective-permute-start | bytes 1572872 | tf_op jit(solution)/shard_map/ppermute | solution.py:13
  1018.2 105.6 %collective-permute-start.2 = (bf16[8,64,512]{2,0,1:T(8,128)(2,1)}, bf16[8,64,512]{2,0,1:T(8,128)(2,1)}, u32[]{:S(2)}, u32[]{:S(2)}) collective-permute-start(bf16[8,64,512]{2,0,1:T(8,128)(2,1)} %bitcast.33), channel_id=1, source_target_pairs={{0,1},{1,2},{2,3},{3,4},{4,5},{5,6},{6,7},{7,8},{8,9},{9,10},{10,1... | collective-permute-start | bytes 1572872 | tf_op jit(solution)/shard_map/ppermute | solution.py:13
  1352.5 43.8 %copy-start.32 = (s32[12288]{0:T(1024)S(1)}, s32[12288]{0:T(1024)}, u32[]{:S(2)}) copy-start(s32[12288]{0:T(1024)} %get-tuple-element.42) | copy-start | bytes 147460
  1439.6 43.8 %copy-start.27 = (s32[12288]{0:T(1024)S(1)}, s32[12288]{0:T(1024)}, u32[]{:S(2)}) copy-start(s32[12288]{0:T(1024)} %copy-done.26) | copy-start | bytes 147460
  1526.6 44.0 %copy-start.29 = (s32[12288]{0:T(1024)S(1)}, s32[12288]{0:T(1024)}, u32[]{:S(2)}) copy-start(s32[12288]{0:T(1024)} %copy-done.28) | copy-start | bytes 147460
  1613.9 43.8 %copy-start.25 = (s32[12288]{0:T(1024)S(1)}, s32[12288]{0:T(1024)}, u32[]{:S(2)}) copy-start(s32[12288]{0:T(1024)} %copy-done.24) | copy-start | bytes 147460
  1744.3 44.1 %copy-start = (bf16[64,12800]{0,1:T(8,128)(2,1)S(1)}, bf16[64,12800]{0,1:T(8,128)(2,1)}, u32[]{:S(2)}) copy-start(bf16[64,12800]{0,1:T(8,128)(2,1)} %concatenate.41) | copy-start | bytes 4915204
  1835.9 4.4 copy-start.80
  1835.9 7.4 copy-start.9
  1843.3 5.5 copy-start.82
  1845.7 6.0 copy-start.16
  1857.1 4.6 copy-start.85
  1857.1 7.5 copy-start.14
  1870.0 7.4 copy-start.12
  1882.7 4.4 copy-start.91
  1882.7 7.4 copy-start.10
  1895.3 4.5 copy-start.94
  1895.3 7.4 copy-start.8
  1908.1 4.5 copy-start.97
  1908.1 7.4 copy-start.6
  (64 other events, 155.7 us)
Sparse Core Ops, SparseCore 0:
  1957.5 168.0 all-reduce.6
where the time goes:
time: 2150 us; the launch traced here: 2140 us
  local copies, waits for them, and re-layouts  1800 us (84%)
  waiting for transfers between devices  163 us (8%)
  matrix products  110 us (5%)
  starting transfers between devices  23.8 us (1%)
  other arithmetic  21.7 us (1%)
    gather x72, local copies, waits for them, and re-layouts, convolve(): shifted = jnp.take(pool_flat, gather_rows[3 * group:3 * group + 3], axis=1)  1690 us
    psum x1, waiting for transfers between devices, local(): sum_one, sum_two = lax.psum((local_one, local_two), ('wide', 'narrow'))  163 us
    dot_general x36, matrix products, convolve(): jnp.einsum('qcm,cpq->pm', shifted, weights[3 * group:3 * group + 3], pref...  100 us
  transfers between devices with their start and end apart: 9, of which 1 were waited for; matrix products, arithmetic and copies ran while one was open for 9% of the time, Pallas kernels for 0%

commit v1 on v0

v1 whole, which is shorter than its diff:
```python
import jax
import jax.numpy as jnp
from jax import lax
from jax.experimental import pallas as pl
from jax.experimental.pallas import tpu as pltpu
from jax.sharding import PartitionSpec as P

AXES = ("wide", "narrow")
SLOTS = 8
EDGE = 8
VOX = EDGE**3
CH = 64
LANES = 2 * CH
NEAR = 4
POOL = SLOTS + 2 * NEAR + 1
ZERO = POOL - 1
SLAB = (EDGE + 2) * EDGE
TILE_ROWS = (EDGE + 2) * SLAB
ROWS = EDGE * SLAB
TERMS = 2048
VMEM = 48 * 1024 * 1024
F32 = jnp.float32
BF16 = jnp.bfloat16

whole_vmem = pl.BlockSpec(memory_space=pltpu.VMEM)
whole_smem = pl.BlockSpec(memory_space=pltpu.SMEM)
anywhere = pl.BlockSpec(memory_space=pl.ANY)


def lower_half(shape):
    return lax.broadcasted_iota(jnp.int32, shape, len(shape) - 1) < CH


def pack_kernel(position, neighbours, features, cotangent, occupancy, fields, ahead, behind, chosen):
    for b in range(SLOTS):
        active = occupancy[b : b + 1, :].astype(F32)
        both = jnp.concatenate([features[b], cotangent[b]], axis=0).astype(F32) * active
        fields[b] = both.T.astype(BF16)
    here = position[0] * SLOTS
    for r in range(SLOTS):
        chosen[0, r] = 0
        chosen[1, r] = 0
    count_ahead = jnp.int32(0)
    count_behind = jnp.int32(0)
    for b in range(SLOTS):
        highest = jnp.int32(-1)
        lowest = jnp.int32(1 << 20)
        for d in range(26):
            slot = neighbours[b, d]
            highest = jnp.maximum(highest, slot)
            lowest = jnp.minimum(lowest, jnp.where(slot < 0, 1 << 20, slot))
        chosen[0, jnp.minimum(count_ahead, NEAR)] = b
        chosen[1, jnp.minimum(count_behind, NEAR)] = b
        count_ahead += (highest >= here + SLOTS).astype(jnp.int32)
        count_behind += (lowest < here).astype(jnp.int32)
    for r in range(NEAR):
        ahead[r] = fields[chosen[0, r]]
        behind[r] = fields[chosen[1, r]]


def pack(position, neighbours, features, cotangent, occupancy):
    return pl.pallas_call(
        pack_kernel,
        out_shape=(
            jax.ShapeDtypeStruct((SLOTS, VOX, LANES), BF16),
            jax.ShapeDtypeStruct((NEAR, VOX, LANES), BF16),
            jax.ShapeDtypeStruct((NEAR, VOX, LANES), BF16),
            jax.ShapeDtypeStruct((2, SLOTS), jnp.int32),
        ),
        in_specs=[whole_smem, whole_smem, whole_vmem, whole_vmem, whole_vmem],
        out_specs=(whole_vmem, whole_vmem, whole_vmem, whole_smem),
        compiler_params=pltpu.CompilerParams(vmem_limit_bytes=VMEM),
        name="pack",
    )(position, neighbours, features, cotangent, occupancy)


def weight_block(kernel, flip, a, rows, columns):
    def piece(c, e):
        if c is None or e is None:
            return jnp.zeros((CH, CH), F32)
        n = 9 * a + 3 * c + e
        return kernel[26 - n if flip else n].astype(F32)

    if flip:
        block = jnp.concatenate(
            [jnp.concatenate([piece(c, e) for c in columns], axis=1) for e in rows], axis=0
        )
    else:
        block = jnp.concatenate(
            [jnp.concatenate([piece(c, e) for e in rows], axis=1) for c in columns], axis=0
        ).T
    return block.astype(BF16)


def weight_field(kernel, flip, field, target):
    rows = ((0, 1), (2, None)) if field == 0 else ((None, 2), (0, 1))
    columns = ((0, 1), (2, None)) if field == 0 else ((1, 0), (None, 2))
    for a in range(3):
        for r in range(2):
            for s in range(2):
                target[
                    field, a, r * LANES : (r + 1) * LANES, s * LANES : (s + 1) * LANES
                ] = weight_block(kernel, flip, a, rows[r], columns[s])


def prepare_kernel(position, neighbours, kernel_one, kernel_two, first, second, lookup, flags, base):
    weight_field(kernel_one, False, 0, first)
    weight_field(kernel_two, True, 1, first)
    weight_field(kernel_two, False, 0, second)
    weight_field(kernel_one, True, 1, second)
    start = (position[0] - 1) * SLOTS
    for s in range(3 * SLOTS + 1):
        flags[s] = 0
    for b in range(SLOTS):
        for d in range(26):
            slot = neighbours[b, d]
            flags[jnp.where(slot < 0, 3 * SLOTS, slot - start)] = 1
    count = jnp.int32(0)
    for s in range(SLOTS):
        base[s] = SLOTS + jnp.minimum(count, NEAR - 1)
        count += flags[s]
        base[SLOTS + s] = s
    count = jnp.int32(0)
    for s in range(SLOTS):
        base[2 * SLOTS + s] = SLOTS + NEAR + jnp.minimum(count, NEAR - 1)
        count += flags[2 * SLOTS + s]
    base[3 * SLOTS] = ZERO
    for b in range(SLOTS):
        lookup[b * 27 + 13] = b
        for d in range(26):
            slot = neighbours[b, d]
            lookup[b * 27 + d + (d > 12)] = base[jnp.where(slot < 0, 3 * SLOTS, slot - start)]


def prepare(position, neighbours, kernel_one, kernel_two):
    return pl.pallas_call(
        prepare_kernel,
        out_shape=(
            jax.ShapeDtypeStruct((2, 3, 2 * LANES, 2 * LANES), BF16),
            jax.ShapeDtypeStruct((2, 3, 2 * LANES, 2 * LANES), BF16),
            jax.ShapeDtypeStruct((27 * SLOTS,), jnp.int32),
        ),
        in_specs=[whole_smem, whole_smem, whole_vmem, whole_vmem],
        out_specs=(whole_vmem, whole_vmem, whole_smem),
        scratch_shapes=[pltpu.SMEM((32,), jnp.int32), pltpu.SMEM((32,), jnp.int32)],
        compiler_params=pltpu.CompilerParams(vmem_limit_bytes=VMEM),
        cost_estimate=pl.CostEstimate(flops=4000000, bytes_accessed=2000000, transcendentals=0),
        name="prepare",
    )(position, neighbours, kernel_one, kernel_two)


def fill_pool(own, before, after, pool, sems):
    copies = [
        pltpu.make_async_copy(own, pool.at[pl.ds(0, SLOTS)], sems.at[0]),
        pltpu.make_async_copy(before, pool.at[pl.ds(SLOTS, NEAR)], sems.at[1]),
        pltpu.make_async_copy(after, pool.at[pl.ds(SLOTS + NEAR, NEAR)], sems.at[2]),
    ]
    for copy in copies:
        copy.start()
    pool[ZERO] = jnp.zeros((VOX, LANES), BF16)
    for copy in copies:
        copy.wait()


def extend(pool, lookup, b, tile):
    def slabs(bricks, first, count):
        return [
            pool[brick, first : first + count, :].astype(F32).reshape(count // EDGE, EDGE, LANES)
            for brick in bricks
        ]

    for i in range(EDGE + 2):
        side = (i + EDGE - 1) // EDGE
        source = (i - 1) % EDGE
        bricks = [
            [lookup[b * 27 + side * 9 + j * 3 + k] for k in range(3)] for j in range(3)
        ]
        left = slabs(bricks[0], source * 64 + 48, 16)
        middle = slabs(bricks[1], source * 64, 64)
        right = slabs(bricks[2], source * 64, 16)
        low, centre, high = [
            jnp.concatenate([left[k][1:2], middle[k], right[k][0:1]], axis=0) for k in range(3)
        ]
        along = lax.broadcasted_iota(jnp.int32, centre.shape, 1)
        first = pltpu.roll(jnp.where(along == EDGE - 1, low, centre), 1, 1)
        last = pltpu.roll(jnp.where(along == 0, high, centre), EDGE - 1, 1)
        first, centre, last = [m.reshape(SLAB, LANES) for m in (first, centre, last)]
        lower = lower_half((SLAB, LANES))
        crossed = pltpu.roll(jnp.where(lower, centre, first), CH, 1)
        rows = pl.ds(i * SLAB, SLAB)
        tile[rows, 0:LANES] = jnp.where(lower, first, crossed).astype(BF16)
        tile[rows, LANES : 2 * LANES] = last.astype(BF16)
        tile[rows, 2 * LANES : 3 * LANES] = jnp.where(lower, crossed, centre).astype(BF16)


def convolve(tile, weights):
    sums = []
    for field in range(2):
        total = None
        for a in range(3):
            part = jnp.dot(
                tile[a * SLAB : a * SLAB + ROWS, field * LANES : (field + 2) * LANES],
                weights[field, a],
                preferred_element_type=F32,
            )
            total = part if total is None else total + part
        sums.append(total)

    def block(field, half):
        return sums[field][:, half * LANES : (half + 1) * LANES].reshape(
            EDGE, EDGE + 2, EDGE, LANES
        )

    zero, one = block(0, 0), block(1, 0)
    shape = (EDGE, EDGE, EDGE, LANES)
    lower = lower_half(shape)
    straight = jnp.where(lower, zero[:, 0:8], one[:, 0:8])
    crossed = jnp.where(lower, one[:, 1:9], zero[:, 1:9]).reshape(VOX, LANES)
    ends = block(0, 1)[:, 2:10] + block(1, 1)[:, 2:10]
    return (straight + ends).reshape(VOX, LANES) + pltpu.roll(crossed, CH, 1)


def row_mask(occupancy, b):
    active = occupancy[pl.ds(b, 1), :].astype(F32)
    return jnp.broadcast_to(active, (LANES, VOX)).T


def first_kernel(
    lookup, chosen, occupancy, weights, own, before, after,
    result, ahead, behind, terms, pool, tile, sum_one, sum_two, sems,
):
    fill_pool(own, before, after, pool, sems)
    sum_one[...] = jnp.zeros_like(sum_one)
    sum_two[...] = jnp.zeros_like(sum_two)

    @pl.loop(0, SLOTS)
    def _(b):
        extend(pool, lookup, b, tile)
        both = convolve(tile, weights)
        lower = lower_half((VOX, LANES))
        preact = jnp.where(lower, both, pltpu.roll(both, CH, 1))
        s = jax.nn.sigmoid(preact)
        value = jnp.where(lower, preact * s, both * s * (1.0 + preact * (1.0 - s)))
        value = value * row_mask(occupancy, b)
        result[b] = value.astype(BF16)
        cube = value.reshape(EDGE, EDGE, EDGE, LANES)
        turned = []
        for c in range(3):
            parts = [cube]
            if c > 0:
                parts.insert(0, jnp.zeros((EDGE, c, EDGE, LANES), F32))
            if c < 2:
                parts.append(jnp.zeros((EDGE, 2 - c, EDGE, LANES), F32))
            padded = jnp.concatenate(parts, axis=1).reshape(ROWS, LANES)
            turned.append(padded.astype(BF16).T)
        hidden = jnp.concatenate([t[:CH] for t in turned], axis=0)
        grad_pre = jnp.concatenate([t[CH:] for t in turned], axis=0)
        for a in range(3):
            rows = pl.ds(a * SLAB, ROWS)
            sum_one[a] += jnp.dot(
                grad_pre, tile[rows, 0 : 2 * LANES], preferred_element_type=F32
            )
            sum_two[a] += jnp.dot(
                hidden, tile[rows, LANES : 3 * LANES], preferred_element_type=F32
            )

    for r in range(NEAR):
        ahead[r] = result[chosen[0, r]]
        behind[r] = result[chosen[1, r]]
    part = 3 * CH
    for a in range(3):
        start = a * 3 * part
        terms[start : start + part] = sum_one[a, :, 0:LANES].astype(BF16)
        terms[start + part : start + 2 * part] = sum_two[a, :, LANES:].astype(BF16)
        terms[start + 2 * part : start + 3 * part] = jnp.where(
            lower_half((part, LANES)), sum_one[a, :, LANES:], sum_two[a, :, 0:LANES]
        ).astype(BF16)
    terms[9 * part :] = jnp.zeros((TERMS - 9 * part, LANES), BF16)


def first_stage(lookup, chosen, occupancy, weights, own, before, after):
    return pl.pallas_call(
        first_kernel,
        out_shape=(
            jax.ShapeDtypeStruct((SLOTS, VOX, LANES), BF16),
            jax.ShapeDtypeStruct((NEAR, VOX, LANES), BF16),
            jax.ShapeDtypeStruct((NEAR, VOX, LANES), BF16),
            jax.ShapeDtypeStruct((TERMS, LANES), BF16),
        ),
        in_specs=[whole_smem, whole_smem, whole_vmem, whole_vmem, anywhere, anywhere, anywhere],
        out_specs=(whole_vmem,) * 4,
        scratch_shapes=[
            pltpu.VMEM((POOL, VOX, LANES), BF16),
            pltpu.VMEM((TILE_ROWS, 3 * LANES), BF16),
            pltpu.VMEM((3, 3 * CH, 2 * LANES), F32),
            pltpu.VMEM((3, 3 * CH, 2 * LANES), F32),
            pltpu.SemaphoreType.DMA((3,)),
        ],
        compiler_params=pltpu.CompilerParams(vmem_limit_bytes=VMEM),
        cost_estimate=pl.CostEstimate(
            flops=8000000000, bytes_accessed=6000000, transcendentals=600000
        ),
        name="first_stage",
    )(lookup, chosen, occupancy, weights, own, before, after)


def second_kernel(
    lookup, occupancy, weights, own, before, after, output, grad_in, pool, tile, sems
):
    fill_pool(own, before, after, pool, sems)

    @pl.loop(0, SLOTS)
    def _(b):
        extend(pool, lookup, b, tile)
        both = convolve(tile, weights).T * occupancy[pl.ds(b, 1), :].astype(F32)
        output[b] = both[:CH].astype(BF16)
        grad_in[b] = both[CH:].astype(BF16)


def second_stage(lookup, occupancy, weights, own, before, after):
    return pl.pallas_call(
        second_kernel,
        out_shape=(
            jax.ShapeDtypeStruct((SLOTS, CH, VOX), BF16),
            jax.ShapeDtypeStruct((SLOTS, CH, VOX), BF16),
        ),
        in_specs=[whole_smem, whole_vmem, whole_vmem, anywhere, anywhere, anywhere],
        out_specs=(whole_vmem,) * 2,
        scratch_shapes=[
            pltpu.VMEM((POOL, VOX, LANES), BF16),
            pltpu.VMEM((TILE_ROWS, 3 * LANES), BF16),
            pltpu.SemaphoreType.DMA((3,)),
        ],
        compiler_params=pltpu.CompilerParams(vmem_limit_bytes=VMEM),
        cost_estimate=pl.CostEstimate(
            flops=8000000000, bytes_accessed=6000000, transcendentals=0
        ),
        name="second_stage",
    )(lookup, occupancy, weights, own, before, after)


def combine_kernel(blocks, spread):
    count, rows = blocks.shape[0], blocks.shape[1]
    total = jnp.zeros((rows, LANES), F32)
    for d in range(count):
        total += blocks[d].astype(F32)
    spread[...] = jnp.broadcast_to(total.astype(BF16)[None], spread.shape)


def combine(blocks):
    return pl.pallas_call(
        combine_kernel,
        out_shape=jax.ShapeDtypeStruct(blocks.shape, BF16),
        in_specs=[whole_vmem],
        out_specs=whole_vmem,
        name="combine",
    )(blocks)


def unpack_kernel(scale, sums, grad_one, grad_two):
    part = 3 * CH
    for a in range(3):
        for c in range(3):
            start = a * 3 * part + c * CH
            n = 9 * a + 3 * c

            def block(which):
                return sums[start + which * part : start + which * part + CH].astype(F32) * scale

            one, two, last = block(0), block(1).T, block(2)
            grad_one[n] = one[:, :CH]
            grad_one[n + 1] = one[:, CH:]
            grad_one[n + 2] = last[:, :CH]
            grad_two[26 - n] = two[:CH]
            grad_two[25 - n] = two[CH:]
            grad_two[24 - n] = last.T[CH:]


def unpack(scale, sums):
    def kernel(*refs):
        unpack_kernel(scale, *refs)

    return pl.pallas_call(
        kernel,
        out_shape=(
            jax.ShapeDtypeStruct((27, CH, CH), F32),
            jax.ShapeDtypeStruct((27, CH, CH), F32),
        ),
        in_specs=[whole_vmem],
        out_specs=(whole_vmem,) * 2,
        name="unpack",
    )(sums)


def exchange(ahead, behind, devices):
    before = lax.ppermute(ahead, AXES, [(k, k + 1) for k in range(devices - 1)])
    after = lax.ppermute(behind, AXES, [(k + 1, k) for k in range(devices - 1)])
    return before, after


def local(devices, features, kernel_one, kernel_two, cotangent, neighbours, occupancy):
    position = lax.axis_index(AXES).astype(jnp.int32).reshape(1)
    fields, ahead, behind, chosen = pack(position, neighbours, features, cotangent, occupancy)
    before, after = exchange(ahead, behind, devices)
    first, second, lookup = prepare(position, neighbours, kernel_one, kernel_two)
    result, ahead, behind, terms = first_stage(
        lookup, chosen, occupancy, first, fields, before, after
    )
    before, after = exchange(ahead, behind, devices)
    terms = lax.all_to_all(terms, AXES, 0, 0, tiled=True)
    output, grad_in = second_stage(lookup, occupancy, second, result, before, after)
    spread = combine(terms.reshape(devices, TERMS // devices, LANES)).reshape(TERMS, LANES)
    sums = lax.all_to_all(spread, AXES, 0, 0, tiled=True)
    scale = float((SLOTS * VOX * devices) ** -0.5)
    grad_one, grad_two = unpack(scale, sums)
    return output, grad_in, grad_one, grad_two


def solution(mesh):
    devices = mesh.shape["wide"] * mesh.shape["narrow"]
    bricks = P(AXES, None, None)
    in_specs = (bricks, P(), P(), bricks, P(AXES, None), P(AXES, None))
    out_specs = (bricks, bricks, P(), P())

    def run(*arrays):
        return local(devices, *arrays)

    return jax.shard_map(
        run, mesh=mesh, in_specs=in_specs, out_specs=out_specs, check_vma=False
    )
```

time: 2150 us -> 91.2 us (0.04)
  local copies, waits for them, and re-layouts: 1800 us -> 6.47 us
  waiting for transfers between devices: 163 us -> 9.34 us
  matrix products: 110 us -> 0 us
  Pallas kernels: 0 us -> 31.4 us
  blocking collectives: 0 us -> 25.6 us
  other arithmetic: 21.7 us -> 0 us
    gather x75 -> x0, local copies, waits for them, and re-layouts: 1750 us -> none  [the longest x72 1690 us: convolve(): shifted = jnp.take(pool_flat, gather_rows[3 * group:3 * group + 3], axis=1)]
    psum x1 -> x0, waiting for transfers between devices: 163 us -> none  [local(): sum_one, sum_two = lax.psum((local_one, local_two), ('wide', 'narrow'))]
    dot_general x54 -> x0, matrix products: 110 us -> none  [the longest x36 100 us: convolve(): jnp.einsum('qcm,cpq->pm', shifted, weights[3 * group:3 * group + 3], pref...]
    pallas_call x0 -> x6, Pallas kernels: none -> 31.4 us  [the longest x1 13.3 us: first_stage(): pl.pallas_call(first_kernel, out_shape=(jax.ShapeDtypeStruct((SLOTS, VOX,...]
    all_to_all x0 -> x1, blocking collectives: none -> 25.6 us  [local(): terms = lax.all_to_all(terms, AXES, 0, 0, tiled=True)]
  transfers between devices with their start and end apart: 9 -> 5, of which waited for: 1 -> 3; matrix products, arithmetic and copies ran while one was open for 9% -> 0% of each run, Pallas kernels for 0% -> 15%
where the time goes in v1:
time: 91.2 us; the launch traced here: 90.7 us
  Pallas kernels  31.4 us (34%)
  blocking collectives  25.6 us (28%)
  starting transfers between devices  17 us (19%)
  waiting for transfers between devices  9.34 us (10%)
  local copies, waits for them, and re-layouts  6.47 us (7%)
    all_to_all x1, blocking collectives, local(): terms = lax.all_to_all(terms, AXES, 0, 0, tiled=True)  25.6 us
    pallas_call x1, Pallas kernels, first_stage(): pl.pallas_call(first_kernel, out_shape=(jax.ShapeDtypeStruct((SLOTS, VOX,...  13.3 us
    pallas_call x1, Pallas kernels, second_stage(): pl.pallas_call(second_kernel, out_shape=(jax.ShapeDtypeStruct((SLOTS, CH,...  9.3 us
    ppermute x2, starting transfers between devices, exchange(): before = lax.ppermute(ahead, AXES, [(k, k + 1) for k in range(devices - 1)])  6.84 us
    unnamed x18, local copies, waits for them, and re-layouts  6.47 us
    all_to_all x1, starting transfers between devices, local(): sums = lax.all_to_all(spread, AXES, 0, 0, tiled=True)  5.84 us
    ppermute x2, waiting for transfers between devices, exchange(): after = lax.ppermute(behind, AXES, [(k + 1, k) for k in range(devices - 1)])  4.4 us
    ppermute x2, starting transfers between devices, exchange(): after = lax.ppermute(behind, AXES, [(k + 1, k) for k in range(devices - 1)])  4.36 us
  transfers between devices with their start and end apart: 5, of which 3 were waited for; matrix products, arithmetic and copies ran while one was open for 0% of the time, Pallas kernels for 15%

profile of v1, /device:TPU:1, one launch (start us, length us, event | category | flops | bytes accessed | tf_op | source)
XLA Modules:
  0.0 90.7 jit_solution(16417049841262907865)
XLA Ops:
  0.6 0.0 copy-start.4
  0.6 0.7 copy-done.4
  1.4 0.0 copy-start
  1.4 1.0 %copy-done = bf16[8,64,512]{2,1,0:T(8,128)(2,1)S(1)} copy-done((bf16[8,64,512]{2,1,0:T(8,128)(2,1)S(1)}, bf16[8,64,512]{2,1,0:T(8,128)(2,1)}, u32[]{:S(2)}) %copy-start) | copy-done | bytes 524312
  2.4 0.0 copy-start.1
  2.4 1.0 %copy-done.1 = bf16[8,64,512]{2,1,0:T(8,128)(2,1)S(1)} copy-done((bf16[8,64,512]{2,1,0:T(8,128)(2,1)S(1)}, bf16[8,64,512]{2,1,0:T(8,128)(2,1)}, u32[]{:S(2)}) %copy-start.1) | copy-done | bytes 524312
  3.4 0.0 copy-start.5
  3.4 0.7 copy-done.5
  4.1 0.0 copy-start.2
  4.1 0.0 copy-start.3
  4.1 1.8 %pack.1 = (bf16[8,512,128]{2,1,0:T(8,128)(2,1)S(1)}, bf16[4,512,128]{2,1,0:T(8,128)(2,1)S(1)}, bf16[4,512,128]{2,1,0:T(8,128)(2,1)S(1)}, s32[2,8]{1,0:T(2,128)S(1)}) custom-call(s32[1]{0:T(128)} %bitcast.position, s32[8,26]{1,0:T(8,128)S(1)} %copy-done.5, bf16[8,64,512]{2,1,0:T(8,128)(2,1)S(1)} %copy-done, bf16[8,64,512]{2,1,0:T(8,128)(2,1)S(1)} %copy-done.1, ...), custom_call_target="tpu_custom_call" | custom-call | tf_op jit(solution)/shard_map/pack/pallas_call | solution.py:62
  5.9 4.9 %collective-permute-start = (bf16[4,512,128]{2,1,0:T(8,128)(2,1)S(1)}, bf16[4,512,128]{2,1,0:T(8,128)(2,1)S(1)}, u32[]{:S(2)}, u32[]{:S(2)}) collective-permute-start(bf16[4,512,128]{2,1,0:T(8,128)(2,1)S(1)} %get-tuple-element.24), channel_id=1, source_target_pairs={{0,1},{1,2},{2,3},{3,4},{4,5},{5,6},{6,7},{7,8},{8,9},{9,10},{10,1... | collective-permute-start | bytes 1572872 | tf_op jit(solution)/shard_map/ppermute | solution.py:396
  10.9 1.9 %collective-permute-start.1 = (bf16[4,512,128]{2,1,0:T(8,128)(2,1)S(1)}, bf16[4,512,128]{2,1,0:T(8,128)(2,1)S(1)}, u32[]{:S(2)}, u32[]{:S(2)}) collective-permute-start(bf16[4,512,128]{2,1,0:T(8,128)(2,1)S(1)} %get-tuple-element.25), channel_id=1, source_target_pairs={{1,0},{2,1},{3,2},{4,3},{5,4},{6,5},{7,6},{8,7},{9,8},{10,9},{11,1... | collective-permute-start | bytes 1572872 | tf_op jit(solution)/shard_map/ppermute | solution.py:397
  12.8 0.0 copy-done.2
  12.8 0.0 copy-done.3
  12.8 2.3 %prepare.1 = (bf16[2,3,256,256]{3,2,1,0:T(8,128)(2,1)S(1)}, bf16[2,3,256,256]{3,2,1,0:T(8,128)(2,1)S(1)}, s32[216]{0:T(256)S(1)}) custom-call(s32[1]{0:T(128)} %bitcast.position, s32[8,26]{1,0:T(8,128)S(1)} %copy-done.5, bf16[27,64,64]{2,1,0:T(8,128)(2,1)S(1)} %copy-done.2, bf16[27,64,64]{2,1,0:T(8,128)(2,1)S(1)} %copy-done.3), custom_call_target="tpu_custom_call" | custom-call | flops 4000000 | bytes 2000000 | tf_op jit(solution)/shard_map/prepare/pallas_call | solution.py:136
  15.1 1.8 %collective-permute-done.before = bf16[4,512,128]{2,1,0:T(8,128)(2,1)S(1)} collective-permute-done((bf16[4,512,128]{2,1,0:T(8,128)(2,1)S(1)}, bf16[4,512,128]{2,1,0:T(8,128)(2,1)S(1)}, u32[]{:S(2)}, u32[]{:S(2)}) %collective-permute-start) | collective-permute-done | bytes 524320 | tf_op jit(solution)/shard_map/ppermute | solution.py:396
  17.0 4.4 %collective-permute-done.1.after = bf16[4,512,128]{2,1,0:T(8,128)(2,1)S(1)} collective-permute-done((bf16[4,512,128]{2,1,0:T(8,128)(2,1)S(1)}, bf16[4,512,128]{2,1,0:T(8,128)(2,1)S(1)}, u32[]{:S(2)}, u32[]{:S(2)}) %collective-permute-start.1) | collective-permute-done | bytes 524320 | tf_op jit(solution)/shard_map/ppermute | solution.py:397
  21.4 13.3 %first_stage.1 = (bf16[8,512,128]{2,1,0:T(8,128)(2,1)S(1)}, bf16[4,512,128]{2,1,0:T(8,128)(2,1)S(1)}, bf16[4,512,128]{2,1,0:T(8,128)(2,1)S(1)}, bf16[2048,128]{1,0:T(8,128)(2,1)S(1)}) custom-call(s32[216]{0:T(256)S(1)} %get-tuple-element.19.lookup, s32[2,8]{1,0:T(2,128)S(1)} %get-tuple-element.21.chosen, s32[8,512]{1,0:T(8,128)S(1)} %copy-done.4, ...), custom_call_target="tpu_custom_call" | custom-call | flops 8000000000 | bytes 6000000 | tf_op jit(solution)/shard_map/first_stage/pallas_call | solution.py:282
  34.7 0.0 copy-start.6
  34.7 1.0 %copy-done.6 = bf16[8,512,128]{2,1,0:T(8,128)(2,1)} copy-done((bf16[8,512,128]{2,1,0:T(8,128)(2,1)}, bf16[8,512,128]{2,1,0:T(8,128)(2,1)S(1)}, u32[]{:S(2)}) %copy-start.6) | copy-done | bytes 1048600
  35.7 1.9 %collective-permute-start.2 = (bf16[4,512,128]{2,1,0:T(8,128)(2,1)S(1)}, bf16[4,512,128]{2,1,0:T(8,128)(2,1)S(1)}, u32[]{:S(2)}, u32[]{:S(2)}) collective-permute-start(bf16[4,512,128]{2,1,0:T(8,128)(2,1)S(1)} %get-tuple-element.27), channel_id=1, source_target_pairs={{0,1},{1,2},{2,3},{3,4},{4,5},{5,6},{6,7},{7,8},{8,9},{9,10},{10,1... | collective-permute-start | bytes 1572872 | tf_op jit(solution)/shard_map/ppermute | solution.py:396
  37.6 2.4 %collective-permute-start.3 = (bf16[4,512,128]{2,1,0:T(8,128)(2,1)S(1)}, bf16[4,512,128]{2,1,0:T(8,128)(2,1)S(1)}, u32[]{:S(2)}, u32[]{:S(2)}) collective-permute-start(bf16[4,512,128]{2,1,0:T(8,128)(2,1)S(1)} %get-tuple-element.28), channel_id=1, source_target_pairs={{1,0},{2,1},{3,2},{4,3},{5,4},{6,5},{7,6},{8,7},{9,8},{10,9},{11,1... | collective-permute-start | bytes 1572872 | tf_op jit(solution)/shard_map/ppermute | solution.py:397
  40.0 25.6 %all_to_all.17.blocks = bf16[128,16,128]{2,1,0:T(8,128)(2,1)} all-to-all(bf16[128,16,128]{2,1,0:T(8,128)(2,1)S(1)} %bitcast.3), channel_id=1, replica_groups=mesh['wide'=16,'narrow'=8] {'wide','narrow'}, dimensions={0} | all-to-all | bytes 1048576 | tf_op jit(solution)/shard_map/all_to_all | solution.py:410
  65.6 2.0 %combine.1 = bf16[128,16,128]{2,1,0:T(8,128)(2,1)} custom-call(bf16[128,16,128]{2,1,0:T(8,128)(2,1)} %all_to_all.17.blocks), custom_call_target="tpu_custom_call" | custom-call | tf_op jit(solution)/shard_map/combine/pallas_call | solution.py:351
  67.6 5.8 %all-to-all-start.1 = ((bf16[128,16,128]{2,1,0:T(8,128)(2,1)}), bf16[128,16,128]{2,1,0:T(8,128)(2,1)S(1)}, u32[]{:S(2)}, u32[]{:S(2)}) async-start(bf16[128,16,128]{2,1,0:T(8,128)(2,1)} %combine.1), calls=%async_computation.1 | async-start | bytes 1048576 | tf_op jit(solution)/shard_map/all_to_all | solution.py:413
  73.5 0.0 collective-permute-done.2.before
  73.5 0.0 collective-permute-done.3.after
  73.5 0.0 copy-start.7
  73.5 1.2 %copy-done.7 = bf16[8,512,128]{2,1,0:T(8,128)(2,1)S(1)} copy-done((bf16[8,512,128]{2,1,0:T(8,128)(2,1)S(1)}, bf16[8,512,128]{2,1,0:T(8,128)(2,1)}, u32[]{:S(2)}) %copy-start.7) | copy-done | bytes 1048600
  74.7 9.3 %second_stage.1 = (bf16[8,64,512]{2,1,0:T(8,128)(2,1)}, bf16[8,64,512]{2,1,0:T(8,128)(2,1)}) custom-call(s32[216]{0:T(256)S(1)} %get-tuple-element.19.lookup, s32[8,512]{1,0:T(8,128)S(1)} %copy-done.4, bf16[2,3,256,256]{3,2,1,0:T(8,128)(2,1)S(1)} %get-tuple-element.20.weights, bf16[8,512,128]{2,1,0:T(8,128)(2,1)S(1)} %copy-done.7, ...), custom_call_target="tpu_custom_call" | custom-call | flops 8000000000 | bytes 6000000 | tf_op jit(solution)/shard_map/second_stage/pallas_call | solution.py:321
  84.0 3.1 %all-to-all-done.1 = bf16[128,16,128]{2,1,0:T(8,128)(2,1)S(1)} async-done(((bf16[128,16,128]{2,1,0:T(8,128)(2,1)}), bf16[128,16,128]{2,1,0:T(8,128)(2,1)S(1)}, u32[]{:S(2)}, u32[]{:S(2)}) %all-to-all-start.1) | async-done | bytes 524320 | tf_op jit(solution)/shard_map/all_to_all | solution.py:413
  87.2 0.0 copy-start.8
  87.2 0.8 copy-done.8
  88.0 2.7 %unpack.1 = (f32[27,64,64]{2,1,0:T(8,128)}, f32[27,64,64]{2,1,0:T(8,128)}) custom-call(bf16[2048,128]{1,0:T(8,128)(2,1)} %bitcast.4), custom_call_target="tpu_custom_call" | custom-call | tf_op jit(solution)/shard_map/unpack/pallas_call | solution.py:383
Async XLA Ops:
  0.6 0.7 copy-start.4
  1.4 1.0 %copy-start = (bf16[8,64,512]{2,1,0:T(8,128)(2,1)S(1)}, bf16[8,64,512]{2,1,0:T(8,128)(2,1)}, u32[]{:S(2)}) copy-start(bf16[8,64,512]{2,1,0:T(8,128)(2,1)} %features.1) | copy-start | bytes 1572868
  2.4 1.0 %copy-start.1 = (bf16[8,64,512]{2,1,0:T(8,128)(2,1)S(1)}, bf16[8,64,512]{2,1,0:T(8,128)(2,1)}, u32[]{:S(2)}) copy-start(bf16[8,64,512]{2,1,0:T(8,128)(2,1)} %cotangent.1) | copy-start | bytes 1572868
  3.4 0.7 copy-start.5
  4.1 8.7 %copy-start.2 = (bf16[27,64,64]{2,1,0:T(8,128)(2,1)S(1)}, bf16[27,64,64]{2,1,0:T(8,128)(2,1)}, u32[]{:S(2)}) copy-start(bf16[27,64,64]{2,1,0:T(8,128)(2,1)} %kernel_one.1) | copy-start | bytes 663556
  4.1 8.7 %copy-start.3 = (bf16[27,64,64]{2,1,0:T(8,128)(2,1)S(1)}, bf16[27,64,64]{2,1,0:T(8,128)(2,1)}, u32[]{:S(2)}) copy-start(bf16[27,64,64]{2,1,0:T(8,128)(2,1)} %kernel_two.1) | copy-start | bytes 663556
  5.9 11.0 %collective-permute-start = (bf16[4,512,128]{2,1,0:T(8,128)(2,1)S(1)}, bf16[4,512,128]{2,1,0:T(8,128)(2,1)S(1)}, u32[]{:S(2)}, u32[]{:S(2)}) collective-permute-start(bf16[4,512,128]{2,1,0:T(8,128)(2,1)S(1)} %get-tuple-element.24), channel_id=1, source_target_pairs={{0,1},{1,2},{2,3},{3,4},{4,5},{5,6},{6,7},{7,8},{8,9},{9,10},{10,1... | collective-permute-start | bytes 1572872 | tf_op jit(solution)/shard_map/ppermute | solution.py:396
  10.9 10.5 %collective-permute-start.1 = (bf16[4,512,128]{2,1,0:T(8,128)(2,1)S(1)}, bf16[4,512,128]{2,1,0:T(8,128)(2,1)S(1)}, u32[]{:S(2)}, u32[]{:S(2)}) collective-permute-start(bf16[4,512,128]{2,1,0:T(8,128)(2,1)S(1)} %get-tuple-element.25), channel_id=1, source_target_pairs={{1,0},{2,1},{3,2},{4,3},{5,4},{6,5},{7,6},{8,7},{9,8},{10,9},{11,1... | collective-permute-start | bytes 1572872 | tf_op jit(solution)/shard_map/ppermute | solution.py:397
  34.7 1.0 %copy-start.6 = (bf16[8,512,128]{2,1,0:T(8,128)(2,1)}, bf16[8,512,128]{2,1,0:T(8,128)(2,1)S(1)}, u32[]{:S(2)}) copy-start(bf16[8,512,128]{2,1,0:T(8,128)(2,1)S(1)} %get-tuple-element.26.own) | copy-start | bytes 3145732
  35.7 37.8 %collective-permute-start.2 = (bf16[4,512,128]{2,1,0:T(8,128)(2,1)S(1)}, bf16[4,512,128]{2,1,0:T(8,128)(2,1)S(1)}, u32[]{:S(2)}, u32[]{:S(2)}) collective-permute-start(bf16[4,512,128]{2,1,0:T(8,128)(2,1)S(1)} %get-tuple-element.27), channel_id=1, source_target_pairs={{0,1},{1,2},{2,3},{3,4},{4,5},{5,6},{6,7},{7,8},{8,9},{9,10},{10,1... | collective-permute-start | bytes 1572872 | tf_op jit(solution)/shard_map/ppermute | solution.py:396
  37.6 35.9 %collective-permute-start.3 = (bf16[4,512,128]{2,1,0:T(8,128)(2,1)S(1)}, bf16[4,512,128]{2,1,0:T(8,128)(2,1)S(1)}, u32[]{:S(2)}, u32[]{:S(2)}) collective-permute-start(bf16[4,512,128]{2,1,0:T(8,128)(2,1)S(1)} %get-tuple-element.28), channel_id=1, source_target_pairs={{1,0},{2,1},{3,2},{4,3},{5,4},{6,5},{7,6},{8,7},{9,8},{10,9},{11,1... | collective-permute-start | bytes 1572872 | tf_op jit(solution)/shard_map/ppermute | solution.py:397
  67.6 19.5 %all-to-all-start.1 = ((bf16[128,16,128]{2,1,0:T(8,128)(2,1)}), bf16[128,16,128]{2,1,0:T(8,128)(2,1)S(1)}, u32[]{:S(2)}, u32[]{:S(2)}) async-start(bf16[128,16,128]{2,1,0:T(8,128)(2,1)} %combine.1), calls=%async_computation.1 | async-start | bytes 1048576 | tf_op jit(solution)/shard_map/all_to_all | solution.py:413
  73.5 1.2 %copy-start.7 = (bf16[8,512,128]{2,1,0:T(8,128)(2,1)S(1)}, bf16[8,512,128]{2,1,0:T(8,128)(2,1)}, u32[]{:S(2)}) copy-start(bf16[8,512,128]{2,1,0:T(8,128)(2,1)} %copy-done.6) | copy-start | bytes 3145732
  87.2 0.8 copy-start.8

commit v2 on v1

--- a/solution.py
+++ b/solution.py
@@ -18,7 +18,7 @@
 TILE_ROWS = (EDGE + 2) * SLAB
 ROWS = EDGE * SLAB
 TERMS = 2048
-VMEM = 48 * 1024 * 1024
+VMEM = 24 * 1024 * 1024
 F32 = jnp.float32
 BF16 = jnp.bfloat16
 
@@ -31,11 +31,22 @@
     return lax.broadcasted_iota(jnp.int32, shape, len(shape) - 1) < CH
 
 
-def pack_kernel(position, neighbours, features, cotangent, occupancy, fields, ahead, behind, chosen):
+def pack_kernel(
+    position, neighbours, features_far, cotangent_far, occupancy_far,
+    fields, ahead, behind, chosen, features, cotangent, occupancy, sems,
+):
+    mask_copy = pltpu.make_async_copy(occupancy_far, occupancy, sems.at[0, 0])
+    mask_copy.start()
+    copies = []
     for b in range(SLOTS):
-        active = occupancy[b : b + 1, :].astype(F32)
-        both = jnp.concatenate([features[b], cotangent[b]], axis=0).astype(F32) * active
-        fields[b] = both.T.astype(BF16)
+        copies.append(
+            (
+                pltpu.make_async_copy(features_far.at[b], features.at[b], sems.at[1, b]),
+                pltpu.make_async_copy(cotangent_far.at[b], cotangent.at[b], sems.at[2, b]),
+            )
+        )
+        for copy in copies[-1]:
+            copy.start()
     here = position[0] * SLOTS
     for r in range(SLOTS):
         chosen[0, r] = 0
@@ -53,6 +64,13 @@
         chosen[1, jnp.minimum(count_behind, NEAR)] = b
         count_ahead += (highest >= here + SLOTS).astype(jnp.int32)
         count_behind += (lowest < here).astype(jnp.int32)
+    mask_copy.wait()
+    for b in range(SLOTS):
+        for copy in copies[b]:
+            copy.wait()
+        active = occupancy[b : b + 1, :].astype(F32)
+        both = jnp.concatenate([features[b], cotangent[b]], axis=0).astype(F32) * active
+        fields[b] = both.T.astype(BF16)
     for r in range(NEAR):
         ahead[r] = fields[chosen[0, r]]
         behind[r] = fields[chosen[1, r]]
@@ -67,9 +85,15 @@
             jax.ShapeDtypeStruct((NEAR, VOX, LANES), BF16),
             jax.ShapeDtypeStruct((2, SLOTS), jnp.int32),
         ),
-        in_specs=[whole_smem, whole_smem, whole_vmem, whole_vmem, whole_vmem],
+        in_specs=[whole_smem, whole_smem, anywhere, anywhere, anywhere],
         out_specs=(whole_vmem, whole_vmem, whole_vmem, whole_smem),
-        compiler_params=pltpu.CompilerParams(vmem_limit_bytes=VMEM),
+        scratch_shapes=[
+            pltpu.VMEM((SLOTS, CH, VOX), BF16),
+            pltpu.VMEM((SLOTS, CH, VOX), BF16),
+            pltpu.VMEM((SLOTS, VOX), jnp.int32),
+            pltpu.SemaphoreType.DMA((3, SLOTS)),
+        ],
+        compiler_params=pltpu.CompilerParams(vmem_limit_bytes=60 * 1024 * 1024),
         name="pack",
     )(position, neighbours, features, cotangent, occupancy)
 
@@ -225,44 +249,63 @@
     return jnp.broadcast_to(active, (LANES, VOX)).T
 
 
+def hidden_and_grad(both, mask):
+    lower = lower_half((VOX, LANES))
+    preact = jnp.where(lower, both, pltpu.roll(both, CH, 1))
+    s = jax.nn.sigmoid(preact)
+    value = jnp.where(lower, preact * s, both * s * (1.0 + preact * (1.0 - s)))
+    return value * mask
+
+
+def turned_over(value):
+    cube = value.reshape(EDGE, EDGE, EDGE, LANES)
+    turned = []
+    for c in range(3):
+        parts = [cube]
+        if c > 0:
+            parts.insert(0, jnp.zeros((EDGE, c, EDGE, LANES), F32))
+        if c < 2:
+            parts.append(jnp.zeros((EDGE, 2 - c, EDGE, LANES), F32))
+        padded = jnp.concatenate(parts, axis=1).reshape(ROWS, LANES)
+        turned.append(padded.astype(BF16).T)
+    hidden = jnp.concatenate([t[:CH] for t in turned], axis=0)
+    grad_pre = jnp.concatenate([t[CH:] for t in turned], axis=0)
+    return hidden, grad_pre
+
+
 def first_kernel(
     lookup, chosen, occupancy, weights, own, before, after,
-    result, ahead, behind, terms, pool, tile, sum_one, sum_two, sems,
+    result, ahead, behind, terms, pool, tiles, sum_one, sum_two, sems,
 ):
     fill_pool(own, before, after, pool, sems)
     sum_one[...] = jnp.zeros_like(sum_one)
     sum_two[...] = jnp.zeros_like(sum_two)
-
-    @pl.loop(0, SLOTS)
-    def _(b):
-        extend(pool, lookup, b, tile)
-        both = convolve(tile, weights)
-        lower = lower_half((VOX, LANES))
-        preact = jnp.where(lower, both, pltpu.roll(both, CH, 1))
-        s = jax.nn.sigmoid(preact)
-        value = jnp.where(lower, preact * s, both * s * (1.0 + preact * (1.0 - s)))
-        value = value * row_mask(occupancy, b)
-        result[b] = value.astype(BF16)
-        cube = value.reshape(EDGE, EDGE, EDGE, LANES)
+    group = 4
+
+    @pl.loop(0, SLOTS // group)
+    def _(t):
         turned = []
-        for c in range(3):
-            parts = [cube]
-            if c > 0:
-                parts.insert(0, jnp.zeros((EDGE, c, EDGE, LANES), F32))
-            if c < 2:
-                parts.append(jnp.zeros((EDGE, 2 - c, EDGE, LANES), F32))
-            padded = jnp.concatenate(parts, axis=1).reshape(ROWS, LANES)
-            turned.append(padded.astype(BF16).T)
-        hidden = jnp.concatenate([t[:CH] for t in turned], axis=0)
-        grad_pre = jnp.concatenate([t[CH:] for t in turned], axis=0)
+        for p in range(group):
+            extend(pool, lookup, group * t + p, tiles.at[p])
+        for p in range(group):
+            b = group * t + p
+            value = hidden_and_grad(convolve(tiles.at[p], weights), row_mask(occupancy, b))
+            result[b] = value.astype(BF16)
+            turned.append(turned_over(value))
+        hidden = jnp.concatenate([h for h, _ in turned], axis=1)
+        grad_pre = jnp.concatenate([g for _, g in turned], axis=1)
         for a in range(3):
-            rows = pl.ds(a * SLAB, ROWS)
-            sum_one[a] += jnp.dot(
-                grad_pre, tile[rows, 0 : 2 * LANES], preferred_element_type=F32
-            )
-            sum_two[a] += jnp.dot(
-                hidden, tile[rows, LANES : 3 * LANES], preferred_element_type=F32
-            )
+            def rows(first):
+                return jnp.concatenate(
+                    [
+                        tiles[p, a * SLAB : a * SLAB + ROWS, first : first + 2 * LANES]
+                        for p in range(group)
+                    ],
+                    axis=0,
+                )
+
+            sum_one[a] += jnp.dot(grad_pre, rows(0), preferred_element_type=F32)
+            sum_two[a] += jnp.dot(hidden, rows(LANES), preferred_element_type=F32)
 
     for r in range(NEAR):
         ahead[r] = result[chosen[0, r]]
@@ -291,7 +334,7 @@
         out_specs=(whole_vmem,) * 4,
         scratch_shapes=[
             pltpu.VMEM((POOL, VOX, LANES), BF16),
-            pltpu.VMEM((TILE_ROWS, 3 * LANES), BF16),
+            pltpu.VMEM((4, TILE_ROWS, 3 * LANES), BF16),
             pltpu.VMEM((3, 3 * CH, 2 * LANES), F32),
             pltpu.VMEM((3, 3 * CH, 2 * LANES), F32),
             pltpu.SemaphoreType.DMA((3,)),
@@ -305,16 +348,20 @@
 
 
 def second_kernel(
-    lookup, occupancy, weights, own, before, after, output, grad_in, pool, tile, sems
+    lookup, occupancy, weights, own, before, after, output, grad_in, pool, tiles, sems
 ):
     fill_pool(own, before, after, pool, sems)
-
-    @pl.loop(0, SLOTS)
-    def _(b):
-        extend(pool, lookup, b, tile)
-        both = convolve(tile, weights).T * occupancy[pl.ds(b, 1), :].astype(F32)
-        output[b] = both[:CH].astype(BF16)
-        grad_in[b] = both[CH:].astype(BF16)
+    group = 4
+
+    @pl.loop(0, SLOTS // group)
+    def _(t):
+        for p in range(group):
+            extend(pool, lookup, group * t + p, tiles.at[p])
+        for p in range(group):
+            b = group * t + p
+            both = convolve(tiles.at[p], weights).T * occupancy[pl.ds(b, 1), :].astype(F32)
+            output[b] = both[:CH].astype(BF16)
+            grad_in[b] = both[CH:].astype(BF16)
 
 
 def second_stage(lookup, occupancy, weights, own, before, after):
@@ -328,7 +375,7 @@
         out_specs=(whole_vmem,) * 2,
         scratch_shapes=[
             pltpu.VMEM((POOL, VOX, LANES), BF16),
-            pltpu.VMEM((TILE_ROWS, 3 * LANES), BF16),
+            pltpu.VMEM((4, TILE_ROWS, 3 * LANES), BF16),
             pltpu.SemaphoreType.DMA((3,)),
         ],
         compiler_params=pltpu.CompilerParams(vmem_limit_bytes=VMEM),
@@ -353,6 +400,7 @@
         out_shape=jax.ShapeDtypeStruct(blocks.shape, BF16),
         in_specs=[whole_vmem],
         out_specs=whole_vmem,
+        compiler_params=pltpu.CompilerParams(vmem_limit_bytes=VMEM),
         name="combine",
     )(blocks)
 
@@ -388,6 +436,7 @@
         ),
         in_specs=[whole_vmem],
         out_specs=(whole_vmem,) * 2,
+        compiler_params=pltpu.CompilerParams(vmem_limit_bytes=VMEM),
         name="unpack",
     )(sums)
 
@@ -406,8 +455,9 @@
     result, ahead, behind, terms = first_stage(
         lookup, chosen, occupancy, first, fields, before, after
     )
+    terms = lax.all_to_all(terms, AXES, 0, 0, tiled=True)
     before, after = exchange(ahead, behind, devices)
-    terms = lax.all_to_all(terms, AXES, 0, 0, tiled=True)
+    terms, before, after = lax.optimization_barrier((terms, before, after))
     output, grad_in = second_stage(lookup, occupancy, second, result, before, after)
     spread = combine(terms.reshape(devices, TERMS // devices, LANES)).reshape(TERMS, LANES)
     sums = lax.all_to_all(spread, AXES, 0, 0, tiled=True)

time: 91.2 us -> 84.5 us (0.927)
  Pallas kernels: 31.4 us -> 26.2 us
  local copies, waits for them, and re-layouts: 6.47 us -> 1.92 us
  waiting for transfers between devices: 9.34 us -> 12.6 us
    unnamed x18 -> x12, local copies, waits for them, and re-layouts: 6.47 us -> 1.92 us
    pallas_call x1, Pallas kernels: 13.3 us -> 9.64 us  [first_stage(): pl.pallas_call(first_kernel, out_shape=(jax.ShapeDtypeStruct((SLOTS, VOX,...]
    all_to_all x1, waiting for transfers between devices: 3.13 us -> 6.23 us  [local(): sums = lax.all_to_all(spread, AXES, 0, 0, tiled=True)]
    pallas_call x1, Pallas kernels: 1.77 us -> 4.15 us  [pack(): pl.pallas_call(pack_kernel, out_shape=(jax.ShapeDtypeStruct((SLOTS, VOX,...]
    pallas_call x1, Pallas kernels: 9.3 us -> 7.44 us  [second_stage(): pl.pallas_call(second_kernel, out_shape=(jax.ShapeDtypeStruct((SLOTS, CH,...]
    pallas_call x1, Pallas kernels: 2.71 us -> 1.67 us  [unpack(): pl.pallas_call(kernel, out_shape=(jax.ShapeDtypeStruct((27, CH, CH), F32)...]
    pallas_call x1, Pallas kernels: 2 us -> 0.96 us  [combine(): pl.pallas_call(combine_kernel, out_shape=jax.ShapeDtypeStruct(blocks.shap...]
  transfers between devices with their start and end apart: 5 -> 5, of which waited for: 3 -> 3; matrix products, arithmetic and copies ran while one was open for 0% -> 0% of each run, Pallas kernels for 15% -> 12%
where the time goes in v2:
time: 84.5 us; the launch traced here: 84.1 us
  Pallas kernels  26.2 us (31%)
  blocking collectives  25.5 us (30%)
  starting transfers between devices  17 us (20%)
  waiting for transfers between devices  12.6 us (15%)
  local copies, waits for them, and re-layouts  1.92 us (2%)
    all_to_all x1, blocking collectives, local(): terms = lax.all_to_all(terms, AXES, 0, 0, tiled=True)  25.5 us
    pallas_call x1, Pallas kernels, first_stage(): pl.pallas_call(first_kernel, out_shape=(jax.ShapeDtypeStruct((SLOTS, VOX,...  9.64 us
    pallas_call x1, Pallas kernels, second_stage(): pl.pallas_call(second_kernel, out_shape=(jax.ShapeDtypeStruct((SLOTS, CH,...  7.44 us
    ppermute x2, starting transfers between devices, exchange(): before = lax.ppermute(ahead, AXES, [(k, k + 1) for k in range(devices - 1)])  6.86 us
    all_to_all x1, waiting for transfers between devices, local(): sums = lax.all_to_all(spread, AXES, 0, 0, tiled=True)  6.23 us
    all_to_all x1, starting transfers between devices, local(): sums = lax.all_to_all(spread, AXES, 0, 0, tiled=True)  5.84 us
    ppermute x2, starting transfers between devices, exchange(): after = lax.ppermute(behind, AXES, [(k + 1, k) for k in range(devices - 1)])  4.35 us
    ppermute x2, waiting for transfers between devices, exchange(): after = lax.ppermute(behind, AXES, [(k + 1, k) for k in range(devices - 1)])  4.3 us
  transfers between devices with their start and end apart: 5, of which 3 were waited for; matrix products, arithmetic and copies ran while one was open for 0% of the time, Pallas kernels for 12%

profile of v2, /device:TPU:1, one launch (start us, length us, event | category | flops | bytes accessed | tf_op | source)
XLA Modules:
  0.0 84.1 jit_solution(708994457665531807)
XLA Ops:
  0.6 0.0 copy-start
  0.6 0.0 copy-start.1
  0.7 0.0 copy-start.3
  0.7 4.1 %pack.1 = (bf16[8,512,128]{2,1,0:T(8,128)(2,1)}, bf16[4,512,128]{2,1,0:T(8,128)(2,1)}, bf16[4,512,128]{2,1,0:T(8,128)(2,1)}, s32[2,8]{1,0:T(2,128)}) custom-call(s32[1]{0:T(128)} %bitcast.position, s32[8,26]{1,0:T(8,128)} %neighbours.3, bf16[8,64,512]{2,1,0:T(8,128)(2,1)} %features_far.1, bf16[8,64,512]{2,1,0:T(8,128)(2,1)} %cotangent_far.1, s32[8,512]{1,0:T(8,128)} %occupancy.3), custom_call_target="tpu_custom_call" | custom-call | tf_op jit(solution)/shard_map/pack/pallas_call | solution.py:80
  4.8 4.9 %collective-permute-start = (bf16[4,512,128]{2,1,0:T(8,128)(2,1)}, bf16[4,512,128]{2,1,0:T(8,128)(2,1)S(1)}, u32[]{:S(2)}, u32[]{:S(2)}) collective-permute-start(bf16[4,512,128]{2,1,0:T(8,128)(2,1)} %get-tuple-element.27), channel_id=1, source_target_pairs={{0,1},{1,2},{2,3},{3,4},{4,5},{5,6},{6,7},{7,8},{8,9},{9,10},{10,1... | collective-permute-start | bytes 1572872 | tf_op jit(solution)/shard_map/ppermute | solution.py:445
  9.8 0.0 copy-start.2
  9.8 1.9 %collective-permute-start.1 = (bf16[4,512,128]{2,1,0:T(8,128)(2,1)}, bf16[4,512,128]{2,1,0:T(8,128)(2,1)S(1)}, u32[]{:S(2)}, u32[]{:S(2)}) collective-permute-start(bf16[4,512,128]{2,1,0:T(8,128)(2,1)} %get-tuple-element.28), channel_id=1, source_target_pairs={{1,0},{2,1},{3,2},{4,3},{5,4},{6,5},{7,6},{8,7},{9,8},{10,9},{11,1... | collective-permute-start | bytes 1572872 | tf_op jit(solution)/shard_map/ppermute | solution.py:446
  11.7 0.0 copy-done
  11.7 0.0 copy-done.1
  11.7 0.0 copy-done.3
  11.7 2.3 %prepare.1 = (bf16[2,3,256,256]{3,2,1,0:T(8,128)(2,1)S(1)}, bf16[2,3,256,256]{3,2,1,0:T(8,128)(2,1)S(1)}, s32[216]{0:T(256)S(1)}) custom-call(s32[1]{0:T(128)} %bitcast.position, s32[8,26]{1,0:T(8,128)S(1)} %copy-done.3, bf16[27,64,64]{2,1,0:T(8,128)(2,1)S(1)} %copy-done, bf16[27,64,64]{2,1,0:T(8,128)(2,1)S(1)} %copy-done.1), custom_call_target="tpu_custom_call" | custom-call | flops 4000000 | bytes 2000000 | tf_op jit(solution)/shard_map/prepare/pallas_call | solution.py:160
  14.1 2.1 %collective-permute-done.before = bf16[4,512,128]{2,1,0:T(8,128)(2,1)S(1)} collective-permute-done((bf16[4,512,128]{2,1,0:T(8,128)(2,1)}, bf16[4,512,128]{2,1,0:T(8,128)(2,1)S(1)}, u32[]{:S(2)}, u32[]{:S(2)}) %collective-permute-start) | collective-permute-done | bytes 524320 | tf_op jit(solution)/shard_map/ppermute | solution.py:445
  16.2 4.3 %collective-permute-done.1.after = bf16[4,512,128]{2,1,0:T(8,128)(2,1)S(1)} collective-permute-done((bf16[4,512,128]{2,1,0:T(8,128)(2,1)}, bf16[4,512,128]{2,1,0:T(8,128)(2,1)S(1)}, u32[]{:S(2)}, u32[]{:S(2)}) %collective-permute-start.1) | collective-permute-done | bytes 524320 | tf_op jit(solution)/shard_map/ppermute | solution.py:446
  20.5 0.0 copy-start.5
  20.5 0.0 copy-done.2
  20.5 0.7 copy-done.5
  21.2 0.0 copy-start.4
  21.2 1.2 %copy-done.4 = bf16[8,512,128]{2,1,0:T(8,128)(2,1)S(1)} copy-done((bf16[8,512,128]{2,1,0:T(8,128)(2,1)S(1)}, bf16[8,512,128]{2,1,0:T(8,128)(2,1)}, u32[]{:S(2)}) %copy-start.4) | copy-done | bytes 1048600
  22.4 9.6 %first_stage.1 = (bf16[8,512,128]{2,1,0:T(8,128)(2,1)S(1)}, bf16[4,512,128]{2,1,0:T(8,128)(2,1)S(1)}, bf16[4,512,128]{2,1,0:T(8,128)(2,1)S(1)}, bf16[2048,128]{1,0:T(8,128)(2,1)S(1)}) custom-call(s32[216]{0:T(256)S(1)} %get-tuple-element.22.lookup, s32[2,8]{1,0:T(2,128)S(1)} %copy-done.5, s32[8,512]{1,0:T(8,128)S(1)} %copy-done.2, ...), custom_call_target="tpu_custom_call" | custom-call | flops 8000000000 | bytes 6000000 | tf_op jit(solution)/shard_map/first_stage/pallas_call | solution.py:325
  32.0 1.9 %collective-permute-start.2 = (bf16[4,512,128]{2,1,0:T(8,128)(2,1)S(1)}, bf16[4,512,128]{2,1,0:T(8,128)(2,1)S(1)}, u32[]{:S(2)}, u32[]{:S(2)}) collective-permute-start(bf16[4,512,128]{2,1,0:T(8,128)(2,1)S(1)} %get-tuple-element.31), channel_id=1, source_target_pairs={{0,1},{1,2},{2,3},{3,4},{4,5},{5,6},{6,7},{7,8},{8,9},{9,10},{10,1... | collective-permute-start | bytes 1572872 | tf_op jit(solution)/shard_map/ppermute | solution.py:445
  34.0 2.4 %collective-permute-start.3 = (bf16[4,512,128]{2,1,0:T(8,128)(2,1)S(1)}, bf16[4,512,128]{2,1,0:T(8,128)(2,1)S(1)}, u32[]{:S(2)}, u32[]{:S(2)}) collective-permute-start(bf16[4,512,128]{2,1,0:T(8,128)(2,1)S(1)} %get-tuple-element.32), channel_id=1, source_target_pairs={{1,0},{2,1},{3,2},{4,3},{5,4},{6,5},{7,6},{8,7},{9,8},{10,9},{11,1... | collective-permute-start | bytes 1572872 | tf_op jit(solution)/shard_map/ppermute | solution.py:446
  36.4 25.5 %all_to_all.20 = bf16[128,16,128]{2,1,0:T(8,128)(2,1)S(1)} all-to-all(bf16[128,16,128]{2,1,0:T(8,128)(2,1)S(1)} %bitcast.6), channel_id=1, replica_groups=mesh['wide'=16,'narrow'=8] {'wide','narrow'}, dimensions={0} | all-to-all | bytes 1048576 | tf_op jit(solution)/shard_map/all_to_all | solution.py:458
  61.9 0.0 collective-permute-done.2.before
  61.9 0.0 collective-permute-done.3.after
  61.9 1.0 %combine.1 = bf16[128,16,128]{2,1,0:T(8,128)(2,1)} custom-call(bf16[128,16,128]{2,1,0:T(8,128)(2,1)S(1)} %all_to_all.20), custom_call_target="tpu_custom_call" | custom-call | tf_op jit(solution)/shard_map/combine/pallas_call | solution.py:398
  62.9 5.8 %all-to-all-start.1 = ((bf16[128,16,128]{2,1,0:T(8,128)(2,1)}), bf16[128,16,128]{2,1,0:T(8,128)(2,1)S(1)}, u32[]{:S(2)}, u32[]{:S(2)}) async-start(bf16[128,16,128]{2,1,0:T(8,128)(2,1)} %combine.1), calls=%async_computation.1 | async-start | bytes 1048576 | tf_op jit(solution)/shard_map/all_to_all | solution.py:463
  68.7 7.4 %second_stage.1 = (bf16[8,64,512]{2,1,0:T(8,128)(2,1)}, bf16[8,64,512]{2,1,0:T(8,128)(2,1)}) custom-call(s32[216]{0:T(256)S(1)} %get-tuple-element.22.lookup, s32[8,512]{1,0:T(8,128)S(1)} %copy-done.2, bf16[2,3,256,256]{3,2,1,0:T(8,128)(2,1)S(1)} %get-tuple-element.23.weights, bf16[8,512,128]{2,1,0:T(8,128)(2,1)S(1)} %get-tuple-element.29.own, ...), custom_call_target="tpu_custom_call" | custom-call | flops 8000000000 | bytes 6000000 | tf_op jit(solution)/shard_map/second_stage/pallas_call | solution.py:368
  76.2 6.2 %all-to-all-done.1 = bf16[128,16,128]{2,1,0:T(8,128)(2,1)S(1)} async-done(((bf16[128,16,128]{2,1,0:T(8,128)(2,1)}), bf16[128,16,128]{2,1,0:T(8,128)(2,1)S(1)}, u32[]{:S(2)}, u32[]{:S(2)}) %all-to-all-start.1) | async-done | bytes 524320 | tf_op jit(solution)/shard_map/all_to_all | solution.py:463
  82.4 1.7 %unpack.1 = (f32[27,64,64]{2,1,0:T(8,128)}, f32[27,64,64]{2,1,0:T(8,128)}) custom-call(bf16[2048,128]{1,0:T(8,128)(2,1)S(1)} %bitcast.5), custom_call_target="tpu_custom_call" | custom-call | tf_op jit(solution)/shard_map/unpack/pallas_call | solution.py:431
Async XLA Ops:
  0.6 11.1 %copy-start = (bf16[27,64,64]{2,1,0:T(8,128)(2,1)S(1)}, bf16[27,64,64]{2,1,0:T(8,128)(2,1)}, u32[]{:S(2)}) copy-start(bf16[27,64,64]{2,1,0:T(8,128)(2,1)} %kernel_one.1) | copy-start | bytes 663556
  0.6 11.1 %copy-start.1 = (bf16[27,64,64]{2,1,0:T(8,128)(2,1)S(1)}, bf16[27,64,64]{2,1,0:T(8,128)(2,1)}, u32[]{:S(2)}) copy-start(bf16[27,64,64]{2,1,0:T(8,128)(2,1)} %kernel_two.1) | copy-start | bytes 663556
  0.7 11.1 %copy-start.3 = (s32[8,26]{1,0:T(8,128)S(1)}, s32[8,26]{1,0:T(8,128)}, u32[]{:S(2)}) copy-start(s32[8,26]{1,0:T(8,128)} %neighbours.3) | copy-start | bytes 2500
  4.8 11.4 %collective-permute-start = (bf16[4,512,128]{2,1,0:T(8,128)(2,1)}, bf16[4,512,128]{2,1,0:T(8,128)(2,1)S(1)}, u32[]{:S(2)}, u32[]{:S(2)}) collective-permute-start(bf16[4,512,128]{2,1,0:T(8,128)(2,1)} %get-tuple-element.27), channel_id=1, source_target_pairs={{0,1},{1,2},{2,3},{3,4},{4,5},{5,6},{6,7},{7,8},{8,9},{9,10},{10,1... | collective-permute-start | bytes 1572872 | tf_op jit(solution)/shard_map/ppermute | solution.py:445
  9.8 10.7 %copy-start.2 = (s32[8,512]{1,0:T(8,128)S(1)}, s32[8,512]{1,0:T(8,128)}, u32[]{:S(2)}) copy-start(s32[8,512]{1,0:T(8,128)} %occupancy.3) | copy-start | bytes 49156
  9.8 10.7 %collective-permute-start.1 = (bf16[4,512,128]{2,1,0:T(8,128)(2,1)}, bf16[4,512,128]{2,1,0:T(8,128)(2,1)S(1)}, u32[]{:S(2)}, u32[]{:S(2)}) collective-permute-start(bf16[4,512,128]{2,1,0:T(8,128)(2,1)} %get-tuple-element.28), channel_id=1, source_target_pairs={{1,0},{2,1},{3,2},{4,3},{5,4},{6,5},{7,6},{8,7},{9,8},{10,9},{11,1... | collective-permute-start | bytes 1572872 | tf_op jit(solution)/shard_map/ppermute | solution.py:446
  20.5 0.7 copy-start.5
  21.2 1.2 %copy-start.4 = (bf16[8,512,128]{2,1,0:T(8,128)(2,1)S(1)}, bf16[8,512,128]{2,1,0:T(8,128)(2,1)}, u32[]{:S(2)}) copy-start(bf16[8,512,128]{2,1,0:T(8,128)(2,1)} %get-tuple-element.26.own) | copy-start | bytes 3145732
  32.0 29.9 %collective-permute-start.2 = (bf16[4,512,128]{2,1,0:T(8,128)(2,1)S(1)}, bf16[4,512,128]{2,1,0:T(8,128)(2,1)S(1)}, u32[]{:S(2)}, u32[]{:S(2)}) collective-permute-start(bf16[4,512,128]{2,1,0:T(8,128)(2,1)S(1)} %get-tuple-element.31), channel_id=1, source_target_pairs={{0,1},{1,2},{2,3},{3,4},{4,5},{5,6},{6,7},{7,8},{8,9},{9,10},{10,1... | collective-permute-start | bytes 1572872 | tf_op jit(solution)/shard_map/ppermute | solution.py:445
  34.0 28.0 %collective-permute-start.3 = (bf16[4,512,128]{2,1,0:T(8,128)(2,1)S(1)}, bf16[4,512,128]{2,1,0:T(8,128)(2,1)S(1)}, u32[]{:S(2)}, u32[]{:S(2)}) collective-permute-start(bf16[4,512,128]{2,1,0:T(8,128)(2,1)S(1)} %get-tuple-element.32), channel_id=1, source_target_pairs={{1,0},{2,1},{3,2},{4,3},{5,4},{6,5},{7,6},{8,7},{9,8},{10,9},{11,1... | collective-permute-start | bytes 1572872 | tf_op jit(solution)/shard_map/ppermute | solution.py:446
  62.9 19.5 %all-to-all-start.1 = ((bf16[128,16,128]{2,1,0:T(8,128)(2,1)}), bf16[128,16,128]{2,1,0:T(8,128)(2,1)S(1)}, u32[]{:S(2)}, u32[]{:S(2)}) async-start(bf16[128,16,128]{2,1,0:T(8,128)(2,1)} %combine.1), calls=%async_computation.1 | async-start | bytes 1048576 | tf_op jit(solution)/shard_map/all_to_all | solution.py:463

commit v3 on v2

--- a/solution.py
+++ b/solution.py
@@ -14,10 +14,12 @@
 NEAR = 4
 POOL = SLOTS + 2 * NEAR + 1
 ZERO = POOL - 1
+RIM = 304
 SLAB = (EDGE + 2) * EDGE
 TILE_ROWS = (EDGE + 2) * SLAB
 ROWS = EDGE * SLAB
 TERMS = 2048
+HALF = TERMS // 2
 VMEM = 24 * 1024 * 1024
 F32 = jnp.float32
 BF16 = jnp.bfloat16
@@ -31,23 +33,9 @@
     return lax.broadcasted_iota(jnp.int32, shape, len(shape) - 1) < CH
 
 
-def pack_kernel(
-    position, neighbours, features_far, cotangent_far, occupancy_far,
-    fields, ahead, behind, chosen, features, cotangent, occupancy, sems,
-):
-    mask_copy = pltpu.make_async_copy(occupancy_far, occupancy, sems.at[0, 0])
-    mask_copy.start()
-    copies = []
-    for b in range(SLOTS):
-        copies.append(
-            (
-                pltpu.make_async_copy(features_far.at[b], features.at[b], sems.at[1, b]),
-                pltpu.make_async_copy(cotangent_far.at[b], cotangent.at[b], sems.at[2, b]),
-            )
-        )
-        for copy in copies[-1]:
-            copy.start()
+def choose(position, neighbours, chosen):
     here = position[0] * SLOTS
+    odd = position[0] % 2
     for r in range(SLOTS):
         chosen[0, r] = 0
         chosen[1, r] = 0
@@ -60,38 +48,86 @@
             slot = neighbours[b, d]
             highest = jnp.maximum(highest, slot)
             lowest = jnp.minimum(lowest, jnp.where(slot < 0, 1 << 20, slot))
-        chosen[0, jnp.minimum(count_ahead, NEAR)] = b
-        chosen[1, jnp.minimum(count_behind, NEAR)] = b
+        chosen[odd, jnp.minimum(count_ahead, NEAR)] = b
+        chosen[1 - odd, jnp.minimum(count_behind, NEAR)] = b
         count_ahead += (highest >= here + SLOTS).astype(jnp.int32)
         count_behind += (lowest < here).astype(jnp.int32)
-    mask_copy.wait()
-    for b in range(SLOTS):
-        for copy in copies[b]:
-            copy.wait()
-        active = occupancy[b : b + 1, :].astype(F32)
-        both = jnp.concatenate([features[b], cotangent[b]], axis=0).astype(F32) * active
-        fields[b] = both.T.astype(BF16)
-    for r in range(NEAR):
-        ahead[r] = fields[chosen[0, r]]
-        behind[r] = fields[chosen[1, r]]
+    chosen[0, SLOTS - 1] = odd
+
+
+def side_by_side(features, cotangent, occupancy, b):
+    active = occupancy[pl.ds(b, 1), :].astype(F32)
+    both = jnp.concatenate([features[b], cotangent[b]], axis=0).astype(F32) * active
+    return both.T.astype(BF16)
+
+
+def rim_rank(v):
+    i, j, k = v >> 6, (v >> 3) & 7, v & 7
+    inside = jnp.where(j == 0, k, jnp.where(j == 7, 20 + k, 6 + 2 * j + (k == 7).astype(jnp.int32)))
+    inside = jnp.where((j == 0) | (j == 7) | (k == 0) | (k == 7), inside, RIM)
+    return jnp.where(i == 0, v, jnp.where(i == 7, v - 216, 36 + 28 * i + inside))
+
+
+def surface(v):
+    i, j, k = v >> 6, (v >> 3) & 7, v & 7
+    return (i == 0) | (i == 7) | (j == 0) | (j == 7) | (k == 0) | (k == 7)
+
+
+def pack_kernel(
+    position, neighbours, features_far, cotangent_far, occupancy_far,
+    near_send, far_send, features, cotangent, occupancy, chosen, sems,
+):
+    loads = [pltpu.make_async_copy(occupancy_far, occupancy, sems.at[0])]
+    for h in range(2):
+        part = pl.ds(h * NEAR, NEAR)
+        loads.append(
+            pltpu.make_async_copy(features_far.at[part], features.at[part], sems.at[1 + h])
+        )
+        loads.append(
+            pltpu.make_async_copy(cotangent_far.at[part], cotangent.at[part], sems.at[3 + h])
+        )
+    for copy in loads:
+        copy.start()
+    choose(position, neighbours, chosen)
+    voxel = lax.broadcasted_iota(jnp.int32, (1, VOX), 1)
+    rank = jnp.where(surface(voxel), rim_rank(voxel), -1)
+    wanted = lax.broadcasted_iota(jnp.int32, (RIM, VOX), 0)
+    select = jnp.where(rank == wanted, 1.0, 0.0).astype(BF16)
+    for copy in loads:
+        copy.wait()
+    for side, target in ((1, far_send), (0, near_send)):
+        for r in range(0, NEAR, 2):
+            rows = []
+            for q in range(2):
+                b = chosen[side, r + q]
+                active = occupancy[pl.ds(b, 1), :].astype(F32)
+                rows.append((features[b].astype(F32) * active).astype(BF16))
+                rows.append((cotangent[b].astype(F32) * active).astype(BF16))
+            both = lax.dot_general(
+                select,
+                jnp.concatenate(rows, axis=0),
+                (((1,), (1,)), ((), ())),
+                preferred_element_type=F32,
+            )
+            for q in range(2):
+                target[r + q] = both[:, q * LANES : (q + 1) * LANES].astype(BF16)
 
 
 def pack(position, neighbours, features, cotangent, occupancy):
     return pl.pallas_call(
         pack_kernel,
         out_shape=(
-            jax.ShapeDtypeStruct((SLOTS, VOX, LANES), BF16),
-            jax.ShapeDtypeStruct((NEAR, VOX, LANES), BF16),
-            jax.ShapeDtypeStruct((NEAR, VOX, LANES), BF16),
-            jax.ShapeDtypeStruct((2, SLOTS), jnp.int32),
+            jax.ShapeDtypeStruct((NEAR, RIM, LANES), BF16),
+            jax.ShapeDtypeStruct((NEAR, RIM, LANES), BF16),
         ),
         in_specs=[whole_smem, whole_smem, anywhere, anywhere, anywhere],
-        out_specs=(whole_vmem, whole_vmem, whole_vmem, whole_smem),
+        out_specs=(whole_vmem, whole_vmem),
         scratch_shapes=[
             pltpu.VMEM((SLOTS, CH, VOX), BF16),
             pltpu.VMEM((SLOTS, CH, VOX), BF16),
             pltpu.VMEM((SLOTS, VOX), jnp.int32),
-            pltpu.SemaphoreType.DMA((3, SLOTS)),
+            pltpu.SMEM((2, SLOTS), jnp.int32),
+            pltpu.SemaphoreType.DMA((5,)),
         ],
         compiler_params=pltpu.CompilerParams(vmem_limit_bytes=60 * 1024 * 1024),
         name="pack",
@@ -127,11 +163,24 @@
                 ] = weight_block(kernel, flip, a, rows[r], columns[s])
 
 
-def prepare_kernel(position, neighbours, kernel_one, kernel_two, first, second, lookup, flags, base):
+def prepare_kernel(
+    position, neighbours, kernel_one, kernel_two, features, cotangent, occupancy,
+    first, second, lookup, chosen, fields, spread, flags, base,
+):
     weight_field(kernel_one, False, 0, first)
     weight_field(kernel_two, True, 1, first)
     weight_field(kernel_two, False, 0, second)
     weight_field(kernel_one, True, 1, second)
+    for b in range(SLOTS):
+        fields[b] = side_by_side(features, cotangent, occupancy, b)
+    choose(position, neighbours, chosen)
+    voxel = lax.broadcasted_iota(jnp.int32, (VOX, LANES), 0)
+    rank = jnp.where(surface(voxel), rim_rank(voxel), -1)
+    for first_lane in range(0, RIM, LANES):
+        count = min(LANES, RIM - first_lane)
+        lane = lax.broadcasted_iota(jnp.int32, (VOX, LANES), 1) + first_lane
+        block = jnp.where(rank == lane, 1.0, 0.0).astype(BF16)
+        spread[:, first_lane : first_lane + count] = block[:, :count]
     start = (position[0] - 1) * SLOTS
     for s in range(3 * SLOTS + 1):
         flags[s] = 0
@@ -139,14 +188,15 @@
         for d in range(26):
             slot = neighbours[b, d]
             flags[jnp.where(slot < 0, 3 * SLOTS, slot - start)] = 1
+    odd = position[0] % 2
     count = jnp.int32(0)
     for s in range(SLOTS):
-        base[s] = SLOTS + jnp.minimum(count, NEAR - 1)
+        base[s] = SLOTS + NEAR * (1 - odd) + jnp.minimum(count, NEAR - 1)
         count += flags[s]
         base[SLOTS + s] = s
     count = jnp.int32(0)
     for s in range(SLOTS):
-        base[2 * SLOTS + s] = SLOTS + NEAR + jnp.minimum(count, NEAR - 1)
+        base[2 * SLOTS + s] = SLOTS + NEAR * odd + jnp.minimum(count, NEAR - 1)
         count += flags[2 * SLOTS + s]
     base[3 * SLOTS] = ZERO
     for b in range(SLOTS):
@@ -156,21 +206,24 @@
             lookup[b * 27 + d + (d > 12)] = base[jnp.where(slot < 0, 3 * SLOTS, slot - start)]
 
 
-def prepare(position, neighbours, kernel_one, kernel_two):
+def prepare(position, neighbours, kernel_one, kernel_two, features, cotangent, occupancy):
     return pl.pallas_call(
         prepare_kernel,
         out_shape=(
             jax.ShapeDtypeStruct((2, 3, 2 * LANES, 2 * LANES), BF16),
             jax.ShapeDtypeStruct((2, 3, 2 * LANES, 2 * LANES), BF16),
             jax.ShapeDtypeStruct((27 * SLOTS,), jnp.int32),
-        ),
-        in_specs=[whole_smem, whole_smem, whole_vmem, whole_vmem],
-        out_specs=(whole_vmem, whole_vmem, whole_smem),
+            jax.ShapeDtypeStruct((2, SLOTS), jnp.int32),
+            jax.ShapeDtypeStruct((SLOTS, VOX, LANES), BF16),
+            jax.ShapeDtypeStruct((VOX, RIM), BF16),
+        ),
+        in_specs=[whole_smem, whole_smem] + [whole_vmem] * 5,
+        out_specs=(whole_vmem, whole_vmem, whole_smem, whole_smem) + (whole_vmem,) * 2,
         scratch_shapes=[pltpu.SMEM((32,), jnp.int32), pltpu.SMEM((32,), jnp.int32)],
         compiler_params=pltpu.CompilerParams(vmem_limit_bytes=VMEM),
-        cost_estimate=pl.CostEstimate(flops=4000000, bytes_accessed=2000000, transcendentals=0),
+        cost_estimate=pl.CostEstimate(flops=4000000, bytes_accessed=4000000, transcendentals=0),
         name="prepare",
-    )(position, neighbours, kernel_one, kernel_two)
+    )(position, neighbours, kernel_one, kernel_two, features, cotangent, occupancy)
 
 
 def fill_pool(own, before, after, pool, sems):
@@ -274,10 +327,22 @@
 
 
 def first_kernel(
-    lookup, chosen, occupancy, weights, own, before, after,
-    result, ahead, behind, terms, pool, tiles, sum_one, sum_two, sems,
+    lookup, chosen, occupancy, weights, spread, near, far, own,
+    result, ahead, behind, given, kept, pool, tiles, sum_one, sum_two, terms, sems,
 ):
-    fill_pool(own, before, after, pool, sems)
+    load = pltpu.make_async_copy(own, pool.at[pl.ds(0, SLOTS)], sems.at[0])
+    load.start()
+    pool[ZERO] = jnp.zeros((VOX, LANES), BF16)
+    for place, rim in ((SLOTS, near), (SLOTS + NEAR, far)):
+        for r in range(0, NEAR, 2):
+            whole = jnp.dot(
+                spread[...],
+                jnp.concatenate([rim[r], rim[r + 1]], axis=1),
+                preferred_element_type=F32,
+            )
+            for q in range(2):
+                pool[place + r + q] = whole[:, q * LANES : (q + 1) * LANES].astype(BF16)
+    load.wait()
     sum_one[...] = jnp.zeros_like(sum_one)
     sum_two[...] = jnp.zeros_like(sum_two)
     group = 4
@@ -313,30 +378,35 @@
     part = 3 * CH
     for a in range(3):
         start = a * 3 * part
-        terms[start : start + part] = sum_one[a, :, 0:LANES].astype(BF16)
-        terms[start + part : start + 2 * part] = sum_two[a, :, LANES:].astype(BF16)
+        terms[start : start + part] = sum_one[a, :, 0:LANES]
+        terms[start + part : start + 2 * part] = sum_two[a, :, LANES:]
         terms[start + 2 * part : start + 3 * part] = jnp.where(
             lower_half((part, LANES)), sum_one[a, :, LANES:], sum_two[a, :, 0:LANES]
-        ).astype(BF16)
-    terms[9 * part :] = jnp.zeros((TERMS - 9 * part, LANES), BF16)
-
-
-def first_stage(lookup, chosen, occupancy, weights, own, before, after):
+        )
+    terms[9 * part :] = jnp.zeros((TERMS - 9 * part, LANES), F32)
+    odd = chosen[0, SLOTS - 1]
+    given[...] = terms[pl.ds(pl.multiple_of((1 - odd) * HALF, HALF), HALF), :].astype(BF16)
+    kept[...] = terms[pl.ds(pl.multiple_of(odd * HALF, HALF), HALF), :]
+
+
+def first_stage(lookup, chosen, occupancy, weights, spread, near, far, own):
     return pl.pallas_call(
         first_kernel,
         out_shape=(
             jax.ShapeDtypeStruct((SLOTS, VOX, LANES), BF16),
             jax.ShapeDtypeStruct((NEAR, VOX, LANES), BF16),
             jax.ShapeDtypeStruct((NEAR, VOX, LANES), BF16),
-            jax.ShapeDtypeStruct((TERMS, LANES), BF16),
-        ),
-        in_specs=[whole_smem, whole_smem, whole_vmem, whole_vmem, anywhere, anywhere, anywhere],
-        out_specs=(whole_vmem,) * 4,
+            jax.ShapeDtypeStruct((HALF, LANES), BF16),
+            jax.ShapeDtypeStruct((HALF, LANES), F32),
+        ),
+        in_specs=[whole_smem, whole_smem] + [whole_vmem] * 5 + [anywhere],
+        out_specs=(whole_vmem,) * 5,
         scratch_shapes=[
             pltpu.VMEM((POOL, VOX, LANES), BF16),
             pltpu.VMEM((4, TILE_ROWS, 3 * LANES), BF16),
             pltpu.VMEM((3, 3 * CH, 2 * LANES), F32),
             pltpu.VMEM((3, 3 * CH, 2 * LANES), F32),
+            pltpu.VMEM((TERMS, LANES), F32),
             pltpu.SemaphoreType.DMA((3,)),
         ],
         compiler_params=pltpu.CompilerParams(vmem_limit_bytes=VMEM),
@@ -344,7 +414,7 @@
             flops=8000000000, bytes_accessed=6000000, transcendentals=600000
         ),
         name="first_stage",
-    )(lookup, chosen, occupancy, weights, own, before, after)
+    )(lookup, chosen, occupancy, weights, spread, near, far, own)
 
 
 def second_kernel(
@@ -386,6 +456,21 @@
     )(lookup, occupancy, weights, own, before, after)
 
 
+def pair_kernel(kept, received, total):
+    total[...] = (kept[...] + received[...].astype(F32)).astype(BF16)
+
+
+def pair_sum(kept, received):
+    return pl.pallas_call(
+        pair_kernel,
+        out_shape=jax.ShapeDtypeStruct((HALF, LANES), BF16),
+        in_specs=[whole_vmem] * 2,
+        out_specs=whole_vmem,
+        compiler_params=pltpu.CompilerParams(vmem_limit_bytes=VMEM),
+        name="pair_sum",
+    )(kept, received)
+
+
 def combine_kernel(blocks, spread):
     count, rows = blocks.shape[0], blocks.shape[1]
     total = jnp.zeros((rows, LANES), F32)
@@ -405,7 +490,10 @@
     )(blocks)
 
 
-def unpack_kernel(scale, sums, grad_one, grad_two):
+def unpack_kernel(scale, position, own, other, grad_one, grad_two, sums):
+    odd = position[0] % 2
+    sums[pl.ds(pl.multiple_of(odd * HALF, HALF), HALF), :] = own[...]
+    sums[pl.ds(pl.multiple_of((1 - odd) * HALF, HALF), HALF), :] = other[...]
     part = 3 * CH
     for a in range(3):
         for c in range(3):
@@ -424,7 +512,7 @@
             grad_two[24 - n] = last.T[CH:]
 
 
-def unpack(scale, sums):
+def unpack(scale, position, own, other):
     def kernel(*refs):
         unpack_kernel(scale, *refs)
 
@@ -434,35 +522,53 @@
             jax.ShapeDtypeStruct((27, CH, CH), F32),
             jax.ShapeDtypeStruct((27, CH, CH), F32),
         ),
-        in_specs=[whole_vmem],
+        in_specs=[whole_smem, whole_vmem, whole_vmem],
         out_specs=(whole_vmem,) * 2,
+        scratch_shapes=[pltpu.VMEM((TERMS, LANES), BF16)],
         compiler_params=pltpu.CompilerParams(vmem_limit_bytes=VMEM),
         name="unpack",
-    )(sums)
-
-
-def exchange(ahead, behind, devices):
-    before = lax.ppermute(ahead, AXES, [(k, k + 1) for k in range(devices - 1)])
-    after = lax.ppermute(behind, AXES, [(k + 1, k) for k in range(devices - 1)])
-    return before, after
+    )(position, own, other)
+
+
+def near_swap(rows, devices):
+    return lax.ppermute(rows, AXES, [(k, k ^ 1) for k in range(devices)])
+
+
+def far_swap(rows, devices):
+    route = [(k, k + 1) for k in range(1, devices - 1, 2)]
+    route += [(k + 1, k) for k in range(1, devices - 1, 2)]
+    return lax.ppermute(rows, AXES, route)
 
 
 def local(devices, features, kernel_one, kernel_two, cotangent, neighbours, occupancy):
     position = lax.axis_index(AXES).astype(jnp.int32).reshape(1)
-    fields, ahead, behind, chosen = pack(position, neighbours, features, cotangent, occupancy)
-    before, after = exchange(ahead, behind, devices)
-    first, second, lookup = prepare(position, neighbours, kernel_one, kernel_two)
-    result, ahead, behind, terms = first_stage(
-        lookup, chosen, occupancy, first, fields, before, after
+    near_send, far_send = pack(position, neighbours, features, cotangent, occupancy)
+    near_send, far_send, later = lax.optimization_barrier((near_send, far_send, position))
+    far = far_swap(far_send, devices)
+    near = near_swap(near_send, devices)
+    first, second, lookup, chosen, fields, spread = prepare(
+        later, neighbours, kernel_one, kernel_two, features, cotangent, occupancy
     )
-    terms = lax.all_to_all(terms, AXES, 0, 0, tiled=True)
-    before, after = exchange(ahead, behind, devices)
-    terms, before, after = lax.optimization_barrier((terms, before, after))
-    output, grad_in = second_stage(lookup, occupancy, second, result, before, after)
-    spread = combine(terms.reshape(devices, TERMS // devices, LANES)).reshape(TERMS, LANES)
-    sums = lax.all_to_all(spread, AXES, 0, 0, tiled=True)
+    result, near_send, far_send, given, kept = first_stage(
+        lookup, chosen, occupancy, first, spread, near, far, fields
+    )
+    cores = [list(range(c, devices, 2)) for c in range(2)]
+    blocks = devices // 2
+
+    def to_all(rows):
+        return lax.all_to_all(rows, AXES, 0, 0, axis_index_groups=cores, tiled=True)
+
+    terms = to_all(pair_sum(kept, near_swap(given, devices)))
+    far = far_swap(far_send, devices)
+    near = near_swap(near_send, devices)
+    terms, near, far = lax.optimization_barrier((terms, near, far))
+    output, grad_in = second_stage(lookup, occupancy, second, result, near, far)
+    spread = combine(terms.reshape(blocks, HALF // blocks, LANES)).reshape(HALF, LANES)
+    own = to_all(spread)
+    own, output, grad_in = lax.optimization_barrier((own, output, grad_in))
+    other = near_swap(own, devices)
     scale = float((SLOTS * VOX * devices) ** -0.5)
-    grad_one, grad_two = unpack(scale, sums)
+    grad_one, grad_two = unpack(scale, position, own, other)
     return output, grad_in, grad_one, grad_two
 
 

time: 84.5 us -> 75.5 us (0.89)
  waiting for transfers between devices: 12.6 us -> 4.25 us
  blocking collectives: 25.5 us -> 23.7 us
  Pallas kernels: 26.2 us -> 27.5 us
    all_to_all x1, waiting for transfers between devices: 6.23 us -> 1.56 us  [to_all(): return lax.all_to_all(rows, AXES, 0, 0, axis_index_groups=cores, tiled=True)]
    ppermute x4 -> x6, waiting for transfers between devices: 6.42 us -> 2.69 us  [the longest x4 2.69 us: near_swap(): return lax.ppermute(rows, AXES, [(k, k ^ 1) for k in range(devices)])]
    all_to_all x1, blocking collectives: 25.5 us -> 23.7 us  [to_all(): return lax.all_to_all(rows, AXES, 0, 0, axis_index_groups=cores, tiled=True)]
    pallas_call x1, Pallas kernels: 2.33 us -> 3.62 us  [prepare(): pl.pallas_call(prepare_kernel, out_shape=(jax.ShapeDtypeStruct((2, 3, 2 *...]
    all_to_all x1, starting transfers between devices: 5.84 us -> 4.89 us  [to_all(): return lax.all_to_all(rows, AXES, 0, 0, axis_index_groups=cores, tiled=True)]
    ppermute x4 -> x6, starting transfers between devices: 11.2 us -> 12 us  [the longest x2 7.44 us: far_swap(): return lax.ppermute(rows, AXES, route)]
    pallas_call x1 -> x2, Pallas kernels: 4.15 us -> 3.43 us  [the longest x1 3.37 us: pack(): pl.pallas_call(pack_kernel, out_shape=(jax.ShapeDtypeStruct((NEAR, RIM, L...]
  transfers between devices with their start and end apart: 5 -> 7, of which waited for: 3 -> 3; matrix products, arithmetic and copies ran while one was open for 0% -> 0% of each run, Pallas kernels for 12% -> 15%
where the time goes in v3:
time: 75.5 us; the launch traced here: 75.1 us
  Pallas kernels  27.5 us (36%)
  blocking collectives  23.7 us (31%)
  starting transfers between devices  16.9 us (22%)
  waiting for transfers between devices  4.25 us (6%)
  local copies, waits for them, and re-layouts  2.04 us (3%)
  between operations  0.81 us (1%)
    all_to_all x1, blocking collectives, to_all(): return lax.all_to_all(rows, AXES, 0, 0, axis_index_groups=cores, tiled=True)  23.7 us
    pallas_call x1, Pallas kernels, first_stage(): pl.pallas_call(first_kernel, out_shape=(jax.ShapeDtypeStruct((SLOTS, VOX,...  10.3 us
    pallas_call x1, Pallas kernels, second_stage(): pl.pallas_call(second_kernel, out_shape=(jax.ShapeDtypeStruct((SLOTS, CH,...  7.58 us
    ppermute x2, starting transfers between devices, far_swap(): return lax.ppermute(rows, AXES, route)  7.44 us
    all_to_all x1, starting transfers between devices, to_all(): return lax.all_to_all(rows, AXES, 0, 0, axis_index_groups=cores, tiled=True)  4.89 us
    ppermute x4, starting transfers between devices, near_swap(): return lax.ppermute(rows, AXES, [(k, k ^ 1) for k in range(devices)])  4.54 us
    pallas_call x1, Pallas kernels, prepare(): pl.pallas_call(prepare_kernel, out_shape=(jax.ShapeDtypeStruct((2, 3, 2 *...  3.62 us
    pallas_call x1, Pallas kernels, pack(): pl.pallas_call(pack_kernel, out_shape=(jax.ShapeDtypeStruct((NEAR, RIM, L...  3.37 us
  transfers between devices with their start and end apart: 7, of which 3 were waited for; matrix products, arithmetic and copies ran while one was open for 0% of the time, Pallas kernels for 15%

profile of v3, /device:TPU:1, one launch (start us, length us, event | category | flops | bytes accessed | tf_op | source)
XLA Modules:
  0.0 75.1 jit_solution(6956618039469697915)
XLA Ops:
  0.6 0.0 copy-start
  0.6 0.0 copy-start.1
  0.7 0.0 copy-start.4
  0.7 0.0 copy-start.5
  0.7 3.4 %pack.1 = (bf16[4,304,128]{2,1,0:T(8,128)(2,1)}, bf16[4,304,128]{2,1,0:T(8,128)(2,1)}) custom-call(s32[1]{0:T(128)} %bitcast.position.refs_0_, s32[8,26]{1,0:T(8,128)} %neighbours.3, bf16[8,64,512]{2,1,0:T(8,128)(2,1)} %features.1, bf16[8,64,512]{2,1,0:T(8,128)(2,1)} %cotangent.1, s32[8,512]{1,0:T(8,128)} %occupancy.5), custom_call_target="tpu_custom_call" | custom-call | tf_op jit(solution)/shard_map/pack/pallas_call | solution.py:117
  4.1 1.5 %collective-permute-start = (bf16[4,304,128]{2,1,0:T(8,128)(2,1)}, bf16[4,304,128]{2,1,0:T(8,128)(2,1)S(1)}, u32[]{:S(2)}, u32[]{:S(2)}) collective-permute-start(bf16[4,304,128]{2,1,0:T(8,128)(2,1)} %get-tuple-element.37), channel_id=1, source_target_pairs={{0,1},{1,0},{2,3},{3,2},{4,5},{5,4},{6,7},{7,6},{8,9},{9,8},{10,11... | collective-permute-start | bytes 933896 | tf_op jit(solution)/shard_map/ppermute | solution.py:534
  5.6 3.5 %collective-permute-start.1 = (bf16[4,304,128]{2,1,0:T(8,128)(2,1)}, bf16[4,304,128]{2,1,0:T(8,128)(2,1)S(1)}, u32[]{:S(2)}, u32[]{:S(2)}) collective-permute-start(bf16[4,304,128]{2,1,0:T(8,128)(2,1)} %get-tuple-element.38), channel_id=1, source_target_pairs={{1,2},{3,4},{5,6},{7,8},{9,10},{11,12},{13,14},{15,16},{17,18},{19... | collective-permute-start | bytes 933896 | tf_op jit(solution)/shard_map/ppermute | solution.py:540
  9.1 0.0 copy-done
  9.1 0.0 copy-done.1
  9.1 0.0 copy-done.4
  9.1 0.0 copy-done.5
  9.1 0.0 copy-start.2
  9.1 1.0 %copy-done.2 = bf16[27,64,64]{2,1,0:T(8,128)(2,1)S(1)} copy-done((bf16[27,64,64]{2,1,0:T(8,128)(2,1)S(1)}, bf16[27,64,64]{2,1,0:T(8,128)(2,1)}, u32[]{:S(2)}) %copy-start.2) | copy-done | bytes 221208
  10.1 0.0 copy-start.3
  10.2 1.0 %copy-done.3 = bf16[27,64,64]{2,1,0:T(8,128)(2,1)S(1)} copy-done((bf16[27,64,64]{2,1,0:T(8,128)(2,1)S(1)}, bf16[27,64,64]{2,1,0:T(8,128)(2,1)}, u32[]{:S(2)}) %copy-start.3) | copy-done | bytes 221208
  11.2 3.6 %prepare.1 = (bf16[2,3,256,256]{3,2,1,0:T(8,128)(2,1)S(1)}, bf16[2,3,256,256]{3,2,1,0:T(8,128)(2,1)S(1)}, s32[216]{0:T(256)S(1)}, s32[2,8]{1,0:T(2,128)S(1)}, bf...) custom-call(s32[1]{0:T(128)} %bitcast.position.refs_0_, s32[8,26]{1,0:T(8,128)S(1)} %copy-done.5, ...), custom_call_target="tpu_custom_call" | custom-call | flops 4000000 | bytes 4000000 | tf_op jit(solution)/shard_map/prepare/pallas_call | solution.py:210
  14.8 0.0 collective-permute-done.near
  14.8 0.0 collective-permute-done.1.far
  14.8 10.3 %first_stage.1 = (bf16[8,512,128]{2,1,0:T(8,128)(2,1)S(1)}, bf16[4,512,128]{2,1,0:T(8,128)(2,1)S(1)}, bf16[4,512,128]{2,1,0:T(8,128)(2,1)S(1)}, bf16[1024,128]{1,0:T(8,128)(2,1)S(1)}, f32[1024,128]{1,0:T(8,128)S(1)}) custom-call(s32[216]{0:T(256)S(1)} %get-tuple-element.33.lookup, s32[2,8]{1,0:T(2,128)S(1)} %get-tuple-element.34.chosen, ...), custom_call_target="tpu_custom_call" | custom-call | flops 8000000000 | bytes 6000000 | tf_op jit(solution)/shard_map/first_stage/pallas_call | solution.py:393
  25.1 0.1 collective-permute-start.3
  25.2 3.9 %collective-permute-start.4 = (bf16[4,512,128]{2,1,0:T(8,128)(2,1)S(1)}, bf16[4,512,128]{2,1,0:T(8,128)(2,1)S(1)}, u32[]{:S(2)}, u32[]{:S(2)}) collective-permute-start(bf16[4,512,128]{2,1,0:T(8,128)(2,1)S(1)} %get-tuple-element.43), channel_id=1, source_target_pairs={{1,2},{3,4},{5,6},{7,8},{9,10},{11,12},{13,14},{15,16},{17,18},{19... | collective-permute-start | bytes 1572872 | tf_op jit(solution)/shard_map/ppermute | solution.py:540
  29.2 0.1 collective-permute-start.2
  29.2 1.5 %collective-permute-done.2.received = bf16[1024,128]{1,0:T(8,128)(2,1)S(1)} collective-permute-done((bf16[1024,128]{1,0:T(8,128)(2,1)S(1)}, bf16[1024,128]{1,0:T(8,128)(2,1)S(1)}, u32[]{:S(2)}, u32[]{:S(2)}) %collective-permute-start.2) | collective-permute-done | bytes 262176 | tf_op jit(solution)/shard_map/ppermute | solution.py:534
  30.8 0.1 pair_sum.1
  30.8 23.7 %all_to_all.21 = bf16[64,16,128]{2,1,0:T(8,128)(2,1)S(1)} all-to-all(bf16[64,16,128]{2,1,0:T(8,128)(2,1)S(1)} %bitcast.7), channel_id=1, replica_groups={{0,2,4,6,8,10,12,14,16,18,20,22,24,26,28,30,32,34,36,38,40,42,44,46,48,..., dimensions={0} | all-to-all | bytes 524288 | tf_op jit(solution)/shard_map/all_to_all | solution.py:559
  54.5 0.0 collective-permute-done.3.before
  54.5 0.0 collective-permute-done.4.after
  54.5 0.8 %combine.1 = bf16[64,16,128]{2,1,0:T(8,128)(2,1)} custom-call(bf16[64,16,128]{2,1,0:T(8,128)(2,1)S(1)} %all_to_all.21), custom_call_target="tpu_custom_call" | custom-call | tf_op jit(solution)/shard_map/combine/pallas_call | solution.py:483
  55.3 4.9 %all-to-all-start.1 = ((bf16[64,16,128]{2,1,0:T(8,128)(2,1)}), bf16[64,16,128]{2,1,0:T(8,128)(2,1)S(1)}, u32[]{:S(2)}, u32[]{:S(2)}) async-start(bf16[64,16,128]{2,1,0:T(8,128)(2,1)} %combine.1), calls=%async_computation.1 | async-start | bytes 524288 | tf_op jit(solution)/shard_map/all_to_all | solution.py:559
  60.2 7.6 %second_stage.1 = (bf16[8,64,512]{2,1,0:T(8,128)(2,1)}, bf16[8,64,512]{2,1,0:T(8,128)(2,1)}) custom-call(s32[216]{0:T(256)S(1)} %get-tuple-element.33.lookup, s32[8,512]{1,0:T(8,128)S(1)} %copy-done.4, bf16[2,3,256,256]{3,2,1,0:T(8,128)(2,1)S(1)} %get-tuple-element.45.weights, bf16[8,512,128]{2,1,0:T(8,128)(2,1)S(1)} %get-tuple-element.46.own, ...), custom_call_target="tpu_custom_call" | custom-call | flops 8000000000 | bytes 6000000 | tf_op jit(solution)/shard_map/second_stage/pallas_call | solution.py:438
  67.8 1.6 %all-to-all-done.1 = bf16[64,16,128]{2,1,0:T(8,128)(2,1)S(1)} async-done(((bf16[64,16,128]{2,1,0:T(8,128)(2,1)}), bf16[64,16,128]{2,1,0:T(8,128)(2,1)S(1)}, u32[]{:S(2)}, u32[]{:S(2)}) %all-to-all-start.1) | async-done | bytes 262176 | tf_op jit(solution)/shard_map/all_to_all | solution.py:559
  69.3 2.9 %collective-permute-start.5 = (bf16[1024,128]{1,0:T(8,128)(2,1)S(1)}, bf16[1024,128]{1,0:T(8,128)(2,1)S(1)}, u32[]{:S(2)}, u32[]{:S(2)}) collective-permute-start(bf16[1024,128]{1,0:T(8,128)(2,1)S(1)} %bitcast.5), channel_id=1, source_target_pairs={{0,1},{1,0},{2,3},{3,2},{4,5},{5,4},{6,7},{7,6},{8,9},{9,8},{10,11... | collective-permute-start | bytes 786440 | tf_op jit(solution)/shard_map/ppermute | solution.py:534
  72.2 1.2 %collective-permute-done.5.refs_2_ = bf16[1024,128]{1,0:T(8,128)(2,1)S(1)} collective-permute-done((bf16[1024,128]{1,0:T(8,128)(2,1)S(1)}, bf16[1024,128]{1,0:T(8,128)(2,1)S(1)}, u32[]{:S(2)}, u32[]{:S(2)}) %collective-permute-start.5) | collective-permute-done | bytes 262176 | tf_op jit(solution)/shard_map/ppermute | solution.py:534
  73.4 1.7 %unpack.1 = (f32[27,64,64]{2,1,0:T(8,128)}, f32[27,64,64]{2,1,0:T(8,128)}) custom-call(s32[1]{0:T(128)} %bitcast.position.refs_0_, bf16[1024,128]{1,0:T(8,128)(2,1)S(1)} %bitcast.6, bf16[1024,128]{1,0:T(8,128)(2,1)S(1)} %collective-permute-done.5.refs_2_), custom_call_target="tpu_custom_call" | custom-call | tf_op jit(solution)/shard_map/unpack/pallas_call | solution.py:519
Async XLA Ops:
  0.6 8.5 %copy-start = (bf16[8,64,512]{2,1,0:T(8,128)(2,1)S(1)}, bf16[8,64,512]{2,1,0:T(8,128)(2,1)}, u32[]{:S(2)}) copy-start(bf16[8,64,512]{2,1,0:T(8,128)(2,1)} %features.1) | copy-start | bytes 1572868
  0.6 8.5 %copy-start.1 = (bf16[8,64,512]{2,1,0:T(8,128)(2,1)S(1)}, bf16[8,64,512]{2,1,0:T(8,128)(2,1)}, u32[]{:S(2)}) copy-start(bf16[8,64,512]{2,1,0:T(8,128)(2,1)} %cotangent.1) | copy-start | bytes 1572868
  0.7 8.5 %copy-start.4 = (s32[8,512]{1,0:T(8,128)S(1)}, s32[8,512]{1,0:T(8,128)}, u32[]{:S(2)}) copy-start(s32[8,512]{1,0:T(8,128)} %occupancy.5) | copy-start | bytes 49156
  0.7 8.5 %copy-start.5 = (s32[8,26]{1,0:T(8,128)S(1)}, s32[8,26]{1,0:T(8,128)}, u32[]{:S(2)}) copy-start(s32[8,26]{1,0:T(8,128)} %neighbours.3) | copy-start | bytes 2500
  4.1 10.7 %collective-permute-start = (bf16[4,304,128]{2,1,0:T(8,128)(2,1)}, bf16[4,304,128]{2,1,0:T(8,128)(2,1)S(1)}, u32[]{:S(2)}, u32[]{:S(2)}) collective-permute-start(bf16[4,304,128]{2,1,0:T(8,128)(2,1)} %get-tuple-element.37), channel_id=1, source_target_pairs={{0,1},{1,0},{2,3},{3,2},{4,5},{5,4},{6,7},{7,6},{8,9},{9,8},{10,11... | collective-permute-start | bytes 933896 | tf_op jit(solution)/shard_map/ppermute | solution.py:534
  5.6 9.2 %collective-permute-start.1 = (bf16[4,304,128]{2,1,0:T(8,128)(2,1)}, bf16[4,304,128]{2,1,0:T(8,128)(2,1)S(1)}, u32[]{:S(2)}, u32[]{:S(2)}) collective-permute-start(bf16[4,304,128]{2,1,0:T(8,128)(2,1)} %get-tuple-element.38), channel_id=1, source_target_pairs={{1,2},{3,4},{5,6},{7,8},{9,10},{11,12},{13,14},{15,16},{17,18},{19... | collective-permute-start | bytes 933896 | tf_op jit(solution)/shard_map/ppermute | solution.py:540
  9.1 1.0 %copy-start.2 = (bf16[27,64,64]{2,1,0:T(8,128)(2,1)S(1)}, bf16[27,64,64]{2,1,0:T(8,128)(2,1)}, u32[]{:S(2)}) copy-start(bf16[27,64,64]{2,1,0:T(8,128)(2,1)} %kernel_one.1) | copy-start | bytes 663556
  10.1 1.0 %copy-start.3 = (bf16[27,64,64]{2,1,0:T(8,128)(2,1)S(1)}, bf16[27,64,64]{2,1,0:T(8,128)(2,1)}, u32[]{:S(2)}) copy-start(bf16[27,64,64]{2,1,0:T(8,128)(2,1)} %kernel_two.1) | copy-start | bytes 663556
  25.1 29.4 %collective-permute-start.3 = (bf16[4,512,128]{2,1,0:T(8,128)(2,1)S(1)}, bf16[4,512,128]{2,1,0:T(8,128)(2,1)S(1)}, u32[]{:S(2)}, u32[]{:S(2)}) collective-permute-start(bf16[4,512,128]{2,1,0:T(8,128)(2,1)S(1)} %get-tuple-element.42), channel_id=1, source_target_pairs={{0,1},{1,0},{2,3},{3,2},{4,5},{5,4},{6,7},{7,6},{8,9},{9,8},{10,11... | collective-permute-start | bytes 1572872 | tf_op jit(solution)/shard_map/ppermute | solution.py:534
  25.2 29.3 %collective-permute-start.4 = (bf16[4,512,128]{2,1,0:T(8,128)(2,1)S(1)}, bf16[4,512,128]{2,1,0:T(8,128)(2,1)S(1)}, u32[]{:S(2)}, u32[]{:S(2)}) collective-permute-start(bf16[4,512,128]{2,1,0:T(8,128)(2,1)S(1)} %get-tuple-element.43), channel_id=1, source_target_pairs={{1,2},{3,4},{5,6},{7,8},{9,10},{11,12},{13,14},{15,16},{17,18},{19... | collective-permute-start | bytes 1572872 | tf_op jit(solution)/shard_map/ppermute | solution.py:540
  29.2 1.6 %collective-permute-start.2 = (bf16[1024,128]{1,0:T(8,128)(2,1)S(1)}, bf16[1024,128]{1,0:T(8,128)(2,1)S(1)}, u32[]{:S(2)}, u32[]{:S(2)}) collective-permute-start(bf16[1024,128]{1,0:T(8,128)(2,1)S(1)} %get-tuple-element.41), channel_id=1, source_target_pairs={{0,1},{1,0},{2,3},{3,2},{4,5},{5,4},{6,7},{7,6},{8,9},{9,8},{10,11... | collective-permute-start | bytes 786440 | tf_op jit(solution)/shard_map/ppermute | solution.py:534
  55.3 14.0 %all-to-all-start.1 = ((bf16[64,16,128]{2,1,0:T(8,128)(2,1)}), bf16[64,16,128]{2,1,0:T(8,128)(2,1)S(1)}, u32[]{:S(2)}, u32[]{:S(2)}) async-start(bf16[64,16,128]{2,1,0:T(8,128)(2,1)} %combine.1), calls=%async_computation.1 | async-start | bytes 524288 | tf_op jit(solution)/shard_map/all_to_all | solution.py:559
  69.3 4.0 %collective-permute-start.5 = (bf16[1024,128]{1,0:T(8,128)(2,1)S(1)}, bf16[1024,128]{1,0:T(8,128)(2,1)S(1)}, u32[]{:S(2)}, u32[]{:S(2)}) collective-permute-start(bf16[1024,128]{1,0:T(8,128)(2,1)S(1)} %bitcast.5), channel_id=1, source_target_pairs={{0,1},{1,0},{2,3},{3,2},{4,5},{5,4},{6,7},{7,6},{8,9},{9,8},{10,11... | collective-permute-start | bytes 786440 | tf_op jit(solution)/shard_map/ppermute | solution.py:534

commit v4 on v3

--- a/solution.py
+++ b/solution.py
@@ -165,12 +165,10 @@
 
 def prepare_kernel(
     position, neighbours, kernel_one, kernel_two, features, cotangent, occupancy,
-    first, second, lookup, chosen, fields, spread, flags, base,
+    first, lookup, chosen, fields, spread, flags, base,
 ):
     weight_field(kernel_one, False, 0, first)
     weight_field(kernel_two, True, 1, first)
-    weight_field(kernel_two, False, 0, second)
-    weight_field(kernel_one, True, 1, second)
     for b in range(SLOTS):
         fields[b] = side_by_side(features, cotangent, occupancy, b)
     choose(position, neighbours, chosen)
@@ -211,19 +209,46 @@
         prepare_kernel,
         out_shape=(
             jax.ShapeDtypeStruct((2, 3, 2 * LANES, 2 * LANES), BF16),
-            jax.ShapeDtypeStruct((2, 3, 2 * LANES, 2 * LANES), BF16),
             jax.ShapeDtypeStruct((27 * SLOTS,), jnp.int32),
             jax.ShapeDtypeStruct((2, SLOTS), jnp.int32),
             jax.ShapeDtypeStruct((SLOTS, VOX, LANES), BF16),
             jax.ShapeDtypeStruct((VOX, RIM), BF16),
         ),
         in_specs=[whole_smem, whole_smem] + [whole_vmem] * 5,
-        out_specs=(whole_vmem, whole_vmem, whole_smem, whole_smem) + (whole_vmem,) * 2,
+        out_specs=(whole_vmem, whole_smem, whole_smem) + (whole_vmem,) * 2,
         scratch_shapes=[pltpu.SMEM((32,), jnp.int32), pltpu.SMEM((32,), jnp.int32)],
         compiler_params=pltpu.CompilerParams(vmem_limit_bytes=VMEM),
         cost_estimate=pl.CostEstimate(flops=4000000, bytes_accessed=4000000, transcendentals=0),
         name="prepare",
     )(position, neighbours, kernel_one, kernel_two, features, cotangent, occupancy)
+
+
+def relay_kernel(
+    after, chosen, kernel_one, kernel_two, result, second, near_send, far_send
+):
+    for r in range(NEAR):
+        far_send[r] = result[chosen[1, r]]
+        near_send[r] = result[chosen[0, r]]
+    weight_field(kernel_two, False, 0, second)
+    weight_field(kernel_one, True, 1, second)
+
+
+def relay(after, chosen, kernel_one, kernel_two, result):
+    return pl.pallas_call(
+        relay_kernel,
+        out_shape=(
+            jax.ShapeDtypeStruct((2, 3, 2 * LANES, 2 * LANES), BF16),
+            jax.ShapeDtypeStruct((NEAR, VOX, LANES), BF16),
+            jax.ShapeDtypeStruct((NEAR, VOX, LANES), BF16),
+        ),
+        in_specs=[whole_smem, whole_smem] + [whole_vmem] * 3,
+        out_specs=(whole_vmem,) * 3,
+        compiler_params=pltpu.CompilerParams(vmem_limit_bytes=VMEM),
+        cost_estimate=pl.CostEstimate(
+            flops=5000000000, bytes_accessed=2000000, transcendentals=0
+        ),
+        name="relay",
+    )(after, chosen, kernel_one, kernel_two, result)
 
 
 def fill_pool(own, before, after, pool, sems):
@@ -328,7 +353,7 @@
 
 def first_kernel(
     lookup, chosen, occupancy, weights, spread, near, far, own,
-    result, ahead, behind, given, kept, pool, tiles, sum_one, sum_two, terms, sems,
+    result, given, kept, pool, tiles, sum_one, sum_two, terms, sems,
 ):
     load = pltpu.make_async_copy(own, pool.at[pl.ds(0, SLOTS)], sems.at[0])
     load.start()
@@ -372,9 +397,6 @@
             sum_one[a] += jnp.dot(grad_pre, rows(0), preferred_element_type=F32)
             sum_two[a] += jnp.dot(hidden, rows(LANES), preferred_element_type=F32)
 
-    for r in range(NEAR):
-        ahead[r] = result[chosen[0, r]]
-        behind[r] = result[chosen[1, r]]
     part = 3 * CH
     for a in range(3):
         start = a * 3 * part
@@ -394,13 +416,11 @@
         first_kernel,
         out_shape=(
             jax.ShapeDtypeStruct((SLOTS, VOX, LANES), BF16),
-            jax.ShapeDtypeStruct((NEAR, VOX, LANES), BF16),
-            jax.ShapeDtypeStruct((NEAR, VOX, LANES), BF16),
             jax.ShapeDtypeStruct((HALF, LANES), BF16),
             jax.ShapeDtypeStruct((HALF, LANES), F32),
         ),
         in_specs=[whole_smem, whole_smem] + [whole_vmem] * 5 + [anywhere],
-        out_specs=(whole_vmem,) * 5,
+        out_specs=(whole_vmem,) * 3,
         scratch_shapes=[
             pltpu.VMEM((POOL, VOX, LANES), BF16),
             pltpu.VMEM((4, TILE_ROWS, 3 * LANES), BF16),
@@ -486,6 +506,9 @@
         in_specs=[whole_vmem],
         out_specs=whole_vmem,
         compiler_params=pltpu.CompilerParams(vmem_limit_bytes=VMEM),
+        cost_estimate=pl.CostEstimate(
+            flops=20000000000, bytes_accessed=1000000, transcendentals=0
+        ),
         name="combine",
     )(blocks)
 
@@ -546,10 +569,10 @@
     near_send, far_send, later = lax.optimization_barrier((near_send, far_send, position))
     far = far_swap(far_send, devices)
     near = near_swap(near_send, devices)
-    first, second, lookup, chosen, fields, spread = prepare(
+    first, lookup, chosen, fields, spread = prepare(
         later, neighbours, kernel_one, kernel_two, features, cotangent, occupancy
     )
-    result, near_send, far_send, given, kept = first_stage(
+    result, given, kept = first_stage(
         lookup, chosen, occupancy, first, spread, near, far, fields
     )
     cores = [list(range(c, devices, 2)) for c in range(2)]
@@ -558,10 +581,13 @@
     def to_all(rows):
         return lax.all_to_all(rows, AXES, 0, 0, axis_index_groups=cores, tiled=True)
 
-    terms = to_all(pair_sum(kept, near_swap(given, devices)))
+    paired = pair_sum(kept, near_swap(given, devices))
+    paired, later = lax.optimization_barrier((paired, later))
+    terms = to_all(paired)
+    second, near_send, far_send = relay(later, chosen, kernel_one, kernel_two, result)
     far = far_swap(far_send, devices)
     near = near_swap(near_send, devices)
-    terms, near, far = lax.optimization_barrier((terms, near, far))
+    terms, second = lax.optimization_barrier((terms, second))
     output, grad_in = second_stage(lookup, occupancy, second, result, near, far)
     spread = combine(terms.reshape(blocks, HALF // blocks, LANES)).reshape(HALF, LANES)
     own = to_all(spread)

time: 75.5 us -> 73.1 us (0.968)
  blocking collectives: 23.7 us -> 0 us
  starting transfers between devices: 16.9 us -> 31.3 us
  waiting for transfers between devices: 4.25 us -> 7.13 us
  local copies, waits for them, and re-layouts: 2.04 us -> 4.49 us
  Pallas kernels: 27.5 us -> 28.8 us
    all_to_all x1 -> x0, blocking collectives: 23.7 us -> none  [to_all(): return lax.all_to_all(rows, AXES, 0, 0, axis_index_groups=cores, tiled=True)]
    all_to_all x1 -> x2, starting transfers between devices: 4.89 us -> 20.6 us  [to_all(): return lax.all_to_all(rows, AXES, 0, 0, axis_index_groups=cores, tiled=True)]
    all_to_all x1 -> x2, waiting for transfers between devices: 1.56 us -> 4.43 us  [to_all(): return lax.all_to_all(rows, AXES, 0, 0, axis_index_groups=cores, tiled=True)]
    unnamed x12 -> x22, local copies, waits for them, and re-layouts: 2.04 us -> 4.49 us
    pallas_call x0 -> x1, Pallas kernels: none -> 0.94 us  [relay(): pl.pallas_call(relay_kernel, out_shape=(jax.ShapeDtypeStruct((2, 3, 2 * L...]
    ppermute x2, starting transfers between devices: 7.44 us -> 6.62 us  [far_swap(): return lax.ppermute(rows, AXES, route)]
  transfers between devices with their start and end apart: 7 -> 8, of which waited for: 3 -> 4; matrix products, arithmetic and copies ran while one was open for 0% -> 0% of each run, Pallas kernels for 15% -> 17%
where the time goes in v4:
time: 73.1 us; the launch traced here: 72.6 us
  starting transfers between devices  31.3 us (43%)
  Pallas kernels  28.8 us (39%)
  waiting for transfers between devices  7.13 us (10%)
  local copies, waits for them, and re-layouts  4.49 us (6%)
  between operations  0.88 us (1%)
    all_to_all x2, starting transfers between devices, to_all(): return lax.all_to_all(rows, AXES, 0, 0, axis_index_groups=cores, tiled=True)  20.6 us
    pallas_call x1, Pallas kernels, first_stage(): pl.pallas_call(first_kernel, out_shape=(jax.ShapeDtypeStruct((SLOTS, VOX,...  10.3 us
    pallas_call x1, Pallas kernels, second_stage(): pl.pallas_call(second_kernel, out_shape=(jax.ShapeDtypeStruct((SLOTS, CH,...  7.57 us
    ppermute x2, starting transfers between devices, far_swap(): return lax.ppermute(rows, AXES, route)  6.62 us
    unnamed x22, local copies, waits for them, and re-layouts  4.49 us
    all_to_all x2, waiting for transfers between devices, to_all(): return lax.all_to_all(rows, AXES, 0, 0, axis_index_groups=cores, tiled=True)  4.43 us
    ppermute x4, starting transfers between devices, near_swap(): return lax.ppermute(rows, AXES, [(k, k ^ 1) for k in range(devices)])  4.16 us
    pallas_call x1, Pallas kernels, prepare(): pl.pallas_call(prepare_kernel, out_shape=(jax.ShapeDtypeStruct((2, 3, 2 *...  3.38 us
  transfers between devices with their start and end apart: 8, of which 4 were waited for; matrix products, arithmetic and copies ran while one was open for 0% of the time, Pallas kernels for 17%

profile of v4, /device:TPU:1, one launch (start us, length us, event | category | flops | bytes accessed | tf_op | source)
XLA Modules:
  0.0 72.6 jit_solution(9436634139976574574)
XLA Ops:
  0.6 0.0 copy-start
  0.6 0.0 copy-start.1
  0.7 0.0 copy-start.6
  0.7 0.0 copy-start.7
  0.7 3.4 %pack.1 = (bf16[4,304,128]{2,1,0:T(8,128)(2,1)}, bf16[4,304,128]{2,1,0:T(8,128)(2,1)}) custom-call(s32[1]{0:T(128)} %bitcast.position.after.refs_0_, s32[8,26]{1,0:T(8,128)} %neighbours.3, bf16[8,64,512]{2,1,0:T(8,128)(2,1)} %features.1, bf16[8,64,512]{2,1,0:T(8,128)(2,1)} %cotangent.1, s32[8,512]{1,0:T(8,128)} %occupancy.5), custom_call_target="tpu_custom_call" | custom-call | tf_op jit(solution)/shard_map/pack/pallas_call | solution.py:117
  4.1 1.5 %collective-permute-start = (bf16[4,304,128]{2,1,0:T(8,128)(2,1)}, bf16[4,304,128]{2,1,0:T(8,128)(2,1)S(1)}, u32[]{:S(2)}, u32[]{:S(2)}) collective-permute-start(bf16[4,304,128]{2,1,0:T(8,128)(2,1)} %get-tuple-element.38), channel_id=1, source_target_pairs={{0,1},{1,0},{2,3},{3,2},{4,5},{5,4},{6,7},{7,6},{8,9},{9,8},{10,11... | collective-permute-start | bytes 933896 | tf_op jit(solution)/shard_map/ppermute | solution.py:557
  5.6 3.5 %collective-permute-start.1 = (bf16[4,304,128]{2,1,0:T(8,128)(2,1)}, bf16[4,304,128]{2,1,0:T(8,128)(2,1)S(1)}, u32[]{:S(2)}, u32[]{:S(2)}) collective-permute-start(bf16[4,304,128]{2,1,0:T(8,128)(2,1)} %get-tuple-element.39), channel_id=1, source_target_pairs={{1,2},{3,4},{5,6},{7,8},{9,10},{11,12},{13,14},{15,16},{17,18},{19... | collective-permute-start | bytes 933896 | tf_op jit(solution)/shard_map/ppermute | solution.py:563
  9.1 0.0 copy-done
  9.1 0.0 copy-done.1
  9.1 0.0 copy-done.6
  9.1 0.0 copy-done.7
  9.1 0.0 copy-start.2
  9.1 1.0 %copy-done.2 = bf16[27,64,64]{2,1,0:T(8,128)(2,1)S(1)} copy-done((bf16[27,64,64]{2,1,0:T(8,128)(2,1)S(1)}, bf16[27,64,64]{2,1,0:T(8,128)(2,1)}, u32[]{:S(2)}) %copy-start.2) | copy-done | bytes 221208
  10.1 0.0 copy-start.4
  10.2 1.0 %copy-done.4 = bf16[27,64,64]{2,1,0:T(8,128)(2,1)S(1)} copy-done((bf16[27,64,64]{2,1,0:T(8,128)(2,1)S(1)}, bf16[27,64,64]{2,1,0:T(8,128)(2,1)}, u32[]{:S(2)}) %copy-start.4) | copy-done | bytes 221208
  11.2 3.4 %prepare.1 = (bf16[2,3,256,256]{3,2,1,0:T(8,128)(2,1)S(1)}, s32[216]{0:T(256)S(1)}, s32[2,8]{1,0:T(2,128)S(1)}, bf16[8,512,128]{2,1,0:T(8,128)(2,1)S(1)}, bf16[512,304]{1,0:T(8,128)(2,1)S(1)}) custom-call(s32[1]{0:T(128)} %bitcast.position.after.refs_0_, s32[8,26]{1,0:T(8,128)S(1)} %copy-done.7, bf16[27,64,64]{2,1,0:T(8,128)(2,1)S(1)} %copy-done.2, ...), custom_call_target="tpu_custom_call" | custom-call | flops 4000000 | bytes 4000000 | tf_op jit(solution)/shard_map/prepare/pallas_call | solution.py:208
  14.6 0.0 collective-permute-done.near
  14.6 0.0 collective-permute-done.1.far
  14.6 10.3 %first_stage.1 = (bf16[8,512,128]{2,1,0:T(8,128)(2,1)S(1)}, bf16[1024,128]{1,0:T(8,128)(2,1)S(1)}, f32[1024,128]{1,0:T(8,128)S(1)}) custom-call(s32[216]{0:T(256)S(1)} %get-tuple-element.34.lookup, s32[2,8]{1,0:T(2,128)S(1)} %get-tuple-element.35.chosen, s32[8,512]{1,0:T(8,128)S(1)} %copy-done.6, bf16[2,3,256,256]{3,2,1,0:T(8,128)(2,1)S(1)} %get-tuple-element.36.weights, ...), custom_call_target="tpu_custom_call" | custom-call | flops 8000000000 | bytes 6000000 | tf_op jit(solution)/shard_map/first_stage/pallas_call | solution.py:415
  24.9 0.0 copy-start.8
  24.9 0.1 collective-permute-start.2
  25.0 1.5 %collective-permute-done.2.received = bf16[1024,128]{1,0:T(8,128)(2,1)S(1)} collective-permute-done((bf16[1024,128]{1,0:T(8,128)(2,1)S(1)}, bf16[1024,128]{1,0:T(8,128)(2,1)S(1)}, u32[]{:S(2)}, u32[]{:S(2)}) %collective-permute-start.2) | collective-permute-done | bytes 262176 | tf_op jit(solution)/shard_map/ppermute | solution.py:557
  26.5 0.0 copy-start.5
  26.5 0.8 %pair_sum.1 = bf16[1024,128]{1,0:T(8,128)(2,1)} custom-call(f32[1024,128]{1,0:T(8,128)S(1)} %get-tuple-element.41.kept, bf16[1024,128]{1,0:T(8,128)(2,1)S(1)} %collective-permute-done.2.received), custom_call_target="tpu_custom_call" | custom-call | tf_op jit(solution)/shard_map/pair_sum/pallas_call | solution.py:484
  27.2 0.0 copy-start.3
  27.2 14.8 %all-to-all-start = ((bf16[64,16,128]{2,1,0:T(8,128)(2,1)}), bf16[64,16,128]{2,1,0:T(8,128)(2,1)S(1)}, u32[]{:S(2)}, u32[]{:S(2)}) async-start(bf16[64,16,128]{2,1,0:T(8,128)(2,1)} %bitcast.1), calls=%async_computation | async-start | bytes 524288 | tf_op jit(solution)/shard_map/all_to_all | solution.py:582
  42.0 0.0 copy-done.8
  42.0 0.0 copy-done.5
  42.1 0.0 copy-done.3
  42.1 0.0 copy-start.9
  42.1 1.2 %copy-done.9 = bf16[8,512,128]{2,1,0:T(8,128)(2,1)S(1)} copy-done((bf16[8,512,128]{2,1,0:T(8,128)(2,1)S(1)}, bf16[8,512,128]{2,1,0:T(8,128)(2,1)}, u32[]{:S(2)}) %copy-start.9) | copy-done | bytes 1048600
  43.3 0.9 %relay.1 = (bf16[2,3,256,256]{3,2,1,0:T(8,128)(2,1)S(1)}, bf16[4,512,128]{2,1,0:T(8,128)(2,1)S(1)}, bf16[4,512,128]{2,1,0:T(8,128)(2,1)S(1)}) custom-call(s32[1]{0:T(128)} %bitcast.position.after.refs_0_, s32[2,8]{1,0:T(2,128)S(1)} %get-tuple-element.35.chosen, bf16[27,64,64]{2,1,0:T(8,128)(2,1)S(1)} %copy-done.3, bf16[27,64,64]{2,1,0:T(8,128)(2,1)S(1)} %copy-done.5, ...), custom_call_target="tpu_custom_call" | custom-call | flops 5000000000 | bytes 2000000 | tf_op jit(solution)/shard_map/relay/pallas_call | solution.py:237
  44.2 0.5 collective-permute-start.3
  44.7 3.1 %collective-permute-start.4 = (bf16[4,512,128]{2,1,0:T(8,128)(2,1)S(1)}, bf16[4,512,128]{2,1,0:T(8,128)(2,1)S(1)}, u32[]{:S(2)}, u32[]{:S(2)}) collective-permute-start(bf16[4,512,128]{2,1,0:T(8,128)(2,1)S(1)} %get-tuple-element.50), channel_id=1, source_target_pairs={{1,2},{3,4},{5,6},{7,8},{9,10},{11,12},{13,14},{15,16},{17,18},{19... | collective-permute-start | bytes 1572872 | tf_op jit(solution)/shard_map/ppermute | solution.py:563
  47.9 4.1 %all-to-all-done = bf16[64,16,128]{2,1,0:T(8,128)(2,1)S(1)} async-done(((bf16[64,16,128]{2,1,0:T(8,128)(2,1)}), bf16[64,16,128]{2,1,0:T(8,128)(2,1)S(1)}, u32[]{:S(2)}, u32[]{:S(2)}) %all-to-all-start) | async-done | bytes 262176 | tf_op jit(solution)/shard_map/all_to_all | solution.py:582
  51.9 0.8 %combine.1 = bf16[64,16,128]{2,1,0:T(8,128)(2,1)} custom-call(bf16[64,16,128]{2,1,0:T(8,128)(2,1)S(1)} %all-to-all-done), custom_call_target="tpu_custom_call" | custom-call | flops 20000000000 | bytes 1000000 | tf_op jit(solution)/shard_map/combine/pallas_call | solution.py:503
  52.7 5.8 %all-to-all-start.1 = ((bf16[64,16,128]{2,1,0:T(8,128)(2,1)}), bf16[64,16,128]{2,1,0:T(8,128)(2,1)S(1)}, u32[]{:S(2)}, u32[]{:S(2)}) async-start(bf16[64,16,128]{2,1,0:T(8,128)(2,1)} %combine.1), calls=%async_computation.1 | async-start | bytes 524288 | tf_op jit(solution)/shard_map/all_to_all | solution.py:582
  58.5 0.0 collective-permute-done.3.before
  58.5 0.0 collective-permute-done.4.after
  58.5 0.0 copy-start.10
  58.5 1.2 %copy-done.10 = bf16[8,512,128]{2,1,0:T(8,128)(2,1)S(1)} copy-done((bf16[8,512,128]{2,1,0:T(8,128)(2,1)S(1)}, bf16[8,512,128]{2,1,0:T(8,128)(2,1)}, u32[]{:S(2)}) %copy-start.10) | copy-done | bytes 1048600
  59.7 7.6 %second_stage.1 = (bf16[8,64,512]{2,1,0:T(8,128)(2,1)}, bf16[8,64,512]{2,1,0:T(8,128)(2,1)}) custom-call(s32[216]{0:T(256)S(1)} %get-tuple-element.34.lookup, s32[8,512]{1,0:T(8,128)S(1)} %copy-done.6, bf16[2,3,256,256]{3,2,1,0:T(8,128)(2,1)S(1)} %get-tuple-element.48.weights, bf16[8,512,128]{2,1,0:T(8,128)(2,1)S(1)} %copy-done.10, ...), custom_call_target="tpu_custom_call" | custom-call | flops 8000000000 | bytes 6000000 | tf_op jit(solution)/shard_map/second_stage/pallas_call | solution.py:458
  67.3 0.4 all-to-all-done.1
  67.7 2.1 %collective-permute-start.5 = (bf16[1024,128]{1,0:T(8,128)(2,1)S(1)}, bf16[1024,128]{1,0:T(8,128)(2,1)S(1)}, u32[]{:S(2)}, u32[]{:S(2)}) collective-permute-start(bf16[1024,128]{1,0:T(8,128)(2,1)S(1)} %bitcast.5), channel_id=1, source_target_pairs={{0,1},{1,0},{2,3},{3,2},{4,5},{5,4},{6,7},{7,6},{8,9},{9,8},{10,11... | collective-permute-start | bytes 786440 | tf_op jit(solution)/shard_map/ppermute | solution.py:557
  69.7 1.2 %collective-permute-done.5.refs_2_ = bf16[1024,128]{1,0:T(8,128)(2,1)S(1)} collective-permute-done((bf16[1024,128]{1,0:T(8,128)(2,1)S(1)}, bf16[1024,128]{1,0:T(8,128)(2,1)S(1)}, u32[]{:S(2)}, u32[]{:S(2)}) %collective-permute-start.5) | collective-permute-done | bytes 262176 | tf_op jit(solution)/shard_map/ppermute | solution.py:557
  70.9 1.7 %unpack.1 = (f32[27,64,64]{2,1,0:T(8,128)}, f32[27,64,64]{2,1,0:T(8,128)}) custom-call(s32[1]{0:T(128)} %bitcast.position.after.refs_0_, bf16[1024,128]{1,0:T(8,128)(2,1)S(1)} %bitcast.6, bf16[1024,128]{1,0:T(8,128)(2,1)S(1)} %collective-permute-done.5.refs_2_), custom_call_target="tpu_custom_call" | custom-call | tf_op jit(solution)/shard_map/unpack/pallas_call | solution.py:542
Async XLA Ops:
  0.6 8.5 %copy-start = (bf16[8,64,512]{2,1,0:T(8,128)(2,1)S(1)}, bf16[8,64,512]{2,1,0:T(8,128)(2,1)}, u32[]{:S(2)}) copy-start(bf16[8,64,512]{2,1,0:T(8,128)(2,1)} %features.1) | copy-start | bytes 1572868
  0.6 8.5 %copy-start.1 = (bf16[8,64,512]{2,1,0:T(8,128)(2,1)S(1)}, bf16[8,64,512]{2,1,0:T(8,128)(2,1)}, u32[]{:S(2)}) copy-start(bf16[8,64,512]{2,1,0:T(8,128)(2,1)} %cotangent.1) | copy-start | bytes 1572868
  0.7 8.5 %copy-start.6 = (s32[8,512]{1,0:T(8,128)S(1)}, s32[8,512]{1,0:T(8,128)}, u32[]{:S(2)}) copy-start(s32[8,512]{1,0:T(8,128)} %occupancy.5) | copy-start | bytes 49156
  0.7 8.5 %copy-start.7 = (s32[8,26]{1,0:T(8,128)S(1)}, s32[8,26]{1,0:T(8,128)}, u32[]{:S(2)}) copy-start(s32[8,26]{1,0:T(8,128)} %neighbours.3) | copy-start | bytes 2500
  4.1 10.5 %collective-permute-start = (bf16[4,304,128]{2,1,0:T(8,128)(2,1)}, bf16[4,304,128]{2,1,0:T(8,128)(2,1)S(1)}, u32[]{:S(2)}, u32[]{:S(2)}) collective-permute-start(bf16[4,304,128]{2,1,0:T(8,128)(2,1)} %get-tuple-element.38), channel_id=1, source_target_pairs={{0,1},{1,0},{2,3},{3,2},{4,5},{5,4},{6,7},{7,6},{8,9},{9,8},{10,11... | collective-permute-start | bytes 933896 | tf_op jit(solution)/shard_map/ppermute | solution.py:557
  5.6 9.0 %collective-permute-start.1 = (bf16[4,304,128]{2,1,0:T(8,128)(2,1)}, bf16[4,304,128]{2,1,0:T(8,128)(2,1)S(1)}, u32[]{:S(2)}, u32[]{:S(2)}) collective-permute-start(bf16[4,304,128]{2,1,0:T(8,128)(2,1)} %get-tuple-element.39), channel_id=1, source_target_pairs={{1,2},{3,4},{5,6},{7,8},{9,10},{11,12},{13,14},{15,16},{17,18},{19... | collective-permute-start | bytes 933896 | tf_op jit(solution)/shard_map/ppermute | solution.py:563
  9.1 1.0 %copy-start.2 = (bf16[27,64,64]{2,1,0:T(8,128)(2,1)S(1)}, bf16[27,64,64]{2,1,0:T(8,128)(2,1)}, u32[]{:S(2)}) copy-start(bf16[27,64,64]{2,1,0:T(8,128)(2,1)} %kernel_one.3) | copy-start | bytes 663556
  10.1 1.0 %copy-start.4 = (bf16[27,64,64]{2,1,0:T(8,128)(2,1)S(1)}, bf16[27,64,64]{2,1,0:T(8,128)(2,1)}, u32[]{:S(2)}) copy-start(bf16[27,64,64]{2,1,0:T(8,128)(2,1)} %kernel_two.3) | copy-start | bytes 663556
  24.9 17.2 %copy-start.8 = (bf16[8,512,128]{2,1,0:T(8,128)(2,1)}, bf16[8,512,128]{2,1,0:T(8,128)(2,1)S(1)}, u32[]{:S(2)}) copy-start(bf16[8,512,128]{2,1,0:T(8,128)(2,1)S(1)} %get-tuple-element.45.result.own) | copy-start | bytes 3145732
  24.9 1.6 %collective-permute-start.2 = (bf16[1024,128]{1,0:T(8,128)(2,1)S(1)}, bf16[1024,128]{1,0:T(8,128)(2,1)S(1)}, u32[]{:S(2)}, u32[]{:S(2)}) collective-permute-start(bf16[1024,128]{1,0:T(8,128)(2,1)S(1)} %get-tuple-element.42), channel_id=1, source_target_pairs={{0,1},{1,0},{2,3},{3,2},{4,5},{5,4},{6,7},{7,6},{8,9},{9,8},{10,11... | collective-permute-start | bytes 786440 | tf_op jit(solution)/shard_map/ppermute | solution.py:557
  26.5 15.6 %copy-start.5 = (bf16[27,64,64]{2,1,0:T(8,128)(2,1)S(1)}, bf16[27,64,64]{2,1,0:T(8,128)(2,1)}, u32[]{:S(2)}) copy-start(bf16[27,64,64]{2,1,0:T(8,128)(2,1)} %kernel_two.3) | copy-start | bytes 663556
  27.2 14.8 %copy-start.3 = (bf16[27,64,64]{2,1,0:T(8,128)(2,1)S(1)}, bf16[27,64,64]{2,1,0:T(8,128)(2,1)}, u32[]{:S(2)}) copy-start(bf16[27,64,64]{2,1,0:T(8,128)(2,1)} %kernel_one.3) | copy-start | bytes 663556
  27.2 24.7 %all-to-all-start = ((bf16[64,16,128]{2,1,0:T(8,128)(2,1)}), bf16[64,16,128]{2,1,0:T(8,128)(2,1)S(1)}, u32[]{:S(2)}, u32[]{:S(2)}) async-start(bf16[64,16,128]{2,1,0:T(8,128)(2,1)} %bitcast.1), calls=%async_computation | async-start | bytes 524288 | tf_op jit(solution)/shard_map/all_to_all | solution.py:582
  42.1 1.2 %copy-start.9 = (bf16[8,512,128]{2,1,0:T(8,128)(2,1)S(1)}, bf16[8,512,128]{2,1,0:T(8,128)(2,1)}, u32[]{:S(2)}) copy-start(bf16[8,512,128]{2,1,0:T(8,128)(2,1)} %copy-done.8) | copy-start | bytes 3145732
  44.2 14.3 %collective-permute-start.3 = (bf16[4,512,128]{2,1,0:T(8,128)(2,1)S(1)}, bf16[4,512,128]{2,1,0:T(8,128)(2,1)S(1)}, u32[]{:S(2)}, u32[]{:S(2)}) collective-permute-start(bf16[4,512,128]{2,1,0:T(8,128)(2,1)S(1)} %get-tuple-element.49), channel_id=1, source_target_pairs={{0,1},{1,0},{2,3},{3,2},{4,5},{5,4},{6,7},{7,6},{8,9},{9,8},{10,11... | collective-permute-start | bytes 1572872 | tf_op jit(solution)/shard_map/ppermute | solution.py:557
  44.7 13.8 %collective-permute-start.4 = (bf16[4,512,128]{2,1,0:T(8,128)(2,1)S(1)}, bf16[4,512,128]{2,1,0:T(8,128)(2,1)S(1)}, u32[]{:S(2)}, u32[]{:S(2)}) collective-permute-start(bf16[4,512,128]{2,1,0:T(8,128)(2,1)S(1)} %get-tuple-element.50), channel_id=1, source_target_pairs={{1,2},{3,4},{5,6},{7,8},{9,10},{11,12},{13,14},{15,16},{17,18},{19... | collective-permute-start | bytes 1572872 | tf_op jit(solution)/shard_map/ppermute | solution.py:563
  52.7 15.0 %all-to-all-start.1 = ((bf16[64,16,128]{2,1,0:T(8,128)(2,1)}), bf16[64,16,128]{2,1,0:T(8,128)(2,1)S(1)}, u32[]{:S(2)}, u32[]{:S(2)}) async-start(bf16[64,16,128]{2,1,0:T(8,128)(2,1)} %combine.1), calls=%async_computation.1 | async-start | bytes 524288 | tf_op jit(solution)/shard_map/all_to_all | solution.py:582
  58.5 1.2 %copy-start.10 = (bf16[8,512,128]{2,1,0:T(8,128)(2,1)S(1)}, bf16[8,512,128]{2,1,0:T(8,128)(2,1)}, u32[]{:S(2)}) copy-start(bf16[8,512,128]{2,1,0:T(8,128)(2,1)} %copy-done.8) | copy-start | bytes 3145732
  67.7 3.2 %collective-permute-start.5 = (bf16[1024,128]{1,0:T(8,128)(2,1)S(1)}, bf16[1024,128]{1,0:T(8,128)(2,1)S(1)}, u32[]{:S(2)}, u32[]{:S(2)}) collective-permute-start(bf16[1024,128]{1,0:T(8,128)(2,1)S(1)} %bitcast.5), channel_id=1, source_target_pairs={{0,1},{1,0},{2,3},{3,2},{4,5},{5,4},{6,7},{7,6},{8,9},{9,8},{10,11... | collective-permute-start | bytes 786440 | tf_op jit(solution)/shard_map/ppermute | solution.py:557

commit v5 on v4

--- a/solution.py
+++ b/solution.py
@@ -1,3 +1,5 @@
+import functools
+
 import jax
 import jax.numpy as jnp
 from jax import lax
@@ -33,9 +35,9 @@
     return lax.broadcasted_iota(jnp.int32, shape, len(shape) - 1) < CH
 
 
-def choose(position, neighbours, chosen):
-    here = position[0] * SLOTS
-    odd = position[0] % 2
+def choose(index, neighbours, chosen):
+    here = index * SLOTS
+    odd = index % 2
     for r in range(SLOTS):
         chosen[0, r] = 0
         chosen[1, r] = 0
@@ -74,9 +76,11 @@
 
 
 def pack_kernel(
-    position, neighbours, features_far, cotangent_far, occupancy_far,
-    near_send, far_send, features, cotangent, occupancy, chosen, sems,
+    narrow, neighbours_far, features_far, cotangent_far, occupancy_far,
+    near_send, far_send, neighbours, features, cotangent, occupancy, sent, chosen, sems, out_sems,
 ):
+    table = pltpu.make_async_copy(neighbours_far, neighbours, sems.at[5])
+    table.start()
     loads = [pltpu.make_async_copy(occupancy_far, occupancy, sems.at[0])]
     for h in range(2):
         part = pl.ds(h * NEAR, NEAR)
@@ -88,11 +92,13 @@
         )
     for copy in loads:
         copy.start()
-    choose(position, neighbours, chosen)
     voxel = lax.broadcasted_iota(jnp.int32, (1, VOX), 1)
     rank = jnp.where(surface(voxel), rim_rank(voxel), -1)
     wanted = lax.broadcasted_iota(jnp.int32, (RIM, VOX), 0)
     select = jnp.where(rank == wanted, 1.0, 0.0).astype(BF16)
+    table.wait()
+    choose(lax.axis_index("wide") * narrow + lax.axis_index("narrow"), neighbours, chosen)
+    stores = []
     for copy in loads:
         copy.wait()
     for side, target in ((1, far_send), (0, near_send)):
@@ -110,28 +116,40 @@
                 preferred_element_type=F32,
             )
             for q in range(2):
-                target[r + q] = both[:, q * LANES : (q + 1) * LANES].astype(BF16)
-
-
-def pack(position, neighbours, features, cotangent, occupancy):
-    return pl.pallas_call(
-        pack_kernel,
+                sent[side, r + q] = both[:, q * LANES : (q + 1) * LANES].astype(BF16)
+            pair = pl.ds(r, 2)
+            stores.append(
+                pltpu.make_async_copy(
+                    sent.at[side, pair], target.at[pair], out_sems.at[side, r // 2]
+                )
+            )
+            stores[-1].start()
+    for copy in stores:
+        copy.wait()
+
+
+def pack(narrow, neighbours, features, cotangent, occupancy):
+    return pl.pallas_call(
+        functools.partial(pack_kernel, narrow),
         out_shape=(
             jax.ShapeDtypeStruct((NEAR, RIM, LANES), BF16),
             jax.ShapeDtypeStruct((NEAR, RIM, LANES), BF16),
         ),
-        in_specs=[whole_smem, whole_smem, anywhere, anywhere, anywhere],
-        out_specs=(whole_vmem, whole_vmem),
+        in_specs=[anywhere] * 4,
+        out_specs=(anywhere, anywhere),
         scratch_shapes=[
+            pltpu.SMEM((SLOTS, 26), jnp.int32),
             pltpu.VMEM((SLOTS, CH, VOX), BF16),
             pltpu.VMEM((SLOTS, CH, VOX), BF16),
             pltpu.VMEM((SLOTS, VOX), jnp.int32),
+            pltpu.VMEM((2, NEAR, RIM, LANES), BF16),
             pltpu.SMEM((2, SLOTS), jnp.int32),
-            pltpu.SemaphoreType.DMA((5,)),
+            pltpu.SemaphoreType.DMA((6,)),
+            pltpu.SemaphoreType.DMA((2, 2)),
         ],
         compiler_params=pltpu.CompilerParams(vmem_limit_bytes=60 * 1024 * 1024),
         name="pack",
-    )(position, neighbours, features, cotangent, occupancy)
+    )(neighbours, features, cotangent, occupancy)
 
 
 def weight_block(kernel, flip, a, rows, columns):
@@ -171,7 +189,7 @@
     weight_field(kernel_two, True, 1, first)
     for b in range(SLOTS):
         fields[b] = side_by_side(features, cotangent, occupancy, b)
-    choose(position, neighbours, chosen)
+    choose(position[0], neighbours, chosen)
     voxel = lax.broadcasted_iota(jnp.int32, (VOX, LANES), 0)
     rank = jnp.where(surface(voxel), rim_rank(voxel), -1)
     for first_lane in range(0, RIM, LANES):
@@ -513,7 +531,10 @@
     )(blocks)
 
 
-def unpack_kernel(scale, position, own, other, grad_one, grad_two, sums):
+def unpack_kernel(
+    scale, position, own, other, one_far, two_far, sums, grad_one, grad_two, sems
+):
+    stores = []
     odd = position[0] % 2
     sums[pl.ds(pl.multiple_of(odd * HALF, HALF), HALF), :] = own[...]
     sums[pl.ds(pl.multiple_of((1 - odd) * HALF, HALF), HALF), :] = other[...]
@@ -533,6 +554,16 @@
             grad_two[26 - n] = two[:CH]
             grad_two[25 - n] = two[CH:]
             grad_two[24 - n] = last.T[CH:]
+        for which, (source, target, first) in enumerate(
+            ((grad_one, one_far, 9 * a), (grad_two, two_far, 18 - 9 * a))
+        ):
+            rows = pl.ds(first, 9)
+            stores.append(
+                pltpu.make_async_copy(source.at[rows], target.at[rows], sems.at[which, a])
+            )
+            stores[-1].start()
+    for copy in stores:
+        copy.wait()
 
 
 def unpack(scale, position, own, other):
@@ -546,8 +577,13 @@
             jax.ShapeDtypeStruct((27, CH, CH), F32),
         ),
         in_specs=[whole_smem, whole_vmem, whole_vmem],
-        out_specs=(whole_vmem,) * 2,
-        scratch_shapes=[pltpu.VMEM((TERMS, LANES), BF16)],
+        out_specs=(anywhere, anywhere),
+        scratch_shapes=[
+            pltpu.VMEM((TERMS, LANES), BF16),
+            pltpu.VMEM((27, CH, CH), F32),
+            pltpu.VMEM((27, CH, CH), F32),
+            pltpu.SemaphoreType.DMA((2, 3)),
+        ],
         compiler_params=pltpu.CompilerParams(vmem_limit_bytes=VMEM),
         name="unpack",
     )(position, own, other)
@@ -563,9 +599,9 @@
     return lax.ppermute(rows, AXES, route)
 
 
-def local(devices, features, kernel_one, kernel_two, cotangent, neighbours, occupancy):
+def local(devices, narrow, features, kernel_one, kernel_two, cotangent, neighbours, occupancy):
     position = lax.axis_index(AXES).astype(jnp.int32).reshape(1)
-    near_send, far_send = pack(position, neighbours, features, cotangent, occupancy)
+    near_send, far_send = pack(narrow, neighbours, features, cotangent, occupancy)
     near_send, far_send, later = lax.optimization_barrier((near_send, far_send, position))
     far = far_swap(far_send, devices)
     near = near_swap(near_send, devices)
@@ -605,7 +641,7 @@
     out_specs = (bricks, bricks, P(), P())
 
     def run(*arrays):
-        return local(devices, *arrays)
+        return local(devices, mesh.shape["narrow"], *arrays)
 
     return jax.shard_map(
         run, mesh=mesh, in_specs=in_specs, out_specs=out_specs, check_vma=False

time: 73.1 us -> 72.5 us (level)
  transfers between devices with their start and end apart: 8 -> 8, of which waited for: 4 -> 4; matrix products, arithmetic and copies ran while one was open for 0% -> 0% of each run, Pallas kernels for 17% -> 18%
where the time goes in v5:
time: 72.5 us; the launch traced here: 72.1 us
  starting transfers between devices  31.4 us (43%)
  Pallas kernels  28.1 us (39%)
  waiting for transfers between devices  7.12 us (10%)
  local copies, waits for them, and re-layouts  4.49 us (6%)
  between operations  1.04 us (1%)
    all_to_all x2, starting transfers between devices, to_all(): return lax.all_to_all(rows, AXES, 0, 0, axis_index_groups=cores, tiled=True)  20.6 us
    pallas_call x1, Pallas kernels, first_stage(): pl.pallas_call(first_kernel, out_shape=(jax.ShapeDtypeStruct((SLOTS, VOX,...  10.3 us
    pallas_call x1, Pallas kernels, second_stage(): pl.pallas_call(second_kernel, out_shape=(jax.ShapeDtypeStruct((SLOTS, CH,...  7.58 us
    ppermute x2, starting transfers between devices, far_swap(): return lax.ppermute(rows, AXES, route)  6.63 us
    unnamed x22, local copies, waits for them, and re-layouts  4.49 us
    all_to_all x2, waiting for transfers between devices, to_all(): return lax.all_to_all(rows, AXES, 0, 0, axis_index_groups=cores, tiled=True)  4.43 us
    ppermute x4, starting transfers between devices, near_swap(): return lax.ppermute(rows, AXES, [(k, k ^ 1) for k in range(devices)])  4.15 us
    pallas_call x1, Pallas kernels, prepare(): pl.pallas_call(prepare_kernel, out_shape=(jax.ShapeDtypeStruct((2, 3, 2 *...  3.38 us
  transfers between devices with their start and end apart: 8, of which 4 were waited for; matrix products, arithmetic and copies ran while one was open for 0% of the time, Pallas kernels for 18%

profile of v5, /device:TPU:1, one launch (start us, length us, event | category | flops | bytes accessed | tf_op | source)
XLA Modules:
  0.0 72.1 jit_solution(17798962437888938268)
XLA Ops:
  0.6 0.0 copy-start
  0.6 0.0 copy-start.1
  0.7 0.0 copy-start.6
  0.7 2.6 %pack.1 = (bf16[4,304,128]{2,1,0:T(8,128)(2,1)}, bf16[4,304,128]{2,1,0:T(8,128)(2,1)}) custom-call(s32[8,26]{1,0:T(8,128)} %neighbours.1, bf16[8,64,512]{2,1,0:T(8,128)(2,1)} %features.1, bf16[8,64,512]{2,1,0:T(8,128)(2,1)} %cotangent.1, s32[8,512]{1,0:T(8,128)} %occupancy.5), custom_call_target="tpu_custom_call" | custom-call | tf_op jit(solution)/shard_map/pack/pallas_call | solution.py:132
  3.3 0.0 copy-start.7
  3.3 1.5 %collective-permute-start = (bf16[4,304,128]{2,1,0:T(8,128)(2,1)}, bf16[4,304,128]{2,1,0:T(8,128)(2,1)S(1)}, u32[]{:S(2)}, u32[]{:S(2)}) collective-permute-start(bf16[4,304,128]{2,1,0:T(8,128)(2,1)} %get-tuple-element.38), channel_id=1, source_target_pairs={{0,1},{1,0},{2,3},{3,2},{4,5},{5,4},{6,7},{7,6},{8,9},{9,8},{10,11... | collective-permute-start | bytes 933896 | tf_op jit(solution)/shard_map/ppermute | solution.py:593
  4.8 3.5 %collective-permute-start.1 = (bf16[4,304,128]{2,1,0:T(8,128)(2,1)}, bf16[4,304,128]{2,1,0:T(8,128)(2,1)S(1)}, u32[]{:S(2)}, u32[]{:S(2)}) collective-permute-start(bf16[4,304,128]{2,1,0:T(8,128)(2,1)} %get-tuple-element.39), channel_id=1, source_target_pairs={{1,2},{3,4},{5,6},{7,8},{9,10},{11,12},{13,14},{15,16},{17,18},{19... | collective-permute-start | bytes 933896 | tf_op jit(solution)/shard_map/ppermute | solution.py:599
  8.4 0.0 copy-done
  8.4 0.0 copy-done.1
  8.4 0.0 copy-done.6
  8.4 0.0 copy-done.7
  8.4 0.0 copy-start.2
  8.4 1.0 %copy-done.2 = bf16[27,64,64]{2,1,0:T(8,128)(2,1)S(1)} copy-done((bf16[27,64,64]{2,1,0:T(8,128)(2,1)S(1)}, bf16[27,64,64]{2,1,0:T(8,128)(2,1)}, u32[]{:S(2)}) %copy-start.2) | copy-done | bytes 221208
  9.4 0.0 copy-start.4
  9.4 1.0 %copy-done.4 = bf16[27,64,64]{2,1,0:T(8,128)(2,1)S(1)} copy-done((bf16[27,64,64]{2,1,0:T(8,128)(2,1)S(1)}, bf16[27,64,64]{2,1,0:T(8,128)(2,1)}, u32[]{:S(2)}) %copy-start.4) | copy-done | bytes 221208
  10.4 3.4 %prepare.1 = (bf16[2,3,256,256]{3,2,1,0:T(8,128)(2,1)S(1)}, s32[216]{0:T(256)S(1)}, s32[2,8]{1,0:T(2,128)S(1)}, bf16[8,512,128]{2,1,0:T(8,128)(2,1)S(1)}, bf16[512,304]{1,0:T(8,128)(2,1)S(1)}) custom-call(s32[1]{0:T(128)} %bitcast.position.after.refs_0_, s32[8,26]{1,0:T(8,128)S(1)} %copy-done.7, bf16[27,64,64]{2,1,0:T(8,128)(2,1)S(1)} %copy-done.2, ...), custom_call_target="tpu_custom_call" | custom-call | flops 4000000 | bytes 4000000 | tf_op jit(solution)/shard_map/prepare/pallas_call | solution.py:226
  13.8 0.0 collective-permute-done.near
  13.8 0.0 collective-permute-done.1.far
  13.8 10.3 %first_stage.1 = (bf16[8,512,128]{2,1,0:T(8,128)(2,1)S(1)}, bf16[1024,128]{1,0:T(8,128)(2,1)S(1)}, f32[1024,128]{1,0:T(8,128)S(1)}) custom-call(s32[216]{0:T(256)S(1)} %get-tuple-element.34.lookup, s32[2,8]{1,0:T(2,128)S(1)} %get-tuple-element.35.chosen, s32[8,512]{1,0:T(8,128)S(1)} %copy-done.6, bf16[2,3,256,256]{3,2,1,0:T(8,128)(2,1)S(1)} %get-tuple-element.36.weights, ...), custom_call_target="tpu_custom_call" | custom-call | flops 8000000000 | bytes 6000000 | tf_op jit(solution)/shard_map/first_stage/pallas_call | solution.py:433
  24.1 0.0 copy-start.8
  24.1 0.1 collective-permute-start.2
  24.2 1.5 %collective-permute-done.2.received = bf16[1024,128]{1,0:T(8,128)(2,1)S(1)} collective-permute-done((bf16[1024,128]{1,0:T(8,128)(2,1)S(1)}, bf16[1024,128]{1,0:T(8,128)(2,1)S(1)}, u32[]{:S(2)}, u32[]{:S(2)}) %collective-permute-start.2) | collective-permute-done | bytes 262176 | tf_op jit(solution)/shard_map/ppermute | solution.py:593
  25.7 0.0 copy-start.5
  25.7 0.8 %pair_sum.1 = bf16[1024,128]{1,0:T(8,128)(2,1)} custom-call(f32[1024,128]{1,0:T(8,128)S(1)} %get-tuple-element.41.kept, bf16[1024,128]{1,0:T(8,128)(2,1)S(1)} %collective-permute-done.2.received), custom_call_target="tpu_custom_call" | custom-call | tf_op jit(solution)/shard_map/pair_sum/pallas_call | solution.py:502
  26.5 0.0 copy-start.3
  26.5 14.8 %all-to-all-start = ((bf16[64,16,128]{2,1,0:T(8,128)(2,1)}), bf16[64,16,128]{2,1,0:T(8,128)(2,1)S(1)}, u32[]{:S(2)}, u32[]{:S(2)}) async-start(bf16[64,16,128]{2,1,0:T(8,128)(2,1)} %bitcast.1), calls=%async_computation | async-start | bytes 524288 | tf_op jit(solution)/shard_map/all_to_all | solution.py:618
  41.3 0.0 copy-done.8
  41.3 0.0 copy-done.5
  41.3 0.0 copy-done.3
  41.3 0.0 copy-start.9
  41.3 1.2 %copy-done.9 = bf16[8,512,128]{2,1,0:T(8,128)(2,1)S(1)} copy-done((bf16[8,512,128]{2,1,0:T(8,128)(2,1)S(1)}, bf16[8,512,128]{2,1,0:T(8,128)(2,1)}, u32[]{:S(2)}) %copy-start.9) | copy-done | bytes 1048600
  42.6 0.9 %relay.1 = (bf16[2,3,256,256]{3,2,1,0:T(8,128)(2,1)S(1)}, bf16[4,512,128]{2,1,0:T(8,128)(2,1)S(1)}, bf16[4,512,128]{2,1,0:T(8,128)(2,1)S(1)}) custom-call(s32[1]{0:T(128)} %bitcast.position.after.refs_0_, s32[2,8]{1,0:T(2,128)S(1)} %get-tuple-element.35.chosen, bf16[27,64,64]{2,1,0:T(8,128)(2,1)S(1)} %copy-done.3, bf16[27,64,64]{2,1,0:T(8,128)(2,1)S(1)} %copy-done.5, ...), custom_call_target="tpu_custom_call" | custom-call | flops 5000000000 | bytes 2000000 | tf_op jit(solution)/shard_map/relay/pallas_call | solution.py:255
  43.5 0.5 collective-permute-start.3
  44.0 3.1 %collective-permute-start.4 = (bf16[4,512,128]{2,1,0:T(8,128)(2,1)S(1)}, bf16[4,512,128]{2,1,0:T(8,128)(2,1)S(1)}, u32[]{:S(2)}, u32[]{:S(2)}) collective-permute-start(bf16[4,512,128]{2,1,0:T(8,128)(2,1)S(1)} %get-tuple-element.50), channel_id=1, source_target_pairs={{1,2},{3,4},{5,6},{7,8},{9,10},{11,12},{13,14},{15,16},{17,18},{19... | collective-permute-start | bytes 1572872 | tf_op jit(solution)/shard_map/ppermute | solution.py:599
  47.1 4.1 %all-to-all-done = bf16[64,16,128]{2,1,0:T(8,128)(2,1)S(1)} async-done(((bf16[64,16,128]{2,1,0:T(8,128)(2,1)}), bf16[64,16,128]{2,1,0:T(8,128)(2,1)S(1)}, u32[]{:S(2)}, u32[]{:S(2)}) %all-to-all-start) | async-done | bytes 262176 | tf_op jit(solution)/shard_map/all_to_all | solution.py:618
  51.2 0.8 %combine.1 = bf16[64,16,128]{2,1,0:T(8,128)(2,1)} custom-call(bf16[64,16,128]{2,1,0:T(8,128)(2,1)S(1)} %all-to-all-done), custom_call_target="tpu_custom_call" | custom-call | flops 20000000000 | bytes 1000000 | tf_op jit(solution)/shard_map/combine/pallas_call | solution.py:521
  52.0 5.8 %all-to-all-start.1 = ((bf16[64,16,128]{2,1,0:T(8,128)(2,1)}), bf16[64,16,128]{2,1,0:T(8,128)(2,1)S(1)}, u32[]{:S(2)}, u32[]{:S(2)}) async-start(bf16[64,16,128]{2,1,0:T(8,128)(2,1)} %combine.1), calls=%async_computation.1 | async-start | bytes 524288 | tf_op jit(solution)/shard_map/all_to_all | solution.py:618
  57.8 0.0 collective-permute-done.3.before
  57.8 0.0 collective-permute-done.4.after
  57.8 0.0 copy-start.10
  57.8 1.2 %copy-done.10 = bf16[8,512,128]{2,1,0:T(8,128)(2,1)S(1)} copy-done((bf16[8,512,128]{2,1,0:T(8,128)(2,1)S(1)}, bf16[8,512,128]{2,1,0:T(8,128)(2,1)}, u32[]{:S(2)}) %copy-start.10) | copy-done | bytes 1048600
  59.0 7.6 %second_stage.1 = (bf16[8,64,512]{2,1,0:T(8,128)(2,1)}, bf16[8,64,512]{2,1,0:T(8,128)(2,1)}) custom-call(s32[216]{0:T(256)S(1)} %get-tuple-element.34.lookup, s32[8,512]{1,0:T(8,128)S(1)} %copy-done.6, bf16[2,3,256,256]{3,2,1,0:T(8,128)(2,1)S(1)} %get-tuple-element.48.weights, bf16[8,512,128]{2,1,0:T(8,128)(2,1)S(1)} %copy-done.10, ...), custom_call_target="tpu_custom_call" | custom-call | flops 8000000000 | bytes 6000000 | tf_op jit(solution)/shard_map/second_stage/pallas_call | solution.py:476
  66.6 0.4 all-to-all-done.1
  67.0 2.1 %collective-permute-start.5 = (bf16[1024,128]{1,0:T(8,128)(2,1)S(1)}, bf16[1024,128]{1,0:T(8,128)(2,1)S(1)}, u32[]{:S(2)}, u32[]{:S(2)}) collective-permute-start(bf16[1024,128]{1,0:T(8,128)(2,1)S(1)} %bitcast.5), channel_id=1, source_target_pairs={{0,1},{1,0},{2,3},{3,2},{4,5},{5,4},{6,7},{7,6},{8,9},{9,8},{10,11... | collective-permute-start | bytes 786440 | tf_op jit(solution)/shard_map/ppermute | solution.py:593
  69.0 1.2 %collective-permute-done.5.refs_2_ = bf16[1024,128]{1,0:T(8,128)(2,1)S(1)} collective-permute-done((bf16[1024,128]{1,0:T(8,128)(2,1)S(1)}, bf16[1024,128]{1,0:T(8,128)(2,1)S(1)}, u32[]{:S(2)}, u32[]{:S(2)}) %collective-permute-start.5) | collective-permute-done | bytes 262176 | tf_op jit(solution)/shard_map/ppermute | solution.py:593
  70.2 1.7 %unpack.1 = (f32[27,64,64]{2,1,0:T(8,128)}, f32[27,64,64]{2,1,0:T(8,128)}) custom-call(s32[1]{0:T(128)} %bitcast.position.after.refs_0_, bf16[1024,128]{1,0:T(8,128)(2,1)S(1)} %bitcast.6, bf16[1024,128]{1,0:T(8,128)(2,1)S(1)} %collective-permute-done.5.refs_2_), custom_call_target="tpu_custom_call" | custom-call | tf_op jit(solution)/shard_map/unpack/pallas_call | solution.py:573
Async XLA Ops:
  0.6 7.7 %copy-start = (bf16[8,64,512]{2,1,0:T(8,128)(2,1)S(1)}, bf16[8,64,512]{2,1,0:T(8,128)(2,1)}, u32[]{:S(2)}) copy-start(bf16[8,64,512]{2,1,0:T(8,128)(2,1)} %features.1) | copy-start | bytes 1572868
  0.6 7.7 %copy-start.1 = (bf16[8,64,512]{2,1,0:T(8,128)(2,1)S(1)}, bf16[8,64,512]{2,1,0:T(8,128)(2,1)}, u32[]{:S(2)}) copy-start(bf16[8,64,512]{2,1,0:T(8,128)(2,1)} %cotangent.1) | copy-start | bytes 1572868
  0.7 7.7 %copy-start.6 = (s32[8,512]{1,0:T(8,128)S(1)}, s32[8,512]{1,0:T(8,128)}, u32[]{:S(2)}) copy-start(s32[8,512]{1,0:T(8,128)} %occupancy.5) | copy-start | bytes 49156
  3.3 5.1 %copy-start.7 = (s32[8,26]{1,0:T(8,128)S(1)}, s32[8,26]{1,0:T(8,128)}, u32[]{:S(2)}) copy-start(s32[8,26]{1,0:T(8,128)} %neighbours.1) | copy-start | bytes 2500
  3.3 10.5 %collective-permute-start = (bf16[4,304,128]{2,1,0:T(8,128)(2,1)}, bf16[4,304,128]{2,1,0:T(8,128)(2,1)S(1)}, u32[]{:S(2)}, u32[]{:S(2)}) collective-permute-start(bf16[4,304,128]{2,1,0:T(8,128)(2,1)} %get-tuple-element.38), channel_id=1, source_target_pairs={{0,1},{1,0},{2,3},{3,2},{4,5},{5,4},{6,7},{7,6},{8,9},{9,8},{10,11... | collective-permute-start | bytes 933896 | tf_op jit(solution)/shard_map/ppermute | solution.py:593
  4.8 9.0 %collective-permute-start.1 = (bf16[4,304,128]{2,1,0:T(8,128)(2,1)}, bf16[4,304,128]{2,1,0:T(8,128)(2,1)S(1)}, u32[]{:S(2)}, u32[]{:S(2)}) collective-permute-start(bf16[4,304,128]{2,1,0:T(8,128)(2,1)} %get-tuple-element.39), channel_id=1, source_target_pairs={{1,2},{3,4},{5,6},{7,8},{9,10},{11,12},{13,14},{15,16},{17,18},{19... | collective-permute-start | bytes 933896 | tf_op jit(solution)/shard_map/ppermute | solution.py:599
  8.4 1.0 %copy-start.2 = (bf16[27,64,64]{2,1,0:T(8,128)(2,1)S(1)}, bf16[27,64,64]{2,1,0:T(8,128)(2,1)}, u32[]{:S(2)}) copy-start(bf16[27,64,64]{2,1,0:T(8,128)(2,1)} %kernel_one.3) | copy-start | bytes 663556
  9.4 1.0 %copy-start.4 = (bf16[27,64,64]{2,1,0:T(8,128)(2,1)S(1)}, bf16[27,64,64]{2,1,0:T(8,128)(2,1)}, u32[]{:S(2)}) copy-start(bf16[27,64,64]{2,1,0:T(8,128)(2,1)} %kernel_two.3) | copy-start | bytes 663556
  24.1 17.2 %copy-start.8 = (bf16[8,512,128]{2,1,0:T(8,128)(2,1)}, bf16[8,512,128]{2,1,0:T(8,128)(2,1)S(1)}, u32[]{:S(2)}) copy-start(bf16[8,512,128]{2,1,0:T(8,128)(2,1)S(1)} %get-tuple-element.45.result.own) | copy-start | bytes 3145732
  24.1 1.6 %collective-permute-start.2 = (bf16[1024,128]{1,0:T(8,128)(2,1)S(1)}, bf16[1024,128]{1,0:T(8,128)(2,1)S(1)}, u32[]{:S(2)}, u32[]{:S(2)}) collective-permute-start(bf16[1024,128]{1,0:T(8,128)(2,1)S(1)} %get-tuple-element.42), channel_id=1, source_target_pairs={{0,1},{1,0},{2,3},{3,2},{4,5},{5,4},{6,7},{7,6},{8,9},{9,8},{10,11... | collective-permute-start | bytes 786440 | tf_op jit(solution)/shard_map/ppermute | solution.py:593
  25.7 15.6 %copy-start.5 = (bf16[27,64,64]{2,1,0:T(8,128)(2,1)S(1)}, bf16[27,64,64]{2,1,0:T(8,128)(2,1)}, u32[]{:S(2)}) copy-start(bf16[27,64,64]{2,1,0:T(8,128)(2,1)} %kernel_two.3) | copy-start | bytes 663556
  26.5 14.8 %copy-start.3 = (bf16[27,64,64]{2,1,0:T(8,128)(2,1)S(1)}, bf16[27,64,64]{2,1,0:T(8,128)(2,1)}, u32[]{:S(2)}) copy-start(bf16[27,64,64]{2,1,0:T(8,128)(2,1)} %kernel_one.3) | copy-start | bytes 663556
  26.5 24.7 %all-to-all-start = ((bf16[64,16,128]{2,1,0:T(8,128)(2,1)}), bf16[64,16,128]{2,1,0:T(8,128)(2,1)S(1)}, u32[]{:S(2)}, u32[]{:S(2)}) async-start(bf16[64,16,128]{2,1,0:T(8,128)(2,1)} %bitcast.1), calls=%async_computation | async-start | bytes 524288 | tf_op jit(solution)/shard_map/all_to_all | solution.py:618
  41.3 1.2 %copy-start.9 = (bf16[8,512,128]{2,1,0:T(8,128)(2,1)S(1)}, bf16[8,512,128]{2,1,0:T(8,128)(2,1)}, u32[]{:S(2)}) copy-start(bf16[8,512,128]{2,1,0:T(8,128)(2,1)} %copy-done.8) | copy-start | bytes 3145732
  43.5 14.3 %collective-permute-start.3 = (bf16[4,512,128]{2,1,0:T(8,128)(2,1)S(1)}, bf16[4,512,128]{2,1,0:T(8,128)(2,1)S(1)}, u32[]{:S(2)}, u32[]{:S(2)}) collective-permute-start(bf16[4,512,128]{2,1,0:T(8,128)(2,1)S(1)} %get-tuple-element.49), channel_id=1, source_target_pairs={{0,1},{1,0},{2,3},{3,2},{4,5},{5,4},{6,7},{7,6},{8,9},{9,8},{10,11... | collective-permute-start | bytes 1572872 | tf_op jit(solution)/shard_map/ppermute | solution.py:593
  44.0 13.8 %collective-permute-start.4 = (bf16[4,512,128]{2,1,0:T(8,128)(2,1)S(1)}, bf16[4,512,128]{2,1,0:T(8,128)(2,1)S(1)}, u32[]{:S(2)}, u32[]{:S(2)}) collective-permute-start(bf16[4,512,128]{2,1,0:T(8,128)(2,1)S(1)} %get-tuple-element.50), channel_id=1, source_target_pairs={{1,2},{3,4},{5,6},{7,8},{9,10},{11,12},{13,14},{15,16},{17,18},{19... | collective-permute-start | bytes 1572872 | tf_op jit(solution)/shard_map/ppermute | solution.py:599
  52.0 15.0 %all-to-all-start.1 = ((bf16[64,16,128]{2,1,0:T(8,128)(2,1)}), bf16[64,16,128]{2,1,0:T(8,128)(2,1)S(1)}, u32[]{:S(2)}, u32[]{:S(2)}) async-start(bf16[64,16,128]{2,1,0:T(8,128)(2,1)} %combine.1), calls=%async_computation.1 | async-start | bytes 524288 | tf_op jit(solution)/shard_map/all_to_all | solution.py:618
  57.8 1.2 %copy-start.10 = (bf16[8,512,128]{2,1,0:T(8,128)(2,1)S(1)}, bf16[8,512,128]{2,1,0:T(8,128)(2,1)}, u32[]{:S(2)}) copy-start(bf16[8,512,128]{2,1,0:T(8,128)(2,1)} %copy-done.8) | copy-start | bytes 3145732
  67.0 3.2 %collective-permute-start.5 = (bf16[1024,128]{1,0:T(8,128)(2,1)S(1)}, bf16[1024,128]{1,0:T(8,128)(2,1)S(1)}, u32[]{:S(2)}, u32[]{:S(2)}) collective-permute-start(bf16[1024,128]{1,0:T(8,128)(2,1)S(1)} %bitcast.5), channel_id=1, source_target_pairs={{0,1},{1,0},{2,3},{3,2},{4,5},{5,4},{6,7},{7,6},{8,9},{9,8},{10,11... | collective-permute-start | bytes 786440 | tf_op jit(solution)/shard_map/ppermute | solution.py:593

commit v6 on v5

--- a/solution.py
+++ b/solution.py
@@ -532,10 +532,10 @@
 
 
 def unpack_kernel(
-    scale, position, own, other, one_far, two_far, sums, grad_one, grad_two, sems
+    scale, narrow, own, other, one_far, two_far, sums, grad_one, grad_two, sems
 ):
     stores = []
-    odd = position[0] % 2
+    odd = (lax.axis_index("wide") * narrow + lax.axis_index("narrow")) % 2
     sums[pl.ds(pl.multiple_of(odd * HALF, HALF), HALF), :] = own[...]
     sums[pl.ds(pl.multiple_of((1 - odd) * HALF, HALF), HALF), :] = other[...]
     part = 3 * CH
@@ -566,9 +566,9 @@
         copy.wait()
 
 
-def unpack(scale, position, own, other):
+def unpack(scale, narrow, own, other):
     def kernel(*refs):
-        unpack_kernel(scale, *refs)
+        unpack_kernel(scale, narrow, *refs)
 
     return pl.pallas_call(
         kernel,
@@ -576,7 +576,7 @@
             jax.ShapeDtypeStruct((27, CH, CH), F32),
             jax.ShapeDtypeStruct((27, CH, CH), F32),
         ),
-        in_specs=[whole_smem, whole_vmem, whole_vmem],
+        in_specs=[whole_vmem, whole_vmem],
         out_specs=(anywhere, anywhere),
         scratch_shapes=[
             pltpu.VMEM((TERMS, LANES), BF16),
@@ -586,7 +586,7 @@
         ],
         compiler_params=pltpu.CompilerParams(vmem_limit_bytes=VMEM),
         name="unpack",
-    )(position, own, other)
+    )(own, other)
 
 
 def near_swap(rows, devices):
@@ -630,7 +630,7 @@
     own, output, grad_in = lax.optimization_barrier((own, output, grad_in))
     other = near_swap(own, devices)
     scale = float((SLOTS * VOX * devices) ** -0.5)
-    grad_one, grad_two = unpack(scale, position, own, other)
+    grad_one, grad_two = unpack(scale, narrow, own, other)
     return output, grad_in, grad_one, grad_two
 
 

time: 72.5 us -> 72.5 us (level)
  no operation moved by 1% of the time
where the time goes in v6:
time: 72.5 us; the launch traced here: 72 us
  starting transfers between devices  31.3 us (43%)
  Pallas kernels  28.1 us (39%)
  waiting for transfers between devices  7.13 us (10%)
  local copies, waits for them, and re-layouts  4.49 us (6%)
  between operations  1.03 us (1%)
    all_to_all x2, starting transfers between devices, to_all(): return lax.all_to_all(rows, AXES, 0, 0, axis_index_groups=cores, tiled=True)  20.6 us
    pallas_call x1, Pallas kernels, first_stage(): pl.pallas_call(first_kernel, out_shape=(jax.ShapeDtypeStruct((SLOTS, VOX,...  10.2 us
    pallas_call x1, Pallas kernels, second_stage(): pl.pallas_call(second_kernel, out_shape=(jax.ShapeDtypeStruct((SLOTS, CH,...  7.58 us
    ppermute x2, starting transfers between devices, far_swap(): return lax.ppermute(rows, AXES, route)  6.63 us
    unnamed x22, local copies, waits for them, and re-layouts  4.49 us
    all_to_all x2, waiting for transfers between devices, to_all(): return lax.all_to_all(rows, AXES, 0, 0, axis_index_groups=cores, tiled=True)  4.43 us
    ppermute x4, starting transfers between devices, near_swap(): return lax.ppermute(rows, AXES, [(k, k ^ 1) for k in range(devices)])  4.16 us
    pallas_call x1, Pallas kernels, prepare(): pl.pallas_call(prepare_kernel, out_shape=(jax.ShapeDtypeStruct((2, 3, 2 *...  3.38 us
  transfers between devices with their start and end apart: 8, of which 4 were waited for; matrix products, arithmetic and copies ran while one was open for 0% of the time, Pallas kernels for 18%

profile of v6, /device:TPU:1, one launch (start us, length us, event | category | flops | bytes accessed | tf_op | source)
XLA Modules:
  0.0 72.0 jit_solution(2256357213312735909)
XLA Ops:
  0.6 0.0 copy-start
  0.6 0.0 copy-start.1
  0.7 0.0 copy-start.6
  0.7 2.6 %pack.1 = (bf16[4,304,128]{2,1,0:T(8,128)(2,1)}, bf16[4,304,128]{2,1,0:T(8,128)(2,1)}) custom-call(s32[8,26]{1,0:T(8,128)} %neighbours.1, bf16[8,64,512]{2,1,0:T(8,128)(2,1)} %features.1, bf16[8,64,512]{2,1,0:T(8,128)(2,1)} %cotangent.1, s32[8,512]{1,0:T(8,128)} %occupancy.5), custom_call_target="tpu_custom_call" | custom-call | tf_op jit(solution)/shard_map/pack/pallas_call | solution.py:132
  3.3 0.0 copy-start.7
  3.3 1.5 %collective-permute-start = (bf16[4,304,128]{2,1,0:T(8,128)(2,1)}, bf16[4,304,128]{2,1,0:T(8,128)(2,1)S(1)}, u32[]{:S(2)}, u32[]{:S(2)}) collective-permute-start(bf16[4,304,128]{2,1,0:T(8,128)(2,1)} %get-tuple-element.38), channel_id=1, source_target_pairs={{0,1},{1,0},{2,3},{3,2},{4,5},{5,4},{6,7},{7,6},{8,9},{9,8},{10,11... | collective-permute-start | bytes 933896 | tf_op jit(solution)/shard_map/ppermute | solution.py:593
  4.8 3.5 %collective-permute-start.1 = (bf16[4,304,128]{2,1,0:T(8,128)(2,1)}, bf16[4,304,128]{2,1,0:T(8,128)(2,1)S(1)}, u32[]{:S(2)}, u32[]{:S(2)}) collective-permute-start(bf16[4,304,128]{2,1,0:T(8,128)(2,1)} %get-tuple-element.39), channel_id=1, source_target_pairs={{1,2},{3,4},{5,6},{7,8},{9,10},{11,12},{13,14},{15,16},{17,18},{19... | collective-permute-start | bytes 933896 | tf_op jit(solution)/shard_map/ppermute | solution.py:599
  8.4 0.0 copy-done
  8.4 0.0 copy-done.1
  8.4 0.0 copy-done.6
  8.4 0.0 copy-done.7
  8.4 0.0 copy-start.2
  8.4 1.0 %copy-done.2 = bf16[27,64,64]{2,1,0:T(8,128)(2,1)S(1)} copy-done((bf16[27,64,64]{2,1,0:T(8,128)(2,1)S(1)}, bf16[27,64,64]{2,1,0:T(8,128)(2,1)}, u32[]{:S(2)}) %copy-start.2) | copy-done | bytes 221208
  9.4 0.0 copy-start.4
  9.4 1.0 %copy-done.4 = bf16[27,64,64]{2,1,0:T(8,128)(2,1)S(1)} copy-done((bf16[27,64,64]{2,1,0:T(8,128)(2,1)S(1)}, bf16[27,64,64]{2,1,0:T(8,128)(2,1)}, u32[]{:S(2)}) %copy-start.4) | copy-done | bytes 221208
  10.4 3.4 %prepare.1 = (bf16[2,3,256,256]{3,2,1,0:T(8,128)(2,1)S(1)}, s32[216]{0:T(256)S(1)}, s32[2,8]{1,0:T(2,128)S(1)}, bf16[8,512,128]{2,1,0:T(8,128)(2,1)S(1)}, bf16[512,304]{1,0:T(8,128)(2,1)S(1)}) custom-call(s32[1]{0:T(128)} %bitcast.position.after, s32[8,26]{1,0:T(8,128)S(1)} %copy-done.7, bf16[27,64,64]{2,1,0:T(8,128)(2,1)S(1)} %copy-done.2, ...), custom_call_target="tpu_custom_call" | custom-call | flops 4000000 | bytes 4000000 | tf_op jit(solution)/shard_map/prepare/pallas_call | solution.py:226
  13.8 0.0 collective-permute-done.near
  13.8 0.0 collective-permute-done.1.far
  13.8 10.2 %first_stage.1 = (bf16[8,512,128]{2,1,0:T(8,128)(2,1)S(1)}, bf16[1024,128]{1,0:T(8,128)(2,1)S(1)}, f32[1024,128]{1,0:T(8,128)S(1)}) custom-call(s32[216]{0:T(256)S(1)} %get-tuple-element.34.lookup, s32[2,8]{1,0:T(2,128)S(1)} %get-tuple-element.35.chosen, s32[8,512]{1,0:T(8,128)S(1)} %copy-done.6, bf16[2,3,256,256]{3,2,1,0:T(8,128)(2,1)S(1)} %get-tuple-element.36.weights, ...), custom_call_target="tpu_custom_call" | custom-call | flops 8000000000 | bytes 6000000 | tf_op jit(solution)/shard_map/first_stage/pallas_call | solution.py:433
  24.1 0.0 copy-start.8
  24.1 0.1 collective-permute-start.2
  24.2 1.5 %collective-permute-done.2.received = bf16[1024,128]{1,0:T(8,128)(2,1)S(1)} collective-permute-done((bf16[1024,128]{1,0:T(8,128)(2,1)S(1)}, bf16[1024,128]{1,0:T(8,128)(2,1)S(1)}, u32[]{:S(2)}, u32[]{:S(2)}) %collective-permute-start.2) | collective-permute-done | bytes 262176 | tf_op jit(solution)/shard_map/ppermute | solution.py:593
  25.7 0.0 copy-start.5
  25.7 0.8 %pair_sum.1 = bf16[1024,128]{1,0:T(8,128)(2,1)} custom-call(f32[1024,128]{1,0:T(8,128)S(1)} %get-tuple-element.41.kept, bf16[1024,128]{1,0:T(8,128)(2,1)S(1)} %collective-permute-done.2.received), custom_call_target="tpu_custom_call" | custom-call | tf_op jit(solution)/shard_map/pair_sum/pallas_call | solution.py:502
  26.5 0.0 copy-done.8
  26.5 0.0 copy-start.3
  26.5 14.8 %all-to-all-start = ((bf16[64,16,128]{2,1,0:T(8,128)(2,1)}), bf16[64,16,128]{2,1,0:T(8,128)(2,1)S(1)}, u32[]{:S(2)}, u32[]{:S(2)}) async-start(bf16[64,16,128]{2,1,0:T(8,128)(2,1)} %bitcast.1), calls=%async_computation | async-start | bytes 524288 | tf_op jit(solution)/shard_map/all_to_all | solution.py:618
  41.3 0.0 copy-done.5
  41.3 0.0 copy-done.3
  41.3 0.0 copy-start.9
  41.3 1.2 %copy-done.9 = bf16[8,512,128]{2,1,0:T(8,128)(2,1)S(1)} copy-done((bf16[8,512,128]{2,1,0:T(8,128)(2,1)S(1)}, bf16[8,512,128]{2,1,0:T(8,128)(2,1)}, u32[]{:S(2)}) %copy-start.9) | copy-done | bytes 1048600
  42.5 0.9 %relay.1 = (bf16[2,3,256,256]{3,2,1,0:T(8,128)(2,1)S(1)}, bf16[4,512,128]{2,1,0:T(8,128)(2,1)S(1)}, bf16[4,512,128]{2,1,0:T(8,128)(2,1)S(1)}) custom-call(s32[1]{0:T(128)} %bitcast.position.after, s32[2,8]{1,0:T(2,128)S(1)} %get-tuple-element.35.chosen, bf16[27,64,64]{2,1,0:T(8,128)(2,1)S(1)} %copy-done.3, bf16[27,64,64]{2,1,0:T(8,128)(2,1)S(1)} %copy-done.5, ...), custom_call_target="tpu_custom_call" | custom-call | flops 5000000000 | bytes 2000000 | tf_op jit(solution)/shard_map/relay/pallas_call | solution.py:255
  43.5 0.5 collective-permute-start.3
  44.0 3.1 %collective-permute-start.4 = (bf16[4,512,128]{2,1,0:T(8,128)(2,1)S(1)}, bf16[4,512,128]{2,1,0:T(8,128)(2,1)S(1)}, u32[]{:S(2)}, u32[]{:S(2)}) collective-permute-start(bf16[4,512,128]{2,1,0:T(8,128)(2,1)S(1)} %get-tuple-element.50), channel_id=1, source_target_pairs={{1,2},{3,4},{5,6},{7,8},{9,10},{11,12},{13,14},{15,16},{17,18},{19... | collective-permute-start | bytes 1572872 | tf_op jit(solution)/shard_map/ppermute | solution.py:599
  47.1 4.1 %all-to-all-done = bf16[64,16,128]{2,1,0:T(8,128)(2,1)S(1)} async-done(((bf16[64,16,128]{2,1,0:T(8,128)(2,1)}), bf16[64,16,128]{2,1,0:T(8,128)(2,1)S(1)}, u32[]{:S(2)}, u32[]{:S(2)}) %all-to-all-start) | async-done | bytes 262176 | tf_op jit(solution)/shard_map/all_to_all | solution.py:618
  51.2 0.8 %combine.1 = bf16[64,16,128]{2,1,0:T(8,128)(2,1)} custom-call(bf16[64,16,128]{2,1,0:T(8,128)(2,1)S(1)} %all-to-all-done), custom_call_target="tpu_custom_call" | custom-call | flops 20000000000 | bytes 1000000 | tf_op jit(solution)/shard_map/combine/pallas_call | solution.py:521
  52.0 5.8 %all-to-all-start.1 = ((bf16[64,16,128]{2,1,0:T(8,128)(2,1)}), bf16[64,16,128]{2,1,0:T(8,128)(2,1)S(1)}, u32[]{:S(2)}, u32[]{:S(2)}) async-start(bf16[64,16,128]{2,1,0:T(8,128)(2,1)} %combine.1), calls=%async_computation.1 | async-start | bytes 524288 | tf_op jit(solution)/shard_map/all_to_all | solution.py:618
  57.8 0.0 collective-permute-done.3.before
  57.8 0.0 collective-permute-done.4.after
  57.8 0.0 copy-start.10
  57.8 1.2 %copy-done.10 = bf16[8,512,128]{2,1,0:T(8,128)(2,1)S(1)} copy-done((bf16[8,512,128]{2,1,0:T(8,128)(2,1)S(1)}, bf16[8,512,128]{2,1,0:T(8,128)(2,1)}, u32[]{:S(2)}) %copy-start.10) | copy-done | bytes 1048600
  59.0 7.6 %second_stage.1 = (bf16[8,64,512]{2,1,0:T(8,128)(2,1)}, bf16[8,64,512]{2,1,0:T(8,128)(2,1)}) custom-call(s32[216]{0:T(256)S(1)} %get-tuple-element.34.lookup, s32[8,512]{1,0:T(8,128)S(1)} %copy-done.6, bf16[2,3,256,256]{3,2,1,0:T(8,128)(2,1)S(1)} %get-tuple-element.48.weights, bf16[8,512,128]{2,1,0:T(8,128)(2,1)S(1)} %copy-done.10, ...), custom_call_target="tpu_custom_call" | custom-call | flops 8000000000 | bytes 6000000 | tf_op jit(solution)/shard_map/second_stage/pallas_call | solution.py:476
  66.6 0.4 all-to-all-done.1
  66.9 2.1 %collective-permute-start.5 = (bf16[1024,128]{1,0:T(8,128)(2,1)S(1)}, bf16[1024,128]{1,0:T(8,128)(2,1)S(1)}, u32[]{:S(2)}, u32[]{:S(2)}) collective-permute-start(bf16[1024,128]{1,0:T(8,128)(2,1)S(1)} %bitcast.5), channel_id=1, source_target_pairs={{0,1},{1,0},{2,3},{3,2},{4,5},{5,4},{6,7},{7,6},{8,9},{9,8},{10,11... | collective-permute-start | bytes 786440 | tf_op jit(solution)/shard_map/ppermute | solution.py:593
  69.0 1.2 %collective-permute-done.5.refs_1_ = bf16[1024,128]{1,0:T(8,128)(2,1)S(1)} collective-permute-done((bf16[1024,128]{1,0:T(8,128)(2,1)S(1)}, bf16[1024,128]{1,0:T(8,128)(2,1)S(1)}, u32[]{:S(2)}, u32[]{:S(2)}) %collective-permute-start.5) | collective-permute-done | bytes 262176 | tf_op jit(solution)/shard_map/ppermute | solution.py:593
  70.2 1.7 %unpack.1 = (f32[27,64,64]{2,1,0:T(8,128)}, f32[27,64,64]{2,1,0:T(8,128)}) custom-call(bf16[1024,128]{1,0:T(8,128)(2,1)S(1)} %bitcast.6, bf16[1024,128]{1,0:T(8,128)(2,1)S(1)} %collective-permute-done.5.refs_1_), custom_call_target="tpu_custom_call" | custom-call | tf_op jit(solution)/shard_map/unpack/pallas_call | solution.py:573
Async XLA Ops:
  0.6 7.7 %copy-start = (bf16[8,64,512]{2,1,0:T(8,128)(2,1)S(1)}, bf16[8,64,512]{2,1,0:T(8,128)(2,1)}, u32[]{:S(2)}) copy-start(bf16[8,64,512]{2,1,0:T(8,128)(2,1)} %features.1) | copy-start | bytes 1572868
  0.6 7.7 %copy-start.1 = (bf16[8,64,512]{2,1,0:T(8,128)(2,1)S(1)}, bf16[8,64,512]{2,1,0:T(8,128)(2,1)}, u32[]{:S(2)}) copy-start(bf16[8,64,512]{2,1,0:T(8,128)(2,1)} %cotangent.1) | copy-start | bytes 1572868
  0.7 7.7 %copy-start.6 = (s32[8,512]{1,0:T(8,128)S(1)}, s32[8,512]{1,0:T(8,128)}, u32[]{:S(2)}) copy-start(s32[8,512]{1,0:T(8,128)} %occupancy.5) | copy-start | bytes 49156
  3.3 5.1 %copy-start.7 = (s32[8,26]{1,0:T(8,128)S(1)}, s32[8,26]{1,0:T(8,128)}, u32[]{:S(2)}) copy-start(s32[8,26]{1,0:T(8,128)} %neighbours.1) | copy-start | bytes 2500
  3.3 10.5 %collective-permute-start = (bf16[4,304,128]{2,1,0:T(8,128)(2,1)}, bf16[4,304,128]{2,1,0:T(8,128)(2,1)S(1)}, u32[]{:S(2)}, u32[]{:S(2)}) collective-permute-start(bf16[4,304,128]{2,1,0:T(8,128)(2,1)} %get-tuple-element.38), channel_id=1, source_target_pairs={{0,1},{1,0},{2,3},{3,2},{4,5},{5,4},{6,7},{7,6},{8,9},{9,8},{10,11... | collective-permute-start | bytes 933896 | tf_op jit(solution)/shard_map/ppermute | solution.py:593
  4.8 9.0 %collective-permute-start.1 = (bf16[4,304,128]{2,1,0:T(8,128)(2,1)}, bf16[4,304,128]{2,1,0:T(8,128)(2,1)S(1)}, u32[]{:S(2)}, u32[]{:S(2)}) collective-permute-start(bf16[4,304,128]{2,1,0:T(8,128)(2,1)} %get-tuple-element.39), channel_id=1, source_target_pairs={{1,2},{3,4},{5,6},{7,8},{9,10},{11,12},{13,14},{15,16},{17,18},{19... | collective-permute-start | bytes 933896 | tf_op jit(solution)/shard_map/ppermute | solution.py:599
  8.4 1.0 %copy-start.2 = (bf16[27,64,64]{2,1,0:T(8,128)(2,1)S(1)}, bf16[27,64,64]{2,1,0:T(8,128)(2,1)}, u32[]{:S(2)}) copy-start(bf16[27,64,64]{2,1,0:T(8,128)(2,1)} %kernel_one.3) | copy-start | bytes 663556
  9.4 1.0 %copy-start.4 = (bf16[27,64,64]{2,1,0:T(8,128)(2,1)S(1)}, bf16[27,64,64]{2,1,0:T(8,128)(2,1)}, u32[]{:S(2)}) copy-start(bf16[27,64,64]{2,1,0:T(8,128)(2,1)} %kernel_two.3) | copy-start | bytes 663556
  24.1 2.4 %copy-start.8 = (bf16[8,512,128]{2,1,0:T(8,128)(2,1)}, bf16[8,512,128]{2,1,0:T(8,128)(2,1)S(1)}, u32[]{:S(2)}) copy-start(bf16[8,512,128]{2,1,0:T(8,128)(2,1)S(1)} %get-tuple-element.45.result.own) | copy-start | bytes 3145732
  24.1 1.6 %collective-permute-start.2 = (bf16[1024,128]{1,0:T(8,128)(2,1)S(1)}, bf16[1024,128]{1,0:T(8,128)(2,1)S(1)}, u32[]{:S(2)}, u32[]{:S(2)}) collective-permute-start(bf16[1024,128]{1,0:T(8,128)(2,1)S(1)} %get-tuple-element.42), channel_id=1, source_target_pairs={{0,1},{1,0},{2,3},{3,2},{4,5},{5,4},{6,7},{7,6},{8,9},{9,8},{10,11... | collective-permute-start | bytes 786440 | tf_op jit(solution)/shard_map/ppermute | solution.py:593
  25.7 15.6 %copy-start.5 = (bf16[27,64,64]{2,1,0:T(8,128)(2,1)S(1)}, bf16[27,64,64]{2,1,0:T(8,128)(2,1)}, u32[]{:S(2)}) copy-start(bf16[27,64,64]{2,1,0:T(8,128)(2,1)} %kernel_two.3) | copy-start | bytes 663556
  26.5 14.8 %copy-start.3 = (bf16[27,64,64]{2,1,0:T(8,128)(2,1)S(1)}, bf16[27,64,64]{2,1,0:T(8,128)(2,1)}, u32[]{:S(2)}) copy-start(bf16[27,64,64]{2,1,0:T(8,128)(2,1)} %kernel_one.3) | copy-start | bytes 663556
  26.5 24.7 %all-to-all-start = ((bf16[64,16,128]{2,1,0:T(8,128)(2,1)}), bf16[64,16,128]{2,1,0:T(8,128)(2,1)S(1)}, u32[]{:S(2)}, u32[]{:S(2)}) async-start(bf16[64,16,128]{2,1,0:T(8,128)(2,1)} %bitcast.1), calls=%async_computation | async-start | bytes 524288 | tf_op jit(solution)/shard_map/all_to_all | solution.py:618
  41.3 1.2 %copy-start.9 = (bf16[8,512,128]{2,1,0:T(8,128)(2,1)S(1)}, bf16[8,512,128]{2,1,0:T(8,128)(2,1)}, u32[]{:S(2)}) copy-start(bf16[8,512,128]{2,1,0:T(8,128)(2,1)} %copy-done.8) | copy-start | bytes 3145732
  43.5 14.3 %collective-permute-start.3 = (bf16[4,512,128]{2,1,0:T(8,128)(2,1)S(1)}, bf16[4,512,128]{2,1,0:T(8,128)(2,1)S(1)}, u32[]{:S(2)}, u32[]{:S(2)}) collective-permute-start(bf16[4,512,128]{2,1,0:T(8,128)(2,1)S(1)} %get-tuple-element.49), channel_id=1, source_target_pairs={{0,1},{1,0},{2,3},{3,2},{4,5},{5,4},{6,7},{7,6},{8,9},{9,8},{10,11... | collective-permute-start | bytes 1572872 | tf_op jit(solution)/shard_map/ppermute | solution.py:593
  44.0 13.8 %collective-permute-start.4 = (bf16[4,512,128]{2,1,0:T(8,128)(2,1)S(1)}, bf16[4,512,128]{2,1,0:T(8,128)(2,1)S(1)}, u32[]{:S(2)}, u32[]{:S(2)}) collective-permute-start(bf16[4,512,128]{2,1,0:T(8,128)(2,1)S(1)} %get-tuple-element.50), channel_id=1, source_target_pairs={{1,2},{3,4},{5,6},{7,8},{9,10},{11,12},{13,14},{15,16},{17,18},{19... | collective-permute-start | bytes 1572872 | tf_op jit(solution)/shard_map/ppermute | solution.py:599
  52.0 15.0 %all-to-all-start.1 = ((bf16[64,16,128]{2,1,0:T(8,128)(2,1)}), bf16[64,16,128]{2,1,0:T(8,128)(2,1)S(1)}, u32[]{:S(2)}, u32[]{:S(2)}) async-start(bf16[64,16,128]{2,1,0:T(8,128)(2,1)} %combine.1), calls=%async_computation.1 | async-start | bytes 524288 | tf_op jit(solution)/shard_map/all_to_all | solution.py:618
  57.8 1.2 %copy-start.10 = (bf16[8,512,128]{2,1,0:T(8,128)(2,1)S(1)}, bf16[8,512,128]{2,1,0:T(8,128)(2,1)}, u32[]{:S(2)}) copy-start(bf16[8,512,128]{2,1,0:T(8,128)(2,1)} %copy-done.8) | copy-start | bytes 3145732
  66.9 3.2 %collective-permute-start.5 = (bf16[1024,128]{1,0:T(8,128)(2,1)S(1)}, bf16[1024,128]{1,0:T(8,128)(2,1)S(1)}, u32[]{:S(2)}, u32[]{:S(2)}) collective-permute-start(bf16[1024,128]{1,0:T(8,128)(2,1)S(1)} %bitcast.5), channel_id=1, source_target_pairs={{0,1},{1,0},{2,3},{3,2},{4,5},{5,4},{6,7},{7,6},{8,9},{9,8},{10,11... | collective-permute-start | bytes 786440 | tf_op jit(solution)/shard_map/ppermute | solution.py:593
